TPU v7x, 128 devices: a whole 4x4x4 slice. The times are simulated.
128 devices in a mesh: fsdp: 16 (over y_hi, x, core), tp: 8 (over z, y_lo).
Axes of the slice: x: 4, y: 4 (y_hi: 2, y_lo: 2; y = y_hi * 2 + y_lo), z: 4, core: 2. Of those that a mesh axis runs over, the one named last changes fastest.
Arguments:
- hidden: bfloat16 [32768, 29568], P('fsdp', 'tp'), may hold values from -6 to 6
- out_grad: bfloat16 [32768, 8192], P('fsdp', 'tp'), may hold values from -0.03125 to 0.03125
- projector_bank: bfloat16 [16, 8192, 256], P('fsdp', 'tp'), may hold values from -0.0625 to 0.0625
- owner: int32 [1], replicated, may hold values from 0 to 15
- first_moment: float32 [8, 3696, 256], P('tp', 'fsdp'), may hold values from -4 to 4
- second_moment: float32 [8, 3696, 256], P('tp', 'fsdp'), may hold values from 0.05 to 2
Outputs:
- new_first: float32 [8, 3696, 256], P('tp', 'fsdp')
- new_second: float32 [8, 3696, 256], P('tp', 'fsdp')
- weight_update: bfloat16 [8, 3696, 8192], P('tp', 'fsdp')
All inputs are finite; a program needn't handle non-finite values.
Results may differ from a plain program's by a relative error of at most 0.0051.
Values may be sent and summed in bfloat16 or wider, within the bound.
No kernel may reach another device: no remote copies, remote signals or barrier semaphores. Data moves between devices by JAX's collectives and lax.ppermute only.
A program may use at most 192 MiB of HBM per device.

v0:
```python
import jax
import jax.numpy as jnp
from jax import lax
from jax.sharding import PartitionSpec as P


def spread(value, axis, source):
    kept = jnp.where(lax.axis_index(axis) == source, value, 0).astype(value.dtype)
    return lax.psum(kept, axis)


def local(hidden, out_grad, projector_bank, owner, first_moment, second_moment):
    root = owner[0]
    local_rows = out_grad.shape[1]
    gathered = lax.all_gather(projector_bank[0], "tp", axis=0, tiled=True)
    projector = spread(gathered, "fsdp", root)
    own_piece = lax.dynamic_slice_in_dim(
        projector, lax.axis_index("tp") * local_rows, local_rows, 0
    )
    partial_coeffs = jnp.dot(out_grad, own_piece, preferred_element_type=jnp.float32)
    coeffs = lax.psum(partial_coeffs, "tp").astype(jnp.bfloat16)
    proj_grad = lax.psum_scatter(
        lax.dot_general(
            hidden, coeffs, (((0,), (0,)), ((), ())), preferred_element_type=jnp.float32
        ),
        "fsdp",
        scatter_dimension=0,
        tiled=True,
    )
    new_first = 0.9 * first_moment[0] + 0.1 * proj_grad
    new_second = 0.95 * second_moment[0] + 0.05 * proj_grad * proj_grad
    direction = (new_first / (jnp.sqrt(new_second) + 1e-08)).astype(jnp.bfloat16)
    update = lax.dot_general(
        direction, projector, (((1,), (1,)), ((), ())), preferred_element_type=jnp.float32
    )
    update = (-4.0 * update).astype(jnp.bfloat16)
    return (new_first[None], new_second[None], update[None])


def solution(mesh):
    in_specs = (
        P("fsdp", "tp"),
        P("fsdp", "tp"),
        P("fsdp", "tp", None),
        P(),
        P("tp", "fsdp", None),
        P("tp", "fsdp", None),
    )
    out_specs = (P("tp", "fsdp", None), P("tp", "fsdp", None), P("tp", "fsdp", None))
    return jax.shard_map(local, mesh=mesh, in_specs=in_specs, out_specs=out_specs, check_vma=False)
```

profile of v0, /device:TPU:1, one launch (start us, length us, event | category | flops | bytes accessed | tf_op | source)
XLA Modules:
  0.0 419.4 jit_solution(11625727379940315931)
XLA Ops:
  7.2 0.0 all-gather.3.cloned.1.call-start
  7.2 0.7 all-gather.3.cloned.1.call-update
  7.9 0.0 all-reduce.5.cloned.1.call-start
  8.6 95.0 %all-gather.3.cloned.1.call-done = bf16[1,8192,256]{2,1,0:T(8,128)(2,1)} async-done(((bf16[1,1024,256]{2,1,0:T(8,128)(2,1)}), bf16[1,8192,256]{2,1,0:T(8,128)(2,1)}) %all-gather.3.cloned.1.call-update) | async-done | bytes 4194320 | tf_op jit(solution)/shard_map/all_gather | solution.py:15
  103.6 2.2 select_bitcast_fusion
  105.8 0.0 all-reduce.5.cloned.1.call-update
  105.9 150.5 %all-reduce.5.cloned.1.call-done = bf16[8192,256]{1,0:T(8,128)(2,1)} async-done(((bf16[8192,256]{1,0:T(8,128)(2,1)}), bf16[8192,256]{1,0:T(8,128)(2,1)}) %all-reduce.5.cloned.1.call-update) | async-done | bytes 4194320 | tf_op jit(solution)/shard_map/psum | solution.py:9
  256.3 3.7 convolution_bitcast_fusion.1
  260.0 83.9 %all-reduce.6 = bf16[2048,256]{0,1:T(8,128)(2,1)S(1)} all-reduce(f32[2048,256]{0,1:T(8,128)S(1)} %convolution_bitcast_fusion.1), channel_id=1, replica_groups=mesh['fsdp'=16,'tp'=8] {'tp'}, use_global_device_ids=true, to_apply=%region_1.2 | all-reduce | flops 524288 | bytes 3145728 | tf_op jit(solution)/shard_map/psum | solution.py:21
  343.9 0.0 copy-start.2
  344.0 9.4 %convolution_bitcast_fusion = f32[3696,256]{1,0:T(8,128)} fusion(bf16[2048,3696]{0,1:T(8,128)(2,1)} %param.6, bf16[2048,256]{0,1:T(8,128)(2,1)S(1)} %all-reduce.6), kind=kOutput, calls=%fused_computation.3 | convolution fusion | flops 3875536896 | bytes 19972096 | tf_op jit(solution)/shard_map/dot_general | solution.py:23
  353.3 0.0 copy-start
  353.3 0.0 copy-start.1
  353.3 46.7 %fusion = f32[232,256]{1,0:T(8,128)S(1)} fusion(f32[3696,256]{1,0:T(8,128)} %convolution_bitcast_fusion), kind=kCustom, calls=%all-reduce-scatter | all-reduce-scatter fusion | flops 950273 | bytes 4022784
  400.1 1.9 collective-permute-start
  402.0 0.0 copy-done.2
  402.0 0.6 dynamic-slice.4
  403.3 1.6 collective-permute-done
  404.8 0.3 concatenate
  405.1 0.0 copy-done
  405.1 0.0 copy-done.1
  405.1 0.1 fusion.9
  405.2 0.9 copy.15
  406.1 0.9 copy.16
  407.1 5.5 %fusion.2 = bf16[1,231,8192]{2,1,0:T(8,128)(2,1)} fusion(bf16[8192,256]{1,0:T(8,128)(2,1)} %all-reduce.5.cloned.1.call-done, f32[1,231,256]{2,0,1:T(1,128)S(1)} %copy-done.1, f32[247,256]{1,0:T(8,128)S(1)} %concatenate, u32[]{:S(6)} %subtract, f32[1,231,256]{2,0,1:T(1,128)S(1)} %copy-done), kind=kOutput, calls=%fused_computation.2 | convolution fusion | flops 973260288 | bytes 8689668 | tf_op jit(solution)/shard_map/dot_general | solution.py:33
  (1 shorter events, 0.0 us)
Async XLA Ops:
  7.2 96.5 %all-gather.3.cloned.1.call-start = ((), (), s32[]{:S(2)}) async-start(), calls=%async_computation.1 | async-start | bytes 4718592 | tf_op jit(solution)/shard_map/all_gather | solution.py:15
  7.9 248.4 %all-reduce.5.cloned.1.call-start = ((), (), s32[]{:S(2)}) async-start(), calls=%async_computation | async-start | bytes 8388608 | tf_op jit(solution)/shard_map/psum | solution.py:9
  343.9 58.1 %copy-start.2 = (u32[128]{0:T(128)S(1)}, u32[128]{0:T(128)}, u32[]{:S(2)}) copy-start(u32[128]{0:T(128)} %constant.34) | copy-start | bytes 1540
  353.3 51.7 %copy-start = (f32[1,231,256]{2,0,1:T(1,128)S(1)}, f32[1,231,256]{2,0,1:T(1,128)}, u32[]{:S(2)}) copy-start(f32[1,231,256]{2,0,1:T(1,128)} %param.11) | copy-start | bytes 709636
  353.3 51.8 %copy-start.1 = (f32[1,231,256]{2,0,1:T(1,128)S(1)}, f32[1,231,256]{2,0,1:T(1,128)}, u32[]{:S(2)}) copy-start(f32[1,231,256]{2,0,1:T(1,128)} %param.10) | copy-start | bytes 709636
  400.1 4.7 %collective-permute-start = (f32[15,256]{1,0:T(8,128)S(1)}, f32[15,256]{1,0:T(8,128)S(1)}, u32[]{:S(2)}, u32[]{:S(2)}) collective-permute-start(f32[15,256]{1,0:T(8,128)S(1)} %slice), channel_id=1, source_target_pairs={{0,8},{8,16},{16,24},{24,32},{32,40},{40,48},{48,56},{56,64},{64,7... | collective-permute-start | bytes 46088
Sparse Core Ops, SparseCore 0:
  9.6 93.9 all-gather.2
  106.1 150.1 all-reduce.4
where the time goes:
time: 423 us; the launch traced here: 419 us
  waiting for transfers between devices  248 us (59%)
  blocking collectives  131 us (31%)
  matrix products  18.5 us (4%)
  between operations  15.4 us (4%)
    psum x1, waiting for transfers between devices, spread(): return lax.psum(kept, axis)  150 us
    all_gather x1, waiting for transfers between devices, local(): gathered = lax.all_gather(projector_bank[0], 'tp', axis=0, tiled=True)  95 us
    psum x1, blocking collectives, local(): coeffs = lax.psum(partial_coeffs, 'tp').astype(jnp.bfloat16)  83.9 us
    unnamed x1, blocking collectives  46.7 us
    dot_general x1, matrix products, local(): lax.dot_general(hidden, coeffs, (((0,), (0,)), ((), ())), preferred_eleme...  9.39 us
  transfers between devices with their start and end apart: 3, of which 3 were waited for; matrix products, arithmetic and copies ran while one was open for 0% of the time, Pallas kernels for 0%

commit v1 on v0

v1 whole, which is shorter than its diff:
```python
import jax
import jax.numpy as jnp
from jax import lax
from jax.sharding import PartitionSpec as P

FSDP = ("yh", "x", "core")
CHIPS = ("yh", "x")
TP = ("z", "yl")
ROWS = 231
WIDE = 240


def starts(blocks, total):
    return [min(ROWS * i // 8 * 8, total - WIDE) for i in range(blocks)]


def local(hidden, out_grad, projector_bank, owner, first_moment, second_moment):
    bf16, f32 = jnp.bfloat16, jnp.float32
    root = owner[0]
    fsdp = lax.axis_index(FSDP)
    core = lax.axis_index("core")

    candidates = lax.all_to_all(projector_bank[0].reshape(16, 64, 256), FSDP, 0, 0)
    piece = lax.dynamic_index_in_dim(candidates, root, 0, keepdims=False)
    own_piece = lax.all_gather(piece, FSDP, axis=0, tiled=True)
    projector = lax.all_gather(own_piece, TP, axis=0, tiled=True)

    partial = jnp.dot(out_grad, own_piece, preferred_element_type=f32).astype(bf16)
    parts = lax.all_to_all(partial.reshape(8, 256, 256), TP, 0, 0)
    summed = jnp.sum(parts.astype(f32), axis=0).astype(bf16)
    coeffs = lax.all_to_all(
        jnp.broadcast_to(summed[None], (8, 256, 256)), TP, 0, 0
    ).reshape(2048, 256)

    grad = lax.dot_general(
        hidden, coeffs, (((0,), (0,)), ((), ())), preferred_element_type=f32
    )
    begin = starts(16, grad.shape[0])
    blocks = [grad[a : a + WIDE] for a in begin]
    even, odd = jnp.stack(blocks[0::2]), jnp.stack(blocks[1::2])
    keep = jnp.where(core == 0, even, odd)
    give = jnp.where(core == 0, odd, even).astype(bf16)
    got = lax.ppermute(give, "core", [(0, 1), (1, 0)])
    pair = (keep + got.astype(f32)).astype(bf16)
    shares = lax.all_to_all(pair, CHIPS, 0, 0)
    wide = jnp.sum(shares.astype(f32), axis=0)
    offset = ROWS * fsdp - jnp.array(begin, jnp.int32)[fsdp]
    proj_grad = lax.dynamic_slice_in_dim(wide, offset, ROWS, 0)

    new_first = 0.9 * first_moment[0] + 0.1 * proj_grad
    new_second = 0.95 * second_moment[0] + 0.05 * proj_grad * proj_grad
    direction = (new_first / (jnp.sqrt(new_second) + 1e-08)).astype(bf16)
    update = lax.dot_general(
        direction, projector, (((1,), (1,)), ((), ())), preferred_element_type=f32
    )
    update = (-4.0 * update).astype(bf16)
    return (new_first[None], new_second[None], update[None])


def solution(mesh):
    fine = jax.sharding.Mesh(
        mesh.devices.reshape(2, 4, 2, 4, 2), ("yh", "x", "core", "z", "yl")
    )
    in_specs = (
        P(FSDP, TP),
        P(FSDP, TP),
        P(FSDP, TP, None),
        P(),
        P(TP, FSDP, None),
        P(TP, FSDP, None),
    )
    out_specs = (P(TP, FSDP, None), P(TP, FSDP, None), P(TP, FSDP, None))
    return jax.shard_map(local, mesh=fine, in_specs=in_specs, out_specs=out_specs, check_vma=False)
```

time: 423 us -> 188 us (0.44)
  waiting for transfers between devices: 248 us -> 100 us
  blocking collectives: 131 us -> 22.1 us
  starting transfers between devices: 2 us -> 25.4 us
    psum x1 -> x0, waiting for transfers between devices: 150 us -> none  [spread(): return lax.psum(kept, axis)]
    psum x1 -> x0, blocking collectives: 83.9 us -> none  [local(): coeffs = lax.psum(partial_coeffs, 'tp').astype(jnp.bfloat16)]
    all_to_all x0 -> x4, waiting for transfers between devices: none -> 68.5 us  [the longest x1 26.4 us: local(): lax.all_to_all(jnp.broadcast_to(summed[None], (8, 256, 256)), TP, 0, 0)]
    all_gather x1, waiting for transfers between devices: 95 us -> 29.1 us  [local(): projector = lax.all_gather(own_piece, TP, axis=0, tiled=True)]
    unnamed x1 -> x0, blocking collectives: 46.7 us -> none
    all_gather x0 -> x1, blocking collectives: none -> 22.1 us  [local(): own_piece = lax.all_gather(piece, FSDP, axis=0, tiled=True)]
    all_to_all x0 -> x4, starting transfers between devices: none -> 21.6 us  [the longest x1 8.46 us: local(): lax.all_to_all(projector_bank[0].reshape(16, 64, 256), FSDP, 0, 0)]
  transfers between devices with their start and end apart: 3 -> 6, of which waited for: 3 -> 6; matrix products, arithmetic and copies ran while one was open for 0% -> 7% of each run, Pallas kernels for 0% -> 0%
where the time goes in v1:
time: 188 us; the launch traced here: 187 us
  waiting for transfers between devices  100 us (53%)
  starting transfers between devices  25.4 us (14%)
  blocking collectives  22.1 us (12%)
  matrix products  16.8 us (9%)
  between operations  15.5 us (8%)
  local copies, waits for them, and re-layouts  4.76 us (3%)
  other arithmetic  2.12 us (1%)
    all_gather x1, waiting for transfers between devices, local(): projector = lax.all_gather(own_piece, TP, axis=0, tiled=True)  29.1 us
    all_to_all x1, waiting for transfers between devices, local(): lax.all_to_all(jnp.broadcast_to(summed[None], (8, 256, 256)), TP, 0, 0)  26.4 us
    all_gather x1, blocking collectives, local(): own_piece = lax.all_gather(piece, FSDP, axis=0, tiled=True)  22.1 us
    all_to_all x1, waiting for transfers between devices, local(): shares = lax.all_to_all(pair, CHIPS, 0, 0)  15.9 us
    all_to_all x1, waiting for transfers between devices, local(): parts = lax.all_to_all(partial.reshape(8, 256, 256), TP, 0, 0)  15.4 us
    all_to_all x1, waiting for transfers between devices, local(): lax.all_to_all(projector_bank[0].reshape(16, 64, 256), FSDP, 0, 0)  10.7 us
    all_to_all x1, starting transfers between devices, local(): lax.all_to_all(projector_bank[0].reshape(16, 64, 256), FSDP, 0, 0)  8.46 us
    dot_general x1, matrix products, local(): lax.dot_general(hidden, coeffs, (((0,), (0,)), ((), ())), preferred_eleme...  7.72 us
  transfers between devices with their start and end apart: 6, of which 6 were waited for; matrix products, arithmetic and copies ran while one was open for 7% of the time, Pallas kernels for 0%

profile of v1, /device:TPU:1, one launch (start us, length us, event | category | flops | bytes accessed | tf_op | source)
XLA Modules:
  0.0 187.1 jit_solution(2718474700474535840)
XLA Ops:
  7.2 8.5 %all-to-all-start = ((bf16[16,64,256]{2,1,0:T(8,128)(2,1)}), bf16[16,64,256]{2,1,0:T(8,128)(2,1)S(1)}, u32[]{:S(2)}, u32[]{:S(2)}) async-start(bf16[16,64,256]{2,1,0:T(8,128)(2,1)} %bitcast.95), calls=%async_computation | async-start | bytes 1048576 | tf_op jit(solution)/shard_map/all_to_all | solution.py:23
  16.3 10.7 %all-to-all-done = bf16[16,64,256]{2,1,0:T(8,128)(2,1)S(1)} async-done(((bf16[16,64,256]{2,1,0:T(8,128)(2,1)}), bf16[16,64,256]{2,1,0:T(8,128)(2,1)S(1)}, u32[]{:S(2)}, u32[]{:S(2)}) %all-to-all-start) | async-done | bytes 524320 | tf_op jit(solution)/shard_map/all_to_all | solution.py:23
  27.0 22.1 %all-gather = bf16[1,1024,256]{2,1,0:T(8,128)(2,1)S(1)} all-gather(bf16[1,64,256]{2,1,0:T(8,128)(2,1)S(1)} %constant_dynamic-slice_fusion), channel_id=2, replica_groups=mesh['yh'=2,'x'=4,'core'=2,'z'=4,'yl'=2] {'yh','x','core'}, dimensions={1}, use_global_device_ids=true | all-gather | bytes 557056 | tf_op jit(solution)/shard_map/all_gather | solution.py:25
  49.1 0.0 copy-start
  49.1 3.7 %convolution_convert_fusion = bf16[256,2048]{1,0:T(8,128)(2,1)S(1)} fusion(bf16[2048,1024]{1,0:T(8,128)(2,1)} %param.8, bf16[1,1024,256]{2,1,0:T(8,128)(2,1)S(1)} %all-gather), kind=kOutput, calls=%fused_computation.5 | convolution fusion | flops 1074266112 | bytes 5767168 | tf_op jit(solution)/shard_map/dot_general | solution.py:28
  52.8 0.0 copy-done
  52.8 1.0 copy.26
  53.9 5.1 %all-to-all-start.1 = ((bf16[8,256,256]{1,2,0:T(8,128)(2,1)}), bf16[8,256,256]{1,2,0:T(8,128)(2,1)S(1)}, u32[]{:S(2)}, u32[]{:S(2)}) async-start(bf16[8,256,256]{1,2,0:T(8,128)(2,1)} %bitcast.89), calls=%async_computation.1 | async-start | bytes 2097152 | tf_op jit(solution)/shard_map/all_to_all | solution.py:29
  59.0 0.0 all-gather.4.cloned.1.call-start
  59.0 0.7 all-gather.4.cloned.1.call-update
  59.7 15.4 %all-to-all-done.1 = bf16[8,256,256]{1,2,0:T(8,128)(2,1)S(1)} async-done(((bf16[8,256,256]{1,2,0:T(8,128)(2,1)}), bf16[8,256,256]{1,2,0:T(8,128)(2,1)S(1)}, u32[]{:S(2)}, u32[]{:S(2)}) %all-to-all-start.1) | async-done | bytes 1048608 | tf_op jit(solution)/shard_map/all_to_all | solution.py:29
  75.2 0.1 reduce_sum.21
  75.3 0.1 copy.15
  75.4 1.0 broadcast_in_dim.15
  76.5 3.6 %all-to-all-start.2 = ((bf16[8,256,256]{2,1,0:T(8,128)(2,1)}), bf16[8,256,256]{2,1,0:T(8,128)(2,1)S(1)}, u32[]{:S(2)}, u32[]{:S(2)}) async-start(bf16[8,256,256]{2,1,0:T(8,128)(2,1)} %broadcast_in_dim.15), calls=%async_computation.2 | async-start | bytes 2097152 | tf_op jit(solution)/shard_map/all_to_all | solution.py:31
  80.0 26.4 %all-to-all-done.2 = bf16[8,256,256]{2,1,0:T(8,128)(2,1)S(1)} async-done(((bf16[8,256,256]{2,1,0:T(8,128)(2,1)}), bf16[8,256,256]{2,1,0:T(8,128)(2,1)S(1)}, u32[]{:S(2)}, u32[]{:S(2)}) %all-to-all-start.2) | async-done | bytes 1048608 | tf_op jit(solution)/shard_map/all_to_all | solution.py:31
  106.4 7.7 %convolution_bitcast_fusion = f32[3696,256]{1,0:T(8,128)S(1)} fusion(bf16[2048,3696]{0,1:T(8,128)(2,1)} %param.7, bf16[2048,256]{1,0:T(8,128)(2,1)S(1)} %bitcast.93), kind=kOutput, calls=%fused_computation.3 | convolution fusion | flops 3875536896 | bytes 19972096 | tf_op jit(solution)/shard_map/dot_general | solution.py:35
  114.5 0.4 select_convert_fusion
  114.9 3.8 %collective-permute-start = (bf16[8,240,256]{2,1,0:T(8,128)(2,1)S(1)}, bf16[8,240,256]{2,1,0:T(8,128)(2,1)S(1)}, u32[]{:S(2)}, u32[]{:S(2)}) collective-permute-start(bf16[8,240,256]{2,1,0:T(8,128)(2,1)S(1)} %select_convert_fusion), channel_id=1, source_target_pairs={{0,8},{8,0},{1,9},{9,1},{2,10},{10,2},{3,11},{11,3},{4,12},{12,4},... | collective-permute-start | bytes 2949128 | tf_op jit(solution)/shard_map/ppermute | solution.py:43
  118.6 2.2 %collective-permute-done = bf16[8,240,256]{2,1,0:T(8,128)(2,1)S(1)} collective-permute-done((bf16[8,240,256]{2,1,0:T(8,128)(2,1)S(1)}, bf16[8,240,256]{2,1,0:T(8,128)(2,1)S(1)}, u32[]{:S(2)}, u32[]{:S(2)}) %collective-permute-start) | collective-permute-done | bytes 983072 | tf_op jit(solution)/shard_map/ppermute | solution.py:43
  120.8 1.3 add_convert_fusion
  122.2 0.0 copy-start.3
  122.2 0.0 copy-start.1
  122.2 0.0 copy-start.2
  122.2 4.5 %all-to-all-start.3 = ((bf16[8,240,256]{2,1,0:T(8,128)(2,1)}), bf16[8,240,256]{2,1,0:T(8,128)(2,1)S(1)}, u32[]{:S(2)}, u32[]{:S(2)}) async-start(bf16[8,240,256]{2,1,0:T(8,128)(2,1)} %add_convert_fusion), calls=%async_computation.3 | async-start | bytes 1966080 | tf_op jit(solution)/shard_map/all_to_all | solution.py:45
  126.6 0.0 copy-done.3
  126.7 0.6 dynamic_slice.11
  127.9 15.9 %all-to-all-done.3 = bf16[8,240,256]{2,1,0:T(8,128)(2,1)S(1)} async-done(((bf16[8,240,256]{2,1,0:T(8,128)(2,1)}), bf16[8,240,256]{2,1,0:T(8,128)(2,1)S(1)}, u32[]{:S(2)}, u32[]{:S(2)}) %all-to-all-start.3) | async-done | bytes 983072 | tf_op jit(solution)/shard_map/all_to_all | solution.py:45
  143.8 0.1 convert_reduce_fusion
  144.0 0.0 copy-done.1
  144.0 0.0 copy-done.2
  144.0 0.1 fusion.20
  144.1 0.9 broadcast_in_dim.16
  144.9 0.9 broadcast_in_dim.17
  145.8 29.1 %all-gather.4.cloned.1.call-done = bf16[1,8192,256]{2,1,0:T(8,128)(2,1)} async-done(((bf16[1,1024,256]{2,1,0:T(8,128)(2,1)}), bf16[1,8192,256]{2,1,0:T(8,128)(2,1)}) %all-gather.4.cloned.1.call-update) | async-done | bytes 4194320 | tf_op jit(solution)/shard_map/all_gather | solution.py:26
  174.9 5.4 %fusion.1 = bf16[1,231,8192]{2,1,0:T(8,128)(2,1)} fusion(bf16[1,8192,256]{2,1,0:T(8,128)(2,1)} %all-gather.4.cloned.1.call-done, f32[231,256]{1,0:T(8,128)S(1)} %get-tuple-element.20, f32[231,256]{1,0:T(8,128)S(1)} %get-tuple-element.19), kind=kOutput, calls=%fused_computation.2 | convolution fusion | flops 972846336 | bytes 8452096 | tf_op jit(solution)/shard_map/dot_general | solution.py:53
  (9 shorter events, 0.3 us)
Async XLA Ops:
  7.2 19.8 %all-to-all-start = ((bf16[16,64,256]{2,1,0:T(8,128)(2,1)}), bf16[16,64,256]{2,1,0:T(8,128)(2,1)S(1)}, u32[]{:S(2)}, u32[]{:S(2)}) async-start(bf16[16,64,256]{2,1,0:T(8,128)(2,1)} %bitcast.95), calls=%async_computation | async-start | bytes 1048576 | tf_op jit(solution)/shard_map/all_to_all | solution.py:23
  49.1 3.7 %copy-start = (bf16[1,1024,256]{2,1,0:T(8,128)(2,1)}, bf16[1,1024,256]{2,1,0:T(8,128)(2,1)S(1)}, u32[]{:S(2)}) copy-start(bf16[1,1024,256]{2,1,0:T(8,128)(2,1)S(1)} %all-gather) | copy-start | bytes 1572868
  53.9 21.3 %all-to-all-start.1 = ((bf16[8,256,256]{1,2,0:T(8,128)(2,1)}), bf16[8,256,256]{1,2,0:T(8,128)(2,1)S(1)}, u32[]{:S(2)}, u32[]{:S(2)}) async-start(bf16[8,256,256]{1,2,0:T(8,128)(2,1)} %bitcast.89), calls=%async_computation.1 | async-start | bytes 2097152 | tf_op jit(solution)/shard_map/all_to_all | solution.py:29
  59.0 115.9 %all-gather.4.cloned.1.call-start = ((), (), s32[]{:S(2)}) async-start(), calls=%async_computation.4 | async-start | bytes 4718592 | tf_op jit(solution)/shard_map/all_gather | solution.py:26
  76.5 29.9 %all-to-all-start.2 = ((bf16[8,256,256]{2,1,0:T(8,128)(2,1)}), bf16[8,256,256]{2,1,0:T(8,128)(2,1)S(1)}, u32[]{:S(2)}, u32[]{:S(2)}) async-start(bf16[8,256,256]{2,1,0:T(8,128)(2,1)} %broadcast_in_dim.15), calls=%async_computation.2 | async-start | bytes 2097152 | tf_op jit(solution)/shard_map/all_to_all | solution.py:31
  114.9 6.0 %collective-permute-start = (bf16[8,240,256]{2,1,0:T(8,128)(2,1)S(1)}, bf16[8,240,256]{2,1,0:T(8,128)(2,1)S(1)}, u32[]{:S(2)}, u32[]{:S(2)}) collective-permute-start(bf16[8,240,256]{2,1,0:T(8,128)(2,1)S(1)} %select_convert_fusion), channel_id=1, source_target_pairs={{0,8},{8,0},{1,9},{9,1},{2,10},{10,2},{3,11},{11,3},{4,12},{12,4},... | collective-permute-start | bytes 2949128 | tf_op jit(solution)/shard_map/ppermute | solution.py:43
  122.2 4.5 %copy-start.3 = (s32[16]{0:T(128)S(1)}, s32[16]{0:T(128)}, u32[]{:S(2)}) copy-start(s32[16]{0:T(128)} %constant.49.clone) | copy-start | bytes 196
  122.2 21.8 %copy-start.1 = (f32[1,231,256]{2,0,1:T(1,128)S(1)}, f32[1,231,256]{2,0,1:T(1,128)}, u32[]{:S(2)}) copy-start(f32[1,231,256]{2,0,1:T(1,128)} %param.12) | copy-start | bytes 709636
  122.2 21.8 %copy-start.2 = (f32[1,231,256]{2,0,1:T(1,128)S(1)}, f32[1,231,256]{2,0,1:T(1,128)}, u32[]{:S(2)}) copy-start(f32[1,231,256]{2,0,1:T(1,128)} %param.11) | copy-start | bytes 709636
  122.2 21.7 %all-to-all-start.3 = ((bf16[8,240,256]{2,1,0:T(8,128)(2,1)}), bf16[8,240,256]{2,1,0:T(8,128)(2,1)S(1)}, u32[]{:S(2)}, u32[]{:S(2)}) async-start(bf16[8,240,256]{2,1,0:T(8,128)(2,1)} %add_convert_fusion), calls=%async_computation.3 | async-start | bytes 1966080 | tf_op jit(solution)/shard_map/all_to_all | solution.py:45
Sparse Core Ops, SparseCore 0:
  61.5 113.3 all-gather.3

commit v2 on v1

v2 whole, which is shorter than its diff:
```python
import jax
import jax.numpy as jnp
from jax import lax
from jax.experimental import pallas as pl
from jax.experimental.pallas import tpu as pltpu
from jax.sharding import PartitionSpec as P

FSDP = ("yh", "x", "core")
CHIPS = ("yh", "x")
TP = ("z", "yl")
ROWS = 231
PADDED = 232
BLOCK = 256
RANK = 256
bf16, f32 = jnp.bfloat16, jnp.float32


def cost(flops, moved):
    return pl.CostEstimate(flops=flops, bytes_accessed=moved, transcendentals=0)


def room(mebibytes):
    return pltpu.CompilerParams(vmem_limit_bytes=mebibytes << 20)


def stream(count, load, use):
    for i in range(3):
        load(i).start()

    @pl.loop(0, count)
    def _(i):
        load(i).wait()

        @pl.when(i + 3 < count)
        def _():
            load(i + 3).start()

        use(i)


def partial_kernel(where, mine, other, grad, out, piece, rows, done):
    core, share = where[0], where[1]
    half = mine.shape[0]

    def load(i):
        begin = 512 * i if isinstance(i, int) else pl.multiple_of(512 * i, 512)
        return pltpu.make_async_copy(grad.at[pl.ds(begin, 512)], rows.at[i], done.at[i])

    def use(i):
        product = jnp.dot(rows[i], piece[...], preferred_element_type=f32).astype(bf16)
        below = piece[pl.ds(pl.multiple_of(share * 128, 128), 128), :]
        for j in range(2):
            out[2 * i + j, :BLOCK, :] = product[BLOCK * j : BLOCK * (j + 1)]
            out[2 * i + j, BLOCK:, :] = below

    piece[pl.ds(pl.multiple_of(core * half, half), half), :] = mine[...]
    piece[pl.ds(pl.multiple_of((1 - core) * half, half), half), :] = other[...]
    stream(4, load, use)


def partial_and_share(where, mine, other, out_grad):
    vmem, any_space = pl.BlockSpec(memory_space=pltpu.VMEM), pl.BlockSpec(memory_space=pl.ANY)
    return pl.pallas_call(
        partial_kernel,
        in_specs=[pl.BlockSpec(memory_space=pltpu.SMEM), vmem, vmem, any_space],
        out_specs=vmem,
        out_shape=jax.ShapeDtypeStruct((8, BLOCK + 128, RANK), bf16),
        scratch_shapes=[
            pltpu.VMEM((1024, RANK), bf16),
            pltpu.VMEM((4, 512, 1024), bf16),
            pltpu.SemaphoreType.DMA((4,)),
        ],
        cost_estimate=cost(2 * 2048 * 1024 * 256, 6 << 20),
        compiler_params=room(59),
        name="partial_coeffs",
    )(where, mine, other, out_grad)


def sum_kernel(parts, out):
    total = parts[0].astype(f32)
    for i in range(1, 8):
        total += parts[i].astype(f32)
    total = total.astype(bf16)
    for i in range(8):
        out[i] = total


def sum_and_copies(parts):
    return pl.pallas_call(
        sum_kernel,
        grid=(1,),
        in_specs=[pl.BlockSpec((8, BLOCK, RANK), lambda i: (0, 0, 0))],
        out_specs=pl.BlockSpec((8, BLOCK, RANK), lambda i: (0, 0, 0)),
        out_shape=jax.ShapeDtypeStruct((8, BLOCK, RANK), bf16),
        cost_estimate=cost(8 * 65536, 2 << 20),
        compiler_params=room(8),
        name="sum_coeffs",
    )(parts)


def block_start(f):
    return jnp.minimum(ROWS * f // 16 * 16, 16 * ROWS - BLOCK)


def grad_kernel(parity, hidden, coeffs, out, rows, done):
    def load(i):
        begin = pl.multiple_of(block_start(2 * i + parity[0]), 16)
        return pltpu.make_async_copy(hidden.at[pl.ds(begin, BLOCK)], rows.at[i], done.at[i])

    def use(i):
        f = 2 * i + parity[0]
        block = jnp.dot(rows[i], coeffs[...], preferred_element_type=f32)
        block = pltpu.roll(block, BLOCK - (ROWS * f - block_start(f)), 0)
        out[i] = block[:PADDED].astype(out.dtype)

    stream(8, load, use)


def grad_blocks(parity, hidden_t, coeffs, dtype):
    return pl.pallas_call(
        grad_kernel,
        in_specs=[
            pl.BlockSpec(memory_space=pltpu.SMEM),
            pl.BlockSpec(memory_space=pl.ANY),
            pl.BlockSpec(memory_space=pltpu.VMEM),
        ],
        out_specs=pl.BlockSpec(memory_space=pltpu.VMEM),
        out_shape=jax.ShapeDtypeStruct((8, PADDED, RANK), dtype),
        scratch_shapes=[
            pltpu.VMEM((8, BLOCK, 2048), bf16),
            pltpu.SemaphoreType.DMA((8,)),
        ],
        cost_estimate=cost(2 * 2048 * 2048 * 256, 9 << 20),
        compiler_params=room(48),
        name="grad_blocks",
    )(parity, hidden_t, coeffs)


def final_kernel(
    shares, first, second, projector, new_first, new_second, update, direction, rows, blocks, came, left
):
    def load(i):
        return pltpu.make_async_copy(projector.at[:, i], rows.at[i], came.at[i])

    def store(i):
        begin = pl.multiple_of(1024 * i, 1024)
        return pltpu.make_async_copy(blocks.at[i], update.at[:, pl.ds(begin, 1024)], left.at[i])

    for i in range(8):
        load(i).start()
    grad = shares[0].astype(f32)
    for i in range(1, 8):
        grad += shares[i].astype(f32)
    grad = grad[:ROWS]
    moved = 0.9 * first[...] + 0.1 * grad
    scale = 0.95 * second[...] + 0.05 * grad * grad
    direction[...] = (moved / (jnp.sqrt(scale) + 1e-08)).astype(bf16)
    new_first[...] = moved.reshape(ROWS, 1, RANK)
    new_second[...] = scale.reshape(ROWS, 1, RANK)

    @pl.loop(0, 8)
    def _(i):
        load(i).wait()
        product = lax.dot_general(
            direction[...],
            rows[i].reshape(1024, RANK),
            (((1,), (1,)), ((), ())),
            preferred_element_type=f32,
        )
        blocks[i] = (-4.0 * product).astype(bf16)
        store(i).start()

    @pl.loop(0, 8)
    def _(i):
        store(i).wait()


def finish(shares, first, second, projector):
    vmem, any_space = pl.BlockSpec(memory_space=pltpu.VMEM), pl.BlockSpec(memory_space=pl.ANY)
    return pl.pallas_call(
        final_kernel,
        in_specs=[vmem, vmem, vmem, any_space],
        out_specs=[vmem, vmem, any_space],
        out_shape=[
            jax.ShapeDtypeStruct((ROWS, 1, RANK), f32),
            jax.ShapeDtypeStruct((ROWS, 1, RANK), f32),
            jax.ShapeDtypeStruct((ROWS, 8192), bf16),
        ],
        scratch_shapes=[
            pltpu.VMEM((ROWS, RANK), bf16),
            pltpu.VMEM((8, 8, 128, RANK), bf16),
            pltpu.VMEM((8, ROWS, 1024), bf16),
            pltpu.SemaphoreType.DMA((8,)),
            pltpu.SemaphoreType.DMA((8,)),
        ],
        cost_estimate=cost(2 * 231 * 8192 * 256, 10 << 20),
        compiler_params=room(56),
        name="adam_update",
    )(shares, first, second, projector)


def swap_cores(value):
    return lax.ppermute(value, FSDP, [(i, i ^ 1) for i in range(16)])


def shift(value, dx, dy):
    pairs = []
    for yh in range(2):
        for x in range(4):
            for core in range(2):
                to = ((yh + dy) % 2 * 4 + (x + dx) % 4) * 2 + core
                pairs.append(((yh * 4 + x) * 2 + core, to))
    return lax.ppermute(value, FSDP, pairs)


def owners_halves(candidate, root):
    yh, x, core = (lax.axis_index(a) for a in FSDP)
    halves = candidate.reshape(2, 512, RANK)
    kept = lax.dynamic_index_in_dim(halves, core, 0, keepdims=False)
    given = lax.dynamic_index_in_dim(halves, 1 - core, 0, keepdims=False)
    held = jnp.where(root % 2 == core, kept, swap_cores(given))
    dx = (x - root // 2 % 4) % 4
    dy = (yh - root // 8) % 2
    right, left, across = shift(held, 1, 0), shift(held, 3, 0), shift(held, 0, 1)
    held = jnp.where(
        (dx == 1) & (dy == 0),
        right,
        jnp.where((dx == 3) & (dy == 0), left, jnp.where((dx == 0) & (dy == 1), across, held)),
    )
    far, across = shift(held, 2, 0), shift(held, 0, 1)
    held = jnp.where(dx == 2, far, jnp.where((dx % 2 == 1) & (dy == 1), across, held))
    return held, swap_cores(held)


def local(hidden, out_grad, projector_bank, owner, first_moment, second_moment):
    core = lax.axis_index("core")
    column = lax.axis_index("x")

    mine, other = owners_halves(projector_bank[0], owner[0])
    where = jnp.stack([core, column * 2 + core]).astype(jnp.int32)
    hidden_t = hidden.T
    outgoing = partial_and_share(where, mine, other, out_grad)
    parts = lax.all_to_all(outgoing, TP, 0, 0)
    projector = lax.all_gather(parts[:, BLOCK:], ("x", "core"))
    coeffs = lax.all_to_all(sum_and_copies(parts), TP, 0, 0).reshape(2048, RANK)

    give = grad_blocks((1 - core)[None], hidden_t, coeffs, bf16)
    got = swap_cores(give)
    keep = grad_blocks(core[None], hidden_t, coeffs, f32)
    pair = (keep + got.astype(f32)).astype(bf16)
    shares = lax.all_to_all(pair, CHIPS, 0, 0)
    new_first, new_second, update = finish(shares, first_moment[0], second_moment[0], projector)
    return (new_first.transpose(1, 0, 2), new_second.transpose(1, 0, 2), update[None])


def solution(mesh):
    fine = jax.sharding.Mesh(
        mesh.devices.reshape(2, 4, 2, 4, 2), ("yh", "x", "core", "z", "yl")
    )
    in_specs = (
        P(FSDP, TP),
        P(FSDP, TP),
        P(FSDP, TP, None),
        P(),
        P(TP, FSDP, None),
        P(TP, FSDP, None),
    )
    out_specs = (P(TP, FSDP, None), P(TP, FSDP, None), P(TP, FSDP, None))
    return jax.shard_map(local, mesh=fine, in_specs=in_specs, out_specs=out_specs, check_vma=False)
```

time: 188 us -> 137 us (0.73)
  waiting for transfers between devices: 100 us -> 30.9 us
  Pallas kernels: 0 us -> 22.4 us
  blocking collectives: 22.1 us -> 43.6 us
  matrix products: 16.8 us -> 0 us
  starting transfers between devices: 25.4 us -> 17.8 us
    all_to_all x3 -> x0, waiting for transfers between devices: 52.5 us -> none  [the longest x1 26.4 us: local(): lax.all_to_all(jnp.broadcast_to(summed[None], (8, 256, 256)), TP, 0, 0)]
    all_to_all x0 -> x2, blocking collectives: none -> 43.6 us  [the longest x1 26.5 us: local(): parts = lax.all_to_all(outgoing, TP, 0, 0)]
    all_gather x1, waiting for transfers between devices: 29.1 us -> 0.01 us  [local(): projector = lax.all_gather(parts[:, BLOCK:], ('x', 'core'))]
    pallas_call x0 -> x5, Pallas kernels: none -> 22.4 us  [the longest x2 10.2 us: grad_blocks(): pl.pallas_call(grad_kernel, in_specs=[pl.BlockSpec(memory_space=pltpu.SME...]
    all_gather x1 -> x0, blocking collectives: 22.1 us -> none  [local(): own_piece = lax.all_gather(piece, FSDP, axis=0, tiled=True)]
    all_to_all x3 -> x0, starting transfers between devices: 17.2 us -> none  [the longest x1 8.46 us: local(): lax.all_to_all(projector_bank[0].reshape(16, 64, 256), FSDP, 0, 0)]
    dot_general x3 -> x0, matrix products: 16.8 us -> none  [the longest x1 7.72 us: local(): lax.dot_general(hidden, coeffs, (((0,), (0,)), ((), ())), preferred_eleme...]
    ppermute x1 -> x8, waiting for transfers between devices: 2.19 us -> 15.4 us  [the longest x5 14.3 us: shift(): return lax.ppermute(value, FSDP, pairs)]
  transfers between devices with their start and end apart: 6 -> 10, of which waited for: 6 -> 7; matrix products, arithmetic and copies ran while one was open for 7% -> 2% of each run, Pallas kernels for 0% -> 8%
where the time goes in v2:
time: 137 us
  blocking collectives  43.6 us (32%)
  waiting for transfers between devices  30.9 us (23%)
  Pallas kernels  22.4 us (16%)
  starting transfers between devices  17.8 us (13%)
  between operations  14.8 us (11%)
  local copies, waits for them, and re-layouts  4.31 us (3%)
  other arithmetic  2.89 us (2%)
    all_to_all x1, blocking collectives, local(): parts = lax.all_to_all(outgoing, TP, 0, 0)  26.5 us
    all_to_all x1, blocking collectives, local(): coeffs = lax.all_to_all(sum_and_copies(parts), TP, 0, 0).reshape(2048, RANK)  17.2 us
    all_to_all x1, waiting for transfers between devices, local(): shares = lax.all_to_all(pair, CHIPS, 0, 0)  15.5 us
    ppermute x5, waiting for transfers between devices, shift(): return lax.ppermute(value, FSDP, pairs)  14.3 us
    pallas_call x2, Pallas kernels, grad_blocks(): pl.pallas_call(grad_kernel, in_specs=[pl.BlockSpec(memory_space=pltpu.SME...  10.2 us
    ppermute x3, starting transfers between devices, swap_cores(): return lax.ppermute(value, FSDP, [(i, i ^ 1) for i in range(16)])  6.92 us
    ppermute x5, starting transfers between devices, shift(): return lax.ppermute(value, FSDP, pairs)  6.85 us
    pallas_call x1, Pallas kernels, finish(): pl.pallas_call(final_kernel, in_specs=[vmem, vmem, vmem, any_space], out_...  6.77 us
  transfers between devices with their start and end apart: 10, of which 7 were waited for; matrix products, arithmetic and copies ran while one was open for 2% of the time, Pallas kernels for 8%

profile of v2, /device:TPU:1, one launch (start us, length us, event | category | flops | bytes accessed | tf_op | source)
XLA Modules:
  0.0 136.7 jit_solution(13765234646645179693)
XLA Ops:
  7.2 0.0 all-gather.3.cloned.1.call-start
  7.2 1.0 dynamic-slice_bitcast_fusion
  8.2 1.5 %collective-permute-start = (bf16[512,256]{1,0:T(8,128)(2,1)S(1)}, bf16[512,256]{1,0:T(8,128)(2,1)S(1)}, u32[]{:S(2)}, u32[]{:S(2)}) collective-permute-start(bf16[512,256]{1,0:T(8,128)(2,1)S(1)} %dynamic-slice_bitcast_fusion), channel_id=1, source_target_pairs={{0,8},{8,0},{16,24},{24,16},{32,40},{40,32},{48,56},{56,48},{64,72... | collective-permute-start | bytes 786440 | tf_op jit(solution)/shard_map/ppermute | solution.py:203
  10.4 0.5 collective-permute-done
  10.9 1.0 bitcast_select_fusion
  11.8 3.1 %collective-permute-start.3 = (bf16[512,256]{1,0:T(8,128)(2,1)S(1)}, bf16[512,256]{1,0:T(8,128)(2,1)S(1)}, u32[]{:S(2)}, u32[]{:S(2)}) collective-permute-start(bf16[512,256]{1,0:T(8,128)(2,1)S(1)} %bitcast_select_fusion), channel_id=1, source_target_pairs={{0,64},{8,72},{16,80},{24,88},{32,96},{40,104},{48,112},{56,120},{... | collective-permute-start | bytes 786440 | tf_op jit(solution)/shard_map/ppermute | solution.py:213
  14.9 2.5 %collective-permute-start.2 = (bf16[512,256]{1,0:T(8,128)(2,1)S(1)}, bf16[512,256]{1,0:T(8,128)(2,1)S(1)}, u32[]{:S(2)}, u32[]{:S(2)}) collective-permute-start(bf16[512,256]{1,0:T(8,128)(2,1)S(1)} %bitcast_select_fusion), channel_id=1, source_target_pairs={{0,48},{8,56},{16,0},{24,8},{32,16},{40,24},{48,32},{56,40},{64,11... | collective-permute-start | bytes 786440 | tf_op jit(solution)/shard_map/ppermute | solution.py:213
  17.4 0.0 collective-permute-start.1
  17.4 3.6 %collective-permute-done.3 = bf16[512,256]{1,0:T(8,128)(2,1)S(1)} collective-permute-done((bf16[512,256]{1,0:T(8,128)(2,1)S(1)}, bf16[512,256]{1,0:T(8,128)(2,1)S(1)}, u32[]{:S(2)}, u32[]{:S(2)}) %collective-permute-start.3) | collective-permute-done | bytes 262176 | tf_op jit(solution)/shard_map/ppermute | solution.py:213
  21.0 1.4 %collective-permute-done.2 = bf16[512,256]{1,0:T(8,128)(2,1)S(1)} collective-permute-done((bf16[512,256]{1,0:T(8,128)(2,1)S(1)}, bf16[512,256]{1,0:T(8,128)(2,1)S(1)}, u32[]{:S(2)}, u32[]{:S(2)}) %collective-permute-start.2) | collective-permute-done | bytes 262176 | tf_op jit(solution)/shard_map/ppermute | solution.py:213
  22.4 3.1 %collective-permute-done.1 = bf16[512,256]{1,0:T(8,128)(2,1)S(1)} collective-permute-done((bf16[512,256]{1,0:T(8,128)(2,1)S(1)}, bf16[512,256]{1,0:T(8,128)(2,1)S(1)}, u32[]{:S(2)}, u32[]{:S(2)}) %collective-permute-start.1) | collective-permute-done | bytes 262176 | tf_op jit(solution)/shard_map/ppermute | solution.py:213
  25.5 0.2 collective-permute-start.5
  25.7 1.1 collective-permute-start.4
  26.8 6.2 %collective-permute-done.5 = bf16[512,256]{1,0:T(8,128)(2,1)S(1)} collective-permute-done((bf16[512,256]{1,0:T(8,128)(2,1)S(1)}, bf16[512,256]{1,0:T(8,128)(2,1)S(1)}, u32[]{:S(2)}, u32[]{:S(2)}) %collective-permute-start.5) | collective-permute-done | bytes 262176 | tf_op jit(solution)/shard_map/ppermute | solution.py:213
  33.1 0.0 collective-permute-done.4
  33.1 0.0 copy-start.1
  33.1 3.0 %collective-permute-start.6 = (bf16[512,256]{1,0:T(8,128)(2,1)S(1)}, bf16[512,256]{1,0:T(8,128)(2,1)S(1)}, u32[]{:S(2)}, u32[]{:S(2)}) collective-permute-start(bf16[512,256]{1,0:T(8,128)(2,1)S(1)} %select_select_fusion.mine), channel_id=1, source_target_pairs={{0,8},{8,0},{16,24},{24,16},{32,40},{40,32},{48,56},{56,48},{64,72... | collective-permute-start | bytes 786440 | tf_op jit(solution)/shard_map/ppermute | solution.py:203
  36.1 0.6 pad_add_fusion.where
  36.7 0.6 collective-permute-done.6.other
  37.2 0.0 copy-done.1
  37.2 0.0 copy-start.2
  37.2 0.7 copy-done.2
  37.9 5.3 %partial_coeffs.1 = bf16[8,384,256]{2,1,0:T(8,128)(2,1)} custom-call(s32[2]{0:T(128)} %pad_add_fusion.where, bf16[512,256]{1,0:T(8,128)(2,1)} %copy-done.1, bf16[512,256]{1,0:T(8,128)(2,1)} %copy-done.2, bf16[2048,1024]{1,0:T(8,128)(2,1)} %grad.1), custom_call_target="tpu_custom_call" | custom-call | flops 1073741824 | bytes 6291456 | tf_op jit(solution)/shard_map/partial_coeffs/pallas_call | solution.py:63
  43.2 26.5 %all_to_all.15.parts = bf16[8,384,256]{2,1,0:T(8,128)(2,1)S(1)} all-to-all(bf16[8,384,256]{2,1,0:T(8,128)(2,1)} %partial_coeffs.1), channel_id=1, replica_groups=mesh['yh'=2,'x'=4,'core'=2,'z'=4,'yl'=2] {'z','yl'}, dimensions={0} | all-to-all | bytes 3145728 | tf_op jit(solution)/shard_map/all_to_all | solution.py:243
  69.7 0.9 slice.4
  70.5 0.0 all-gather.3.cloned.1.call-update
  70.6 0.1 sum_coeffs.1
  70.7 17.2 %all_to_all.16 = bf16[8,256,256]{2,1,0:T(8,128)(2,1)S(1)} all-to-all(bf16[8,256,256]{2,1,0:T(8,128)(2,1)S(1)} %sum_coeffs.1), channel_id=1, replica_groups=mesh['yh'=2,'x'=4,'core'=2,'z'=4,'yl'=2] {'z','yl'}, dimensions={0} | all-to-all | bytes 2097152 | tf_op jit(solution)/shard_map/all_to_all | solution.py:245
  87.9 5.1 %grad_blocks.3 = bf16[8,232,256]{2,1,0:T(8,128)(2,1)S(1)} custom-call(s32[1]{0:T(128)} %bitcast.8.parity, bf16[3696,2048]{1,0:T(8,128)(2,1)} %bitcast.25, bf16[2048,256]{1,0:T(8,128)(2,1)S(1)} %bitcast.23), custom_call_target="tpu_custom_call" | custom-call | flops 2147483648 | bytes 9437184 | tf_op jit(solution)/shard_map/grad_blocks/pallas_call | solution.py:120
  93.0 2.5 %collective-permute-start.7 = (bf16[8,232,256]{2,1,0:T(8,128)(2,1)S(1)}, bf16[8,232,256]{2,1,0:T(8,128)(2,1)S(1)}, u32[]{:S(2)}, u32[]{:S(2)}) collective-permute-start(bf16[8,232,256]{2,1,0:T(8,128)(2,1)S(1)} %grad_blocks.3), channel_id=1, source_target_pairs={{0,8},{8,0},{16,24},{24,16},{32,40},{40,32},{48,56},{56,48},{64,72... | collective-permute-start | bytes 2850824 | tf_op jit(solution)/shard_map/ppermute | solution.py:203
  95.5 5.1 %grad_blocks.2 = f32[8,232,256]{2,1,0:T(8,128)S(1)} custom-call(s32[1]{0:T(128)} %bitcast.parity, bf16[3696,2048]{1,0:T(8,128)(2,1)} %bitcast.26, bf16[2048,256]{1,0:T(8,128)(2,1)S(1)} %bitcast.24), custom_call_target="tpu_custom_call" | custom-call | flops 2147483648 | bytes 9437184 | tf_op jit(solution)/shard_map/grad_blocks/pallas_call | solution.py:120
  100.5 0.0 copy-start.3
  100.6 0.0 copy-start.4
  100.6 0.0 collective-permute-done.7
  100.6 1.2 add_convert_fusion
  101.8 4.0 %all-to-all-start.2 = ((bf16[8,232,256]{2,1,0:T(8,128)(2,1)}), bf16[8,232,256]{2,1,0:T(8,128)(2,1)S(1)}, u32[]{:S(2)}, u32[]{:S(2)}) async-start(bf16[8,232,256]{2,1,0:T(8,128)(2,1)} %add_convert_fusion), calls=%async_computation.2 | async-start | bytes 1900544 | tf_op jit(solution)/shard_map/all_to_all | solution.py:251
  105.8 0.0 copy-done.3
  105.8 0.0 copy-done.4
  105.8 0.8 copy_bitcast_fusion
  106.6 15.5 %all-to-all-done.2.shares = bf16[8,232,256]{2,1,0:T(8,128)(2,1)S(1)} async-done(((bf16[8,232,256]{2,1,0:T(8,128)(2,1)}), bf16[8,232,256]{2,1,0:T(8,128)(2,1)S(1)}, u32[]{:S(2)}, u32[]{:S(2)}) %all-to-all-start.2) | async-done | bytes 950304 | tf_op jit(solution)/shard_map/all_to_all | solution.py:251
  122.1 0.0 copy-start
  122.1 0.0 all-gather.3.cloned.1.call-done
  122.1 0.9 copy-done
  123.1 6.8 %adam_update.1 = (f32[231,1,256]{2,1,0:T(1,128)}, f32[231,1,256]{2,1,0:T(1,128)}, bf16[231,8192]{1,0:T(8,128)(2,1)}) custom-call(bf16[8,232,256]{2,1,0:T(8,128)(2,1)} %copy-done, f32[231,256]{1,0:T(8,128)} %get-tuple-element.10.first, f32[231,256]{1,0:T(8,128)} %get-tuple-element.9.second, bf16[8,8,128,256]{3,2,1,0:T(8,128)(2,1)} %bitcast.27), custom_call_target="tpu_custom_call" | custom-call | flops 968884224 | bytes 10485760 | tf_op jit(solution)/shard_map/adam_update/pallas_call | solution.py:180
  (2 shorter events, 0.1 us)
Async XLA Ops:
  7.2 115.0 %all-gather.3.cloned.1.call-start = ((), (), s32[]{:S(2)}) async-start(), calls=%async_computation.3 | async-start | bytes 4718592 | tf_op jit(solution)/shard_map/all_gather | solution.py:244
  8.2 2.7 %collective-permute-start = (bf16[512,256]{1,0:T(8,128)(2,1)S(1)}, bf16[512,256]{1,0:T(8,128)(2,1)S(1)}, u32[]{:S(2)}, u32[]{:S(2)}) collective-permute-start(bf16[512,256]{1,0:T(8,128)(2,1)S(1)} %dynamic-slice_bitcast_fusion), channel_id=1, source_target_pairs={{0,8},{8,0},{16,24},{24,16},{32,40},{40,32},{48,56},{56,48},{64,72... | collective-permute-start | bytes 786440 | tf_op jit(solution)/shard_map/ppermute | solution.py:203
  11.8 9.2 %collective-permute-start.3 = (bf16[512,256]{1,0:T(8,128)(2,1)S(1)}, bf16[512,256]{1,0:T(8,128)(2,1)S(1)}, u32[]{:S(2)}, u32[]{:S(2)}) collective-permute-start(bf16[512,256]{1,0:T(8,128)(2,1)S(1)} %bitcast_select_fusion), channel_id=1, source_target_pairs={{0,64},{8,72},{16,80},{24,88},{32,96},{40,104},{48,112},{56,120},{... | collective-permute-start | bytes 786440 | tf_op jit(solution)/shard_map/ppermute | solution.py:213
  14.9 7.5 %collective-permute-start.2 = (bf16[512,256]{1,0:T(8,128)(2,1)S(1)}, bf16[512,256]{1,0:T(8,128)(2,1)S(1)}, u32[]{:S(2)}, u32[]{:S(2)}) collective-permute-start(bf16[512,256]{1,0:T(8,128)(2,1)S(1)} %bitcast_select_fusion), channel_id=1, source_target_pairs={{0,48},{8,56},{16,0},{24,8},{32,16},{40,24},{48,32},{56,40},{64,11... | collective-permute-start | bytes 786440 | tf_op jit(solution)/shard_map/ppermute | solution.py:213
  17.4 8.1 %collective-permute-start.1 = (bf16[512,256]{1,0:T(8,128)(2,1)S(1)}, bf16[512,256]{1,0:T(8,128)(2,1)S(1)}, u32[]{:S(2)}, u32[]{:S(2)}) collective-permute-start(bf16[512,256]{1,0:T(8,128)(2,1)S(1)} %bitcast_select_fusion), channel_id=1, source_target_pairs={{0,16},{8,24},{16,32},{24,40},{32,48},{40,56},{48,0},{56,8},{64,80... | collective-permute-start | bytes 786440 | tf_op jit(solution)/shard_map/ppermute | solution.py:213
  25.5 7.5 %collective-permute-start.5 = (bf16[512,256]{1,0:T(8,128)(2,1)S(1)}, bf16[512,256]{1,0:T(8,128)(2,1)S(1)}, u32[]{:S(2)}, u32[]{:S(2)}) collective-permute-start(bf16[512,256]{1,0:T(8,128)(2,1)S(1)} %select_select_fusion.1), channel_id=1, source_target_pairs={{0,64},{8,72},{16,80},{24,88},{32,96},{40,104},{48,112},{56,120},{... | collective-permute-start | bytes 786440 | tf_op jit(solution)/shard_map/ppermute | solution.py:213
  25.7 7.3 %collective-permute-start.4 = (bf16[512,256]{1,0:T(8,128)(2,1)S(1)}, bf16[512,256]{1,0:T(8,128)(2,1)S(1)}, u32[]{:S(2)}, u32[]{:S(2)}) collective-permute-start(bf16[512,256]{1,0:T(8,128)(2,1)S(1)} %select_select_fusion.1), channel_id=1, source_target_pairs={{0,32},{8,40},{16,48},{24,56},{32,0},{40,8},{48,16},{56,24},{64,96... | collective-permute-start | bytes 786440 | tf_op jit(solution)/shard_map/ppermute | solution.py:213
  33.1 4.1 %copy-start.1 = (bf16[512,256]{1,0:T(8,128)(2,1)}, bf16[512,256]{1,0:T(8,128)(2,1)S(1)}, u32[]{:S(2)}) copy-start(bf16[512,256]{1,0:T(8,128)(2,1)S(1)} %select_select_fusion.mine) | copy-start | bytes 786436
  33.1 4.1 %collective-permute-start.6 = (bf16[512,256]{1,0:T(8,128)(2,1)S(1)}, bf16[512,256]{1,0:T(8,128)(2,1)S(1)}, u32[]{:S(2)}, u32[]{:S(2)}) collective-permute-start(bf16[512,256]{1,0:T(8,128)(2,1)S(1)} %select_select_fusion.mine), channel_id=1, source_target_pairs={{0,8},{8,0},{16,24},{24,16},{32,40},{40,32},{48,56},{56,48},{64,72... | collective-permute-start | bytes 786440 | tf_op jit(solution)/shard_map/ppermute | solution.py:203
  37.2 0.7 copy-start.2
  93.0 7.5 %collective-permute-start.7 = (bf16[8,232,256]{2,1,0:T(8,128)(2,1)S(1)}, bf16[8,232,256]{2,1,0:T(8,128)(2,1)S(1)}, u32[]{:S(2)}, u32[]{:S(2)}) collective-permute-start(bf16[8,232,256]{2,1,0:T(8,128)(2,1)S(1)} %grad_blocks.3), channel_id=1, source_target_pairs={{0,8},{8,0},{16,24},{24,16},{32,40},{40,32},{48,56},{56,48},{64,72... | collective-permute-start | bytes 2850824 | tf_op jit(solution)/shard_map/ppermute | solution.py:203
  100.5 5.2 %copy-start.3 = (f32[1,231,256]{2,0,1:T(1,128)S(1)}, f32[1,231,256]{2,0,1:T(1,128)}, u32[]{:S(2)}) copy-start(f32[1,231,256]{2,0,1:T(1,128)} %param.11) | copy-start | bytes 709636
  100.6 5.2 %copy-start.4 = (f32[1,231,256]{2,0,1:T(1,128)S(1)}, f32[1,231,256]{2,0,1:T(1,128)}, u32[]{:S(2)}) copy-start(f32[1,231,256]{2,0,1:T(1,128)} %param.10) | copy-start | bytes 709636
  101.8 20.3 %all-to-all-start.2 = ((bf16[8,232,256]{2,1,0:T(8,128)(2,1)}), bf16[8,232,256]{2,1,0:T(8,128)(2,1)S(1)}, u32[]{:S(2)}, u32[]{:S(2)}) async-start(bf16[8,232,256]{2,1,0:T(8,128)(2,1)} %add_convert_fusion), calls=%async_computation.2 | async-start | bytes 1900544 | tf_op jit(solution)/shard_map/all_to_all | solution.py:251
  122.1 0.9 copy-start
Sparse Core Ops, SparseCore 0:
  70.7 30.3 all-gather.2

commit v3 on v2

--- a/solution.py
+++ b/solution.py
@@ -23,55 +23,31 @@
     return pltpu.CompilerParams(vmem_limit_bytes=mebibytes << 20)
 
 
-def stream(count, load, use):
-    for i in range(3):
-        load(i).start()
-
-    @pl.loop(0, count)
+def partial_kernel(where, mine, other, grad, out, piece):
+    core, half = where[0], mine.shape[0]
+    piece[pl.ds(pl.multiple_of(core * half, half), half), :] = mine[...]
+    piece[pl.ds(pl.multiple_of((1 - core) * half, half), half), :] = other[...]
+
+    @pl.loop(0, 4)
     def _(i):
-        load(i).wait()
-
-        @pl.when(i + 3 < count)
-        def _():
-            load(i + 3).start()
-
-        use(i)
-
-
-def partial_kernel(where, mine, other, grad, out, piece, rows, done):
-    core, share = where[0], where[1]
-    half = mine.shape[0]
-
-    def load(i):
-        begin = 512 * i if isinstance(i, int) else pl.multiple_of(512 * i, 512)
-        return pltpu.make_async_copy(grad.at[pl.ds(begin, 512)], rows.at[i], done.at[i])
-
-    def use(i):
-        product = jnp.dot(rows[i], piece[...], preferred_element_type=f32).astype(bf16)
-        below = piece[pl.ds(pl.multiple_of(share * 128, 128), 128), :]
+        rows = grad[pl.ds(pl.multiple_of(512 * i, 512), 512), :]
+        product = jnp.dot(rows, piece[...], preferred_element_type=f32).astype(bf16)
+        below = piece[pl.ds(pl.multiple_of(where[1] * 128, 128), 128), :]
         for j in range(2):
             out[2 * i + j, :BLOCK, :] = product[BLOCK * j : BLOCK * (j + 1)]
             out[2 * i + j, BLOCK:, :] = below
 
-    piece[pl.ds(pl.multiple_of(core * half, half), half), :] = mine[...]
-    piece[pl.ds(pl.multiple_of((1 - core) * half, half), half), :] = other[...]
-    stream(4, load, use)
-
 
 def partial_and_share(where, mine, other, out_grad):
-    vmem, any_space = pl.BlockSpec(memory_space=pltpu.VMEM), pl.BlockSpec(memory_space=pl.ANY)
+    vmem = pl.BlockSpec(memory_space=pltpu.VMEM)
     return pl.pallas_call(
         partial_kernel,
-        in_specs=[pl.BlockSpec(memory_space=pltpu.SMEM), vmem, vmem, any_space],
+        in_specs=[pl.BlockSpec(memory_space=pltpu.SMEM), vmem, vmem, vmem],
         out_specs=vmem,
         out_shape=jax.ShapeDtypeStruct((8, BLOCK + 128, RANK), bf16),
-        scratch_shapes=[
-            pltpu.VMEM((1024, RANK), bf16),
-            pltpu.VMEM((4, 512, 1024), bf16),
-            pltpu.SemaphoreType.DMA((4,)),
-        ],
+        scratch_shapes=[pltpu.VMEM((1024, RANK), bf16)],
         cost_estimate=cost(2 * 2048 * 1024 * 256, 6 << 20),
-        compiler_params=room(59),
+        compiler_params=room(12),
         name="partial_coeffs",
     )(where, mine, other, out_grad)
 
@@ -107,13 +83,25 @@
         begin = pl.multiple_of(block_start(2 * i + parity[0]), 16)
         return pltpu.make_async_copy(hidden.at[pl.ds(begin, BLOCK)], rows.at[i], done.at[i])
 
-    def use(i):
-        f = 2 * i + parity[0]
-        block = jnp.dot(rows[i], coeffs[...], preferred_element_type=f32)
-        block = pltpu.roll(block, BLOCK - (ROWS * f - block_start(f)), 0)
-        out[i] = block[:PADDED].astype(out.dtype)
-
-    stream(8, load, use)
+    for i in range(4):
+        load(i).start()
+
+    @pl.loop(0, 4)
+    def _(pair):
+        for j in range(2):
+            load(2 * pair + j).wait()
+
+        @pl.when(pair < 2)
+        def _():
+            for j in range(2):
+                load(2 * pair + 4 + j).start()
+
+        for j in range(2):
+            i = 2 * pair + j
+            f = 2 * i + parity[0]
+            block = jnp.dot(rows[i], coeffs[...], preferred_element_type=f32)
+            block = pltpu.roll(block, BLOCK - (ROWS * f - block_start(f)), 0)
+            out[i] = block[:PADDED].astype(out.dtype)
 
 
 def grad_blocks(parity, hidden_t, coeffs, dtype):
@@ -137,7 +125,8 @@
 
 
 def final_kernel(
-    shares, first, second, projector, new_first, new_second, update, direction, rows, blocks, came, left
+    shares, first, second, projector, new_first, new_second, update,
+    parts, old, new, direction, rows, blocks, came, left,
 ):
     def load(i):
         return pltpu.make_async_copy(projector.at[:, i], rows.at[i], came.at[i])
@@ -146,17 +135,32 @@
         begin = pl.multiple_of(1024 * i, 1024)
         return pltpu.make_async_copy(blocks.at[i], update.at[:, pl.ds(begin, 1024)], left.at[i])
 
+    early = [
+        pltpu.make_async_copy(shares, parts, came.at[8]),
+        pltpu.make_async_copy(first, old.at[0], came.at[9]),
+        pltpu.make_async_copy(second, old.at[1], came.at[10]),
+    ]
+    late = [
+        pltpu.make_async_copy(new.at[0], new_first, left.at[8]),
+        pltpu.make_async_copy(new.at[1], new_second, left.at[9]),
+    ]
+    for copy in early:
+        copy.start()
     for i in range(8):
         load(i).start()
-    grad = shares[0].astype(f32)
+    for copy in early:
+        copy.wait()
+    grad = parts[0].astype(f32)
     for i in range(1, 8):
-        grad += shares[i].astype(f32)
+        grad += parts[i].astype(f32)
     grad = grad[:ROWS]
-    moved = 0.9 * first[...] + 0.1 * grad
-    scale = 0.95 * second[...] + 0.05 * grad * grad
+    moved = 0.9 * old[0].reshape(ROWS, RANK) + 0.1 * grad
+    scale = 0.95 * old[1].reshape(ROWS, RANK) + 0.05 * grad * grad
     direction[...] = (moved / (jnp.sqrt(scale) + 1e-08)).astype(bf16)
-    new_first[...] = moved.reshape(ROWS, 1, RANK)
-    new_second[...] = scale.reshape(ROWS, 1, RANK)
+    new[0] = moved.reshape(ROWS, 1, RANK)
+    new[1] = scale.reshape(ROWS, 1, RANK)
+    for copy in late:
+        copy.start()
 
     @pl.loop(0, 8)
     def _(i):
@@ -174,27 +178,33 @@
     def _(i):
         store(i).wait()
 
+    for copy in late:
+        copy.wait()
+
 
 def finish(shares, first, second, projector):
-    vmem, any_space = pl.BlockSpec(memory_space=pltpu.VMEM), pl.BlockSpec(memory_space=pl.ANY)
+    any_space = pl.BlockSpec(memory_space=pl.ANY)
     return pl.pallas_call(
         final_kernel,
-        in_specs=[vmem, vmem, vmem, any_space],
-        out_specs=[vmem, vmem, any_space],
+        in_specs=[any_space] * 4,
+        out_specs=[any_space] * 3,
         out_shape=[
             jax.ShapeDtypeStruct((ROWS, 1, RANK), f32),
             jax.ShapeDtypeStruct((ROWS, 1, RANK), f32),
             jax.ShapeDtypeStruct((ROWS, 8192), bf16),
         ],
         scratch_shapes=[
+            pltpu.VMEM((8, PADDED, RANK), bf16),
+            pltpu.VMEM((2, ROWS, 1, RANK), f32),
+            pltpu.VMEM((2, ROWS, 1, RANK), f32),
             pltpu.VMEM((ROWS, RANK), bf16),
             pltpu.VMEM((8, 8, 128, RANK), bf16),
             pltpu.VMEM((8, ROWS, 1024), bf16),
-            pltpu.SemaphoreType.DMA((8,)),
-            pltpu.SemaphoreType.DMA((8,)),
+            pltpu.SemaphoreType.DMA((11,)),
+            pltpu.SemaphoreType.DMA((10,)),
         ],
         cost_estimate=cost(2 * 231 * 8192 * 256, 10 << 20),
-        compiler_params=room(56),
+        compiler_params=room(57),
         name="adam_update",
     )(shares, first, second, projector)
 
@@ -238,18 +248,20 @@
 
     mine, other = owners_halves(projector_bank[0], owner[0])
     where = jnp.stack([core, column * 2 + core]).astype(jnp.int32)
-    hidden_t = hidden.T
     outgoing = partial_and_share(where, mine, other, out_grad)
     parts = lax.all_to_all(outgoing, TP, 0, 0)
     projector = lax.all_gather(parts[:, BLOCK:], ("x", "core"))
     coeffs = lax.all_to_all(sum_and_copies(parts), TP, 0, 0).reshape(2048, RANK)
 
+    hidden_t = hidden.T
     give = grad_blocks((1 - core)[None], hidden_t, coeffs, bf16)
     got = swap_cores(give)
     keep = grad_blocks(core[None], hidden_t, coeffs, f32)
     pair = (keep + got.astype(f32)).astype(bf16)
     shares = lax.all_to_all(pair, CHIPS, 0, 0)
-    new_first, new_second, update = finish(shares, first_moment[0], second_moment[0], projector)
+    new_first, new_second, update = finish(
+        shares, first_moment.transpose(1, 0, 2), second_moment.transpose(1, 0, 2), projector
+    )
     return (new_first.transpose(1, 0, 2), new_second.transpose(1, 0, 2), update[None])
 
 

time: 137 us -> 131 us (0.956)
  blocking collectives: 43.6 us -> 62.9 us
  waiting for transfers between devices: 30.9 us -> 15.9 us
  Pallas kernels: 22.4 us -> 18 us
  starting transfers between devices: 17.8 us -> 13.8 us
  other arithmetic: 2.89 us -> 1.4 us
    all_to_all x0 -> x1, blocking collectives: none -> 19.5 us  [local(): shares = lax.all_to_all(pair, CHIPS, 0, 0)]
    all_to_all x1 -> x0, waiting for transfers between devices: 15.5 us -> none  [local(): shares = lax.all_to_all(pair, CHIPS, 0, 0)]
    all_to_all x1 -> x0, starting transfers between devices: 3.97 us -> none  [local(): shares = lax.all_to_all(pair, CHIPS, 0, 0)]
    pallas_call x1, Pallas kernels: 5.26 us -> 2.33 us  [partial_and_share(): pl.pallas_call(partial_kernel, in_specs=[pl.BlockSpec(memory_space=pltpu....]
  transfers between devices with their start and end apart: 10 -> 9, of which waited for: 7 -> 6; matrix products, arithmetic and copies ran while one was open for 2% -> 0% of each run, Pallas kernels for 8% -> 8%
where the time goes in v3:
time: 131 us
  blocking collectives  62.9 us (48%)
  Pallas kernels  18 us (14%)
  waiting for transfers between devices  15.9 us (12%)
  between operations  14.8 us (11%)
  starting transfers between devices  13.8 us (11%)
  local copies, waits for them, and re-layouts  3.99 us (3%)
  other arithmetic  1.4 us (1%)
    all_to_all x1, blocking collectives, local(): parts = lax.all_to_all(outgoing, TP, 0, 0)  26.2 us
    all_to_all x1, blocking collectives, local(): shares = lax.all_to_all(pair, CHIPS, 0, 0)  19.5 us
    all_to_all x1, blocking collectives, local(): coeffs = lax.all_to_all(sum_and_copies(parts), TP, 0, 0).reshape(2048, RANK)  17.2 us
    ppermute x5, waiting for transfers between devices, shift(): return lax.ppermute(value, FSDP, pairs)  14.3 us
    pallas_call x2, Pallas kernels, grad_blocks(): pl.pallas_call(grad_kernel, in_specs=[pl.BlockSpec(memory_space=pltpu.SME...  10.1 us
    ppermute x3, starting transfers between devices, swap_cores(): return lax.ppermute(value, FSDP, [(i, i ^ 1) for i in range(16)])  6.93 us
    ppermute x5, starting transfers between devices, shift(): return lax.ppermute(value, FSDP, pairs)  6.85 us
    pallas_call x1, Pallas kernels, finish(): pl.pallas_call(final_kernel, in_specs=[any_space] * 4, out_specs=[any_spa...  5.49 us
  transfers between devices with their start and end apart: 9, of which 6 were waited for; matrix products, arithmetic and copies ran while one was open for 0% of the time, Pallas kernels for 8%

profile of v3, /device:TPU:1, one launch (start us, length us, event | category | flops | bytes accessed | tf_op | source)
XLA Modules:
  0.0 130.9 jit_solution(9930397621890551322)
XLA Ops:
  7.2 0.0 all-gather.3.cloned.1.call-start
  7.2 1.0 dynamic-slice_bitcast_fusion
  8.2 1.5 %collective-permute-start = (bf16[512,256]{1,0:T(8,128)(2,1)S(1)}, bf16[512,256]{1,0:T(8,128)(2,1)S(1)}, u32[]{:S(2)}, u32[]{:S(2)}) collective-permute-start(bf16[512,256]{1,0:T(8,128)(2,1)S(1)} %dynamic-slice_bitcast_fusion), channel_id=1, source_target_pairs={{0,8},{8,0},{16,24},{24,16},{32,40},{40,32},{48,56},{56,48},{64,72... | collective-permute-start | bytes 786440 | tf_op jit(solution)/shard_map/ppermute | solution.py:213
  10.4 0.5 collective-permute-done
  10.9 1.0 bitcast_select_fusion
  11.8 3.1 %collective-permute-start.3 = (bf16[512,256]{1,0:T(8,128)(2,1)S(1)}, bf16[512,256]{1,0:T(8,128)(2,1)S(1)}, u32[]{:S(2)}, u32[]{:S(2)}) collective-permute-start(bf16[512,256]{1,0:T(8,128)(2,1)S(1)} %bitcast_select_fusion), channel_id=1, source_target_pairs={{0,64},{8,72},{16,80},{24,88},{32,96},{40,104},{48,112},{56,120},{... | collective-permute-start | bytes 786440 | tf_op jit(solution)/shard_map/ppermute | solution.py:223
  14.9 2.5 %collective-permute-start.2 = (bf16[512,256]{1,0:T(8,128)(2,1)S(1)}, bf16[512,256]{1,0:T(8,128)(2,1)S(1)}, u32[]{:S(2)}, u32[]{:S(2)}) collective-permute-start(bf16[512,256]{1,0:T(8,128)(2,1)S(1)} %bitcast_select_fusion), channel_id=1, source_target_pairs={{0,48},{8,56},{16,0},{24,8},{32,16},{40,24},{48,32},{56,40},{64,11... | collective-permute-start | bytes 786440 | tf_op jit(solution)/shard_map/ppermute | solution.py:223
  17.4 0.0 collective-permute-start.1
  17.4 3.6 %collective-permute-done.3 = bf16[512,256]{1,0:T(8,128)(2,1)S(1)} collective-permute-done((bf16[512,256]{1,0:T(8,128)(2,1)S(1)}, bf16[512,256]{1,0:T(8,128)(2,1)S(1)}, u32[]{:S(2)}, u32[]{:S(2)}) %collective-permute-start.3) | collective-permute-done | bytes 262176 | tf_op jit(solution)/shard_map/ppermute | solution.py:223
  21.0 1.4 %collective-permute-done.2 = bf16[512,256]{1,0:T(8,128)(2,1)S(1)} collective-permute-done((bf16[512,256]{1,0:T(8,128)(2,1)S(1)}, bf16[512,256]{1,0:T(8,128)(2,1)S(1)}, u32[]{:S(2)}, u32[]{:S(2)}) %collective-permute-start.2) | collective-permute-done | bytes 262176 | tf_op jit(solution)/shard_map/ppermute | solution.py:223
  22.4 3.1 %collective-permute-done.1 = bf16[512,256]{1,0:T(8,128)(2,1)S(1)} collective-permute-done((bf16[512,256]{1,0:T(8,128)(2,1)S(1)}, bf16[512,256]{1,0:T(8,128)(2,1)S(1)}, u32[]{:S(2)}, u32[]{:S(2)}) %collective-permute-start.1) | collective-permute-done | bytes 262176 | tf_op jit(solution)/shard_map/ppermute | solution.py:223
  25.5 0.2 collective-permute-start.5
  25.7 1.1 collective-permute-start.4
  26.8 6.2 %collective-permute-done.5 = bf16[512,256]{1,0:T(8,128)(2,1)S(1)} collective-permute-done((bf16[512,256]{1,0:T(8,128)(2,1)S(1)}, bf16[512,256]{1,0:T(8,128)(2,1)S(1)}, u32[]{:S(2)}, u32[]{:S(2)}) %collective-permute-start.5) | collective-permute-done | bytes 262176 | tf_op jit(solution)/shard_map/ppermute | solution.py:223
  33.1 0.0 collective-permute-done.4
  33.1 3.0 %collective-permute-start.6 = (bf16[512,256]{1,0:T(8,128)(2,1)S(1)}, bf16[512,256]{1,0:T(8,128)(2,1)S(1)}, u32[]{:S(2)}, u32[]{:S(2)}) collective-permute-start(bf16[512,256]{1,0:T(8,128)(2,1)S(1)} %select_select_fusion.mine), channel_id=1, source_target_pairs={{0,8},{8,0},{16,24},{24,16},{32,40},{40,32},{48,56},{56,48},{64,72... | collective-permute-start | bytes 786440 | tf_op jit(solution)/shard_map/ppermute | solution.py:213
  36.1 0.1 pad_add_fusion.where
  36.1 1.1 collective-permute-done.6.other
  37.2 0.0 copy-start
  37.2 2.2 %copy-done = bf16[2048,1024]{1,0:T(8,128)(2,1)S(1)} copy-done((bf16[2048,1024]{1,0:T(8,128)(2,1)S(1)}, bf16[2048,1024]{1,0:T(8,128)(2,1)}, u32[]{:S(2)}) %copy-start) | copy-done | bytes 4194328
  39.4 2.3 %partial_coeffs.1 = bf16[8,384,256]{2,1,0:T(8,128)(2,1)S(1)} custom-call(s32[2]{0:T(128)S(1)} %pad_add_fusion.where, bf16[512,256]{1,0:T(8,128)(2,1)S(1)} %select_select_fusion.mine, bf16[512,256]{1,0:T(8,128)(2,1)S(1)} %collective-permute-done.6.other, bf16[2048,1024]{1,0:T(8,128)(2,1)S(1)} %copy-done), custom_call_target="tpu_custom_call" | custom-call | flops 1073741824 | bytes 6291456 | tf_op jit(solution)/shard_map/partial_coeffs/pallas_call | solution.py:43
  41.8 26.2 %all_to_all.15.parts = bf16[8,384,256]{2,1,0:T(8,128)(2,1)S(1)} all-to-all(bf16[8,384,256]{2,1,0:T(8,128)(2,1)S(1)} %partial_coeffs.1), channel_id=1, replica_groups=mesh['yh'=2,'x'=4,'core'=2,'z'=4,'yl'=2] {'z','yl'}, dimensions={0} | all-to-all | bytes 3145728 | tf_op jit(solution)/shard_map/all_to_all | solution.py:252
  68.0 0.8 slice.4
  68.8 0.0 all-gather.3.cloned.1.call-update
  68.8 0.1 sum_coeffs.1
  69.0 17.2 %all_to_all.16 = bf16[8,256,256]{2,1,0:T(8,128)(2,1)S(1)} all-to-all(bf16[8,256,256]{2,1,0:T(8,128)(2,1)S(1)} %sum_coeffs.1), channel_id=1, replica_groups=mesh['yh'=2,'x'=4,'core'=2,'z'=4,'yl'=2] {'z','yl'}, dimensions={0} | all-to-all | bytes 2097152 | tf_op jit(solution)/shard_map/all_to_all | solution.py:254
  86.2 5.1 %grad_blocks.3 = bf16[8,232,256]{2,1,0:T(8,128)(2,1)S(1)} custom-call(s32[1]{0:T(128)} %bitcast.8.parity, bf16[3696,2048]{1,0:T(8,128)(2,1)} %bitcast.23, bf16[2048,256]{1,0:T(8,128)(2,1)S(1)} %bitcast.21), custom_call_target="tpu_custom_call" | custom-call | flops 2147483648 | bytes 9437184 | tf_op jit(solution)/shard_map/grad_blocks/pallas_call | solution.py:108
  91.3 2.5 %collective-permute-start.7 = (bf16[8,232,256]{2,1,0:T(8,128)(2,1)S(1)}, bf16[8,232,256]{2,1,0:T(8,128)(2,1)S(1)}, u32[]{:S(2)}, u32[]{:S(2)}) collective-permute-start(bf16[8,232,256]{2,1,0:T(8,128)(2,1)S(1)} %grad_blocks.3), channel_id=1, source_target_pairs={{0,8},{8,0},{16,24},{24,16},{32,40},{40,32},{48,56},{56,48},{64,72... | collective-permute-start | bytes 2850824 | tf_op jit(solution)/shard_map/ppermute | solution.py:213
  93.7 5.0 %grad_blocks.2 = f32[8,232,256]{2,1,0:T(8,128)S(1)} custom-call(s32[1]{0:T(128)} %bitcast.parity, bf16[3696,2048]{1,0:T(8,128)(2,1)} %bitcast.24, bf16[2048,256]{1,0:T(8,128)(2,1)S(1)} %bitcast.22), custom_call_target="tpu_custom_call" | custom-call | flops 2147483648 | bytes 9437184 | tf_op jit(solution)/shard_map/grad_blocks/pallas_call | solution.py:108
  98.7 0.0 collective-permute-done.7
  98.7 0.3 add_convert_fusion
  99.0 19.5 %all_to_all.17.shares = bf16[8,232,256]{2,1,0:T(8,128)(2,1)} all-to-all(bf16[8,232,256]{2,1,0:T(8,128)(2,1)S(1)} %add_convert_fusion), channel_id=1, replica_groups=mesh['yh'=2,'x'=4,'core'=2,'z'=4,'yl'=2] {'yh','x'}, dimensions={0} | all-to-all | bytes 1900544 | tf_op jit(solution)/shard_map/all_to_all | solution.py:261
  118.5 0.0 all-gather.3.cloned.1.call-done
  118.5 5.5 %adam_update.1 = (f32[231,1,256]{2,1,0:T(1,128)}, f32[231,1,256]{2,1,0:T(1,128)}, bf16[231,8192]{1,0:T(8,128)(2,1)}) custom-call(bf16[8,232,256]{2,1,0:T(8,128)(2,1)} %all_to_all.17.shares, f32[231,1,256]{2,1,0:T(1,128)} %bitcast.28, f32[231,1,256]{2,1,0:T(1,128)} %bitcast.29, bf16[8,8,128,256]{3,2,1,0:T(8,128)(2,1)} %bitcast.25), custom_call_target="tpu_custom_call" | custom-call | flops 968884224 | bytes 10485760 | tf_op jit(solution)/shard_map/adam_update/pallas_call | solution.py:187
  (2 shorter events, 0.1 us)
Async XLA Ops:
  7.2 111.4 %all-gather.3.cloned.1.call-start = ((), (), s32[]{:S(2)}) async-start(), calls=%async_computation.3 | async-start | bytes 4718592 | tf_op jit(solution)/shard_map/all_gather | solution.py:253
  8.2 2.7 %collective-permute-start = (bf16[512,256]{1,0:T(8,128)(2,1)S(1)}, bf16[512,256]{1,0:T(8,128)(2,1)S(1)}, u32[]{:S(2)}, u32[]{:S(2)}) collective-permute-start(bf16[512,256]{1,0:T(8,128)(2,1)S(1)} %dynamic-slice_bitcast_fusion), channel_id=1, source_target_pairs={{0,8},{8,0},{16,24},{24,16},{32,40},{40,32},{48,56},{56,48},{64,72... | collective-permute-start | bytes 786440 | tf_op jit(solution)/shard_map/ppermute | solution.py:213
  11.8 9.2 %collective-permute-start.3 = (bf16[512,256]{1,0:T(8,128)(2,1)S(1)}, bf16[512,256]{1,0:T(8,128)(2,1)S(1)}, u32[]{:S(2)}, u32[]{:S(2)}) collective-permute-start(bf16[512,256]{1,0:T(8,128)(2,1)S(1)} %bitcast_select_fusion), channel_id=1, source_target_pairs={{0,64},{8,72},{16,80},{24,88},{32,96},{40,104},{48,112},{56,120},{... | collective-permute-start | bytes 786440 | tf_op jit(solution)/shard_map/ppermute | solution.py:223
  14.9 7.5 %collective-permute-start.2 = (bf16[512,256]{1,0:T(8,128)(2,1)S(1)}, bf16[512,256]{1,0:T(8,128)(2,1)S(1)}, u32[]{:S(2)}, u32[]{:S(2)}) collective-permute-start(bf16[512,256]{1,0:T(8,128)(2,1)S(1)} %bitcast_select_fusion), channel_id=1, source_target_pairs={{0,48},{8,56},{16,0},{24,8},{32,16},{40,24},{48,32},{56,40},{64,11... | collective-permute-start | bytes 786440 | tf_op jit(solution)/shard_map/ppermute | solution.py:223
  17.4 8.1 %collective-permute-start.1 = (bf16[512,256]{1,0:T(8,128)(2,1)S(1)}, bf16[512,256]{1,0:T(8,128)(2,1)S(1)}, u32[]{:S(2)}, u32[]{:S(2)}) collective-permute-start(bf16[512,256]{1,0:T(8,128)(2,1)S(1)} %bitcast_select_fusion), channel_id=1, source_target_pairs={{0,16},{8,24},{16,32},{24,40},{32,48},{40,56},{48,0},{56,8},{64,80... | collective-permute-start | bytes 786440 | tf_op jit(solution)/shard_map/ppermute | solution.py:223
  25.5 7.5 %collective-permute-start.5 = (bf16[512,256]{1,0:T(8,128)(2,1)S(1)}, bf16[512,256]{1,0:T(8,128)(2,1)S(1)}, u32[]{:S(2)}, u32[]{:S(2)}) collective-permute-start(bf16[512,256]{1,0:T(8,128)(2,1)S(1)} %select_select_fusion.1), channel_id=1, source_target_pairs={{0,64},{8,72},{16,80},{24,88},{32,96},{40,104},{48,112},{56,120},{... | collective-permute-start | bytes 786440 | tf_op jit(solution)/shard_map/ppermute | solution.py:223
  25.7 7.3 %collective-permute-start.4 = (bf16[512,256]{1,0:T(8,128)(2,1)S(1)}, bf16[512,256]{1,0:T(8,128)(2,1)S(1)}, u32[]{:S(2)}, u32[]{:S(2)}) collective-permute-start(bf16[512,256]{1,0:T(8,128)(2,1)S(1)} %select_select_fusion.1), channel_id=1, source_target_pairs={{0,32},{8,40},{16,48},{24,56},{32,0},{40,8},{48,16},{56,24},{64,96... | collective-permute-start | bytes 786440 | tf_op jit(solution)/shard_map/ppermute | solution.py:223
  33.1 4.1 %collective-permute-start.6 = (bf16[512,256]{1,0:T(8,128)(2,1)S(1)}, bf16[512,256]{1,0:T(8,128)(2,1)S(1)}, u32[]{:S(2)}, u32[]{:S(2)}) collective-permute-start(bf16[512,256]{1,0:T(8,128)(2,1)S(1)} %select_select_fusion.mine), channel_id=1, source_target_pairs={{0,8},{8,0},{16,24},{24,16},{32,40},{40,32},{48,56},{56,48},{64,72... | collective-permute-start | bytes 786440 | tf_op jit(solution)/shard_map/ppermute | solution.py:213
  37.2 2.2 %copy-start = (bf16[2048,1024]{1,0:T(8,128)(2,1)S(1)}, bf16[2048,1024]{1,0:T(8,128)(2,1)}, u32[]{:S(2)}) copy-start(bf16[2048,1024]{1,0:T(8,128)(2,1)} %grad.1) | copy-start | bytes 12582916
  91.3 7.4 %collective-permute-start.7 = (bf16[8,232,256]{2,1,0:T(8,128)(2,1)S(1)}, bf16[8,232,256]{2,1,0:T(8,128)(2,1)S(1)}, u32[]{:S(2)}, u32[]{:S(2)}) collective-permute-start(bf16[8,232,256]{2,1,0:T(8,128)(2,1)S(1)} %grad_blocks.3), channel_id=1, source_target_pairs={{0,8},{8,0},{16,24},{24,16},{32,40},{40,32},{48,56},{56,48},{64,72... | collective-permute-start | bytes 2850824 | tf_op jit(solution)/shard_map/ppermute | solution.py:213
Sparse Core Ops, SparseCore 0:
  69.0 30.3 all-gather.2

commit v4 on v3

--- a/solution.py
+++ b/solution.py
@@ -124,21 +124,32 @@
     )(parity, hidden_t, coeffs)
 
 
-def final_kernel(
-    shares, first, second, projector, new_first, new_second, update,
-    parts, old, new, direction, rows, blocks, came, left,
-):
-    def load(i):
-        return pltpu.make_async_copy(projector.at[:, i], rows.at[i], came.at[i])
+def final_kernel(where, shares, first, second, *refs):
+    pieces, (new_first, new_second, update) = refs[:10], refs[10:13]
+    parts, old, new, direction, rows, blocks, came, left = refs[13:]
+    column, core = where[0], where[1]
+
+    def loads(half):
+        copies = []
+        for i in range(8):
+            away, side = (0, 3, 1, 2)[i // 2], i % 2
+            if away == 2:
+                source = pieces[6 + 2 * half + side]
+            else:
+                source = pieces[i].at[pl.ds(4 * half, 4)]
+            slot = 2 * ((column + away) % 4) + (core + side) % 2
+            to = rows.at[pl.ds(4 * half, 4), slot]
+            copies.append(pltpu.make_async_copy(source, to, came.at[8 * half + i]))
+        return copies
 
     def store(i):
         begin = pl.multiple_of(1024 * i, 1024)
         return pltpu.make_async_copy(blocks.at[i], update.at[:, pl.ds(begin, 1024)], left.at[i])
 
     early = [
-        pltpu.make_async_copy(shares, parts, came.at[8]),
-        pltpu.make_async_copy(first, old.at[0], came.at[9]),
-        pltpu.make_async_copy(second, old.at[1], came.at[10]),
+        pltpu.make_async_copy(shares, parts, came.at[16]),
+        pltpu.make_async_copy(first, old.at[0], came.at[17]),
+        pltpu.make_async_copy(second, old.at[1], came.at[18]),
     ]
     late = [
         pltpu.make_async_copy(new.at[0], new_first, left.at[8]),
@@ -146,8 +157,9 @@
     ]
     for copy in early:
         copy.start()
-    for i in range(8):
-        load(i).start()
+    for half in range(2):
+        for copy in loads(half):
+            copy.start()
     for copy in early:
         copy.wait()
     grad = parts[0].astype(f32)
@@ -161,18 +173,20 @@
     new[1] = scale.reshape(ROWS, 1, RANK)
     for copy in late:
         copy.start()
-
-    @pl.loop(0, 8)
-    def _(i):
-        load(i).wait()
-        product = lax.dot_general(
-            direction[...],
-            rows[i].reshape(1024, RANK),
-            (((1,), (1,)), ((), ())),
-            preferred_element_type=f32,
-        )
-        blocks[i] = (-4.0 * product).astype(bf16)
-        store(i).start()
+    for half in range(2):
+        for copy in loads(half):
+            copy.wait()
+
+        @pl.loop(4 * half, 4 * half + 4)
+        def _(i):
+            product = lax.dot_general(
+                direction[...],
+                rows[i].reshape(1024, RANK),
+                (((1,), (1,)), ((), ())),
+                preferred_element_type=f32,
+            )
+            blocks[i] = (-4.0 * product).astype(bf16)
+            store(i).start()
 
     @pl.loop(0, 8)
     def _(i):
@@ -182,11 +196,11 @@
         copy.wait()
 
 
-def finish(shares, first, second, projector):
+def finish(where, shares, first, second, pieces):
     any_space = pl.BlockSpec(memory_space=pl.ANY)
     return pl.pallas_call(
         final_kernel,
-        in_specs=[any_space] * 4,
+        in_specs=[pl.BlockSpec(memory_space=pltpu.SMEM)] + [any_space] * 13,
         out_specs=[any_space] * 3,
         out_shape=[
             jax.ShapeDtypeStruct((ROWS, 1, RANK), f32),
@@ -200,13 +214,13 @@
             pltpu.VMEM((ROWS, RANK), bf16),
             pltpu.VMEM((8, 8, 128, RANK), bf16),
             pltpu.VMEM((8, ROWS, 1024), bf16),
-            pltpu.SemaphoreType.DMA((11,)),
+            pltpu.SemaphoreType.DMA((19,)),
             pltpu.SemaphoreType.DMA((10,)),
         ],
         cost_estimate=cost(2 * 231 * 8192 * 256, 10 << 20),
         compiler_params=room(57),
         name="adam_update",
-    )(shares, first, second, projector)
+    )(where, shares, first, second, *pieces)
 
 
 def swap_cores(value):
@@ -250,17 +264,27 @@
     where = jnp.stack([core, column * 2 + core]).astype(jnp.int32)
     outgoing = partial_and_share(where, mine, other, out_grad)
     parts = lax.all_to_all(outgoing, TP, 0, 0)
-    projector = lax.all_gather(parts[:, BLOCK:], ("x", "core"))
+    share = parts[:, BLOCK:]
     coeffs = lax.all_to_all(sum_and_copies(parts), TP, 0, 0).reshape(2048, RANK)
+    coeffs, left, right = lax.optimization_barrier(
+        (coeffs, shift(share, 1, 0), shift(share, 3, 0))
+    )
+    ring = [share, left, right, shift(left[:4], 1, 0), shift(right[4:], 3, 0)]
 
     hidden_t = hidden.T
     give = grad_blocks((1 - core)[None], hidden_t, coeffs, bf16)
     got = swap_cores(give)
     keep = grad_blocks(core[None], hidden_t, coeffs, f32)
     pair = (keep + got.astype(f32)).astype(bf16)
+    pair, *ring = lax.optimization_barrier((pair, *ring))
     shares = lax.all_to_all(pair, CHIPS, 0, 0)
+    pieces = [side for piece in ring for side in (piece, swap_cores(piece))]
     new_first, new_second, update = finish(
-        shares, first_moment.transpose(1, 0, 2), second_moment.transpose(1, 0, 2), projector
+        jnp.stack([column, core]).astype(jnp.int32),
+        shares,
+        first_moment.transpose(1, 0, 2),
+        second_moment.transpose(1, 0, 2),
+        pieces,
     )
     return (new_first.transpose(1, 0, 2), new_second.transpose(1, 0, 2), update[None])
 

time: 131 us -> 126 us (0.962)
  blocking collectives: 62.9 us -> 26.2 us
  waiting for transfers between devices: 15.9 us -> 41.5 us
  between operations: 14.8 us -> 1.45 us
  starting transfers between devices: 13.8 us -> 27.1 us
  local copies, waits for them, and re-layouts: 3.99 us -> 7.47 us
  other arithmetic: 1.4 us -> 2.95 us
    all_to_all x2 -> x0, blocking collectives: 36.7 us -> none  [the longest x1 19.5 us: local(): shares = lax.all_to_all(pair, CHIPS, 0, 0)]
    ppermute x5 -> x9, waiting for transfers between devices: 14.3 us -> 27.2 us  [shift(): return lax.ppermute(value, FSDP, pairs)]
    all_to_all x0 -> x2, waiting for transfers between devices: none -> 10.5 us  [the longest x1 9.56 us: local(): shares = lax.all_to_all(pair, CHIPS, 0, 0)]
    all_to_all x0 -> x2, starting transfers between devices: none -> 7.75 us  [the longest x1 4.19 us: local(): shares = lax.all_to_all(pair, CHIPS, 0, 0)]
    unnamed x2 -> x24, local copies, waits for them, and re-layouts: 2.19 us -> 6.42 us
    ppermute x5 -> x9, starting transfers between devices: 6.85 us -> 9.92 us  [shift(): return lax.ppermute(value, FSDP, pairs)]
    ppermute x3 -> x8, starting transfers between devices: 6.93 us -> 9.48 us  [swap_cores(): return lax.ppermute(value, FSDP, [(i, i ^ 1) for i in range(16)])]
    ppermute x3 -> x8, waiting for transfers between devices: 1.58 us -> 3.83 us  [swap_cores(): return lax.ppermute(value, FSDP, [(i, i ^ 1) for i in range(16)])]
  transfers between devices with their start and end apart: 9 -> 19, of which waited for: 6 -> 13; matrix products, arithmetic and copies ran while one was open for 0% -> 2% of each run, Pallas kernels for 8% -> 4%
where the time goes in v4:
time: 126 us; the launch traced here: 125 us
  waiting for transfers between devices  41.5 us (33%)
  starting transfers between devices  27.1 us (22%)
  blocking collectives  26.2 us (21%)
  Pallas kernels  18.6 us (15%)
  local copies, waits for them, and re-layouts  7.47 us (6%)
  other arithmetic  2.95 us (2%)
  between operations  1.45 us (1%)
    ppermute x9, waiting for transfers between devices, shift(): return lax.ppermute(value, FSDP, pairs)  27.2 us
    all_to_all x1, blocking collectives, local(): parts = lax.all_to_all(outgoing, TP, 0, 0)  26.2 us
    ppermute x9, starting transfers between devices, shift(): return lax.ppermute(value, FSDP, pairs)  9.92 us
    pallas_call x2, Pallas kernels, grad_blocks(): pl.pallas_call(grad_kernel, in_specs=[pl.BlockSpec(memory_space=pltpu.SME...  9.83 us
    all_to_all x1, waiting for transfers between devices, local(): shares = lax.all_to_all(pair, CHIPS, 0, 0)  9.56 us
    ppermute x8, starting transfers between devices, swap_cores(): return lax.ppermute(value, FSDP, [(i, i ^ 1) for i in range(16)])  9.48 us
    unnamed x24, local copies, waits for them, and re-layouts  6.42 us
    pallas_call x1, Pallas kernels, finish(): pl.pallas_call(final_kernel, in_specs=[pl.BlockSpec(memory_space=pltpu.SM...  6.29 us
  transfers between devices with their start and end apart: 19, of which 13 were waited for; matrix products, arithmetic and copies ran while one was open for 2% of the time, Pallas kernels for 4%

profile of v4, /device:TPU:1, one launch (start us, length us, event | category | flops | bytes accessed | tf_op | source)
XLA Modules:
  0.0 125.4 jit_solution(9270506930359723690)
XLA Ops:
  0.6 1.0 dynamic-slice_bitcast_fusion
  1.6 1.5 %collective-permute-start = (bf16[512,256]{1,0:T(8,128)(2,1)S(1)}, bf16[512,256]{1,0:T(8,128)(2,1)S(1)}, u32[]{:S(2)}, u32[]{:S(2)}) collective-permute-start(bf16[512,256]{1,0:T(8,128)(2,1)S(1)} %dynamic-slice_bitcast_fusion), channel_id=1, source_target_pairs={{0,8},{8,0},{16,24},{24,16},{32,40},{40,32},{48,56},{56,48},{64,72... | collective-permute-start | bytes 786440 | tf_op jit(solution)/shard_map/ppermute | solution.py:227
  3.8 0.5 collective-permute-done
  4.3 1.0 bitcast_select_fusion
  5.3 3.1 %collective-permute-start.3 = (bf16[512,256]{1,0:T(8,128)(2,1)S(1)}, bf16[512,256]{1,0:T(8,128)(2,1)S(1)}, u32[]{:S(2)}, u32[]{:S(2)}) collective-permute-start(bf16[512,256]{1,0:T(8,128)(2,1)S(1)} %bitcast_select_fusion), channel_id=1, source_target_pairs={{0,64},{8,72},{16,80},{24,88},{32,96},{40,104},{48,112},{56,120},{... | collective-permute-start | bytes 786440 | tf_op jit(solution)/shard_map/ppermute | solution.py:237
  8.3 2.5 %collective-permute-start.2 = (bf16[512,256]{1,0:T(8,128)(2,1)S(1)}, bf16[512,256]{1,0:T(8,128)(2,1)S(1)}, u32[]{:S(2)}, u32[]{:S(2)}) collective-permute-start(bf16[512,256]{1,0:T(8,128)(2,1)S(1)} %bitcast_select_fusion), channel_id=1, source_target_pairs={{0,48},{8,56},{16,0},{24,8},{32,16},{40,24},{48,32},{56,40},{64,11... | collective-permute-start | bytes 786440 | tf_op jit(solution)/shard_map/ppermute | solution.py:237
  10.8 3.6 %collective-permute-done.3 = bf16[512,256]{1,0:T(8,128)(2,1)S(1)} collective-permute-done((bf16[512,256]{1,0:T(8,128)(2,1)S(1)}, bf16[512,256]{1,0:T(8,128)(2,1)S(1)}, u32[]{:S(2)}, u32[]{:S(2)}) %collective-permute-start.3) | collective-permute-done | bytes 262176 | tf_op jit(solution)/shard_map/ppermute | solution.py:237
  14.4 1.4 %collective-permute-done.2 = bf16[512,256]{1,0:T(8,128)(2,1)S(1)} collective-permute-done((bf16[512,256]{1,0:T(8,128)(2,1)S(1)}, bf16[512,256]{1,0:T(8,128)(2,1)S(1)}, u32[]{:S(2)}, u32[]{:S(2)}) %collective-permute-start.2) | collective-permute-done | bytes 262176 | tf_op jit(solution)/shard_map/ppermute | solution.py:237
  15.8 3.1 %collective-permute-done.1 = bf16[512,256]{1,0:T(8,128)(2,1)S(1)} collective-permute-done((bf16[512,256]{1,0:T(8,128)(2,1)S(1)}, bf16[512,256]{1,0:T(8,128)(2,1)S(1)}, u32[]{:S(2)}, u32[]{:S(2)}) %collective-permute-start.1) | collective-permute-done | bytes 262176 | tf_op jit(solution)/shard_map/ppermute | solution.py:237
  18.9 0.2 collective-permute-start.5
  19.1 1.1 collective-permute-start.4
  20.2 6.2 %collective-permute-done.5 = bf16[512,256]{1,0:T(8,128)(2,1)S(1)} collective-permute-done((bf16[512,256]{1,0:T(8,128)(2,1)S(1)}, bf16[512,256]{1,0:T(8,128)(2,1)S(1)}, u32[]{:S(2)}, u32[]{:S(2)}) %collective-permute-start.5) | collective-permute-done | bytes 262176 | tf_op jit(solution)/shard_map/ppermute | solution.py:237
  26.5 3.0 %collective-permute-start.6 = (bf16[512,256]{1,0:T(8,128)(2,1)S(1)}, bf16[512,256]{1,0:T(8,128)(2,1)S(1)}, u32[]{:S(2)}, u32[]{:S(2)}) collective-permute-start(bf16[512,256]{1,0:T(8,128)(2,1)S(1)} %select_select_fusion.mine), channel_id=1, source_target_pairs={{0,8},{8,0},{16,24},{24,16},{32,40},{40,32},{48,56},{56,48},{64,72... | collective-permute-start | bytes 786440 | tf_op jit(solution)/shard_map/ppermute | solution.py:227
  29.6 1.1 collective-permute-done.6.other
  30.7 2.2 %copy-done = bf16[2048,1024]{1,0:T(8,128)(2,1)S(1)} copy-done((bf16[2048,1024]{1,0:T(8,128)(2,1)S(1)}, bf16[2048,1024]{1,0:T(8,128)(2,1)}, u32[]{:S(2)}) %copy-start) | copy-done | bytes 4194328
  32.8 2.3 %partial_coeffs.1 = bf16[8,384,256]{2,1,0:T(8,128)(2,1)S(1)} custom-call(s32[2]{0:T(128)S(1)} %pad_add_fusion.1.where, bf16[512,256]{1,0:T(8,128)(2,1)S(1)} %select_select_fusion.mine, bf16[512,256]{1,0:T(8,128)(2,1)S(1)} %collective-permute-done.6.other, bf16[2048,1024]{1,0:T(8,128)(2,1)S(1)} %copy-done), custom_call_target="tpu_custom_call" | custom-call | flops 1073741824 | bytes 6291456 | tf_op jit(solution)/shard_map/partial_coeffs/pallas_call | solution.py:43
  35.2 26.2 %all_to_all.15.parts = bf16[8,384,256]{2,1,0:T(8,128)(2,1)S(1)} all-to-all(bf16[8,384,256]{2,1,0:T(8,128)(2,1)S(1)} %partial_coeffs.1), channel_id=1, replica_groups=mesh['yh'=2,'x'=4,'core'=2,'z'=4,'yl'=2] {'z','yl'}, dimensions={0} | all-to-all | bytes 3145728 | tf_op jit(solution)/shard_map/all_to_all | solution.py:266
  61.4 0.1 sum_coeffs.1
  61.6 1.0 copy-done.1
  62.5 3.6 %all-to-all-start.1 = ((bf16[8,256,256]{2,1,0:T(8,128)(2,1)}), bf16[8,256,256]{2,1,0:T(8,128)(2,1)S(1)}, u32[]{:S(2)}, u32[]{:S(2)}) async-start(bf16[8,256,256]{2,1,0:T(8,128)(2,1)} %copy-done.1), calls=%async_computation.1 | async-start | bytes 2097152 | tf_op jit(solution)/shard_map/all_to_all | solution.py:268
  66.2 0.4 collective-permute-start.8
  66.5 1.2 collective-permute-start.7
  67.7 10.1 %collective-permute-done.8.refs_4_ = bf16[8,128,256]{2,1,0:T(8,128)(2,1)S(1)} collective-permute-done((bf16[8,128,256]{2,1,0:T(8,128)(2,1)S(1)}, bf16[8,128,256]{2,1,0:T(8,128)(2,1)S(1)}, u32[]{:S(2)}, u32[]{:S(2)}) %collective-permute-start.8) | collective-permute-done | bytes 524320 | tf_op jit(solution)/shard_map/ppermute | solution.py:237
  77.8 1.2 collective-permute-done.7.refs_2_
  79.1 0.9 all-to-all-done.1
  80.0 4.9 %grad_blocks.3 = bf16[8,232,256]{2,1,0:T(8,128)(2,1)S(1)} custom-call(s32[1]{0:T(128)} %bitcast.9.parity, bf16[3696,2048]{1,0:T(8,128)(2,1)} %bitcast.23, bf16[2048,256]{1,0:T(8,128)(2,1)S(1)} %bitcast.21), custom_call_target="tpu_custom_call" | custom-call | flops 2147483648 | bytes 9437184 | tf_op jit(solution)/shard_map/grad_blocks/pallas_call | solution.py:108
  84.9 2.8 %collective-permute-start.9 = (bf16[8,232,256]{2,1,0:T(8,128)(2,1)S(1)}, bf16[8,232,256]{2,1,0:T(8,128)(2,1)S(1)}, u32[]{:S(2)}, u32[]{:S(2)}) collective-permute-start(bf16[8,232,256]{2,1,0:T(8,128)(2,1)S(1)} %grad_blocks.3), channel_id=1, source_target_pairs={{0,8},{8,0},{16,24},{24,16},{32,40},{40,32},{48,56},{56,48},{64,72... | collective-permute-start | bytes 2850824 | tf_op jit(solution)/shard_map/ppermute | solution.py:227
  87.8 0.4 collective-permute-start.11
  88.2 1.1 collective-permute-start.10
  89.3 4.9 %grad_blocks.2 = f32[8,232,256]{2,1,0:T(8,128)S(1)} custom-call(s32[1]{0:T(128)} %bitcast.1.parity, bf16[3696,2048]{1,0:T(8,128)(2,1)} %bitcast.24, bf16[2048,256]{1,0:T(8,128)(2,1)S(1)} %bitcast.22), custom_call_target="tpu_custom_call" | custom-call | flops 2147483648 | bytes 9437184 | tf_op jit(solution)/shard_map/grad_blocks/pallas_call | solution.py:108
  94.2 1.2 add_convert_fusion
  95.4 0.3 collective-permute-done.11.refs_8_
  95.8 1.2 collective-permute-done.10.refs_6_
  97.0 0.7 copy-done.9
  97.7 4.2 %all-to-all-start.2 = ((bf16[8,232,256]{2,1,0:T(8,128)(2,1)}), bf16[8,232,256]{2,1,0:T(8,128)(2,1)S(1)}, u32[]{:S(2)}, u32[]{:S(2)}) async-start(bf16[8,232,256]{2,1,0:T(8,128)(2,1)} %add_convert_fusion), calls=%async_computation.2 | async-start | bytes 1900544 | tf_op jit(solution)/shard_map/all_to_all | solution.py:280
  101.9 1.2 collective-permute-start.12
  103.1 0.1 collective-permute-start.13
  103.2 0.4 collective-permute-start.14
  103.6 0.1 collective-permute-start.15
  103.7 0.4 collective-permute-start.16
  104.1 0.6 pad_add_fusion.where
  104.7 2.2 %collective-permute-done.15.refs_7_ = bf16[4,128,256]{2,1,0:T(8,128)(2,1)S(1)} collective-permute-done((bf16[4,128,256]{2,1,0:T(8,128)(2,1)}, bf16[4,128,256]{2,1,0:T(8,128)(2,1)S(1)}, u32[]{:S(2)}, u32[]{:S(2)}) %collective-permute-start.15) | collective-permute-done | bytes 262176 | tf_op jit(solution)/shard_map/ppermute | solution.py:227
  107.0 0.7 copy-done.10
  107.6 0.1 copy-done.11
  107.8 0.8 copy-done.7
  108.6 9.6 %all-to-all-done.2.shares = bf16[8,232,256]{2,1,0:T(8,128)(2,1)S(1)} async-done(((bf16[8,232,256]{2,1,0:T(8,128)(2,1)}), bf16[8,232,256]{2,1,0:T(8,128)(2,1)S(1)}, u32[]{:S(2)}, u32[]{:S(2)}) %all-to-all-start.2) | async-done | bytes 950304 | tf_op jit(solution)/shard_map/all_to_all | solution.py:280
  118.1 0.9 copy-done.2
  119.1 6.3 %adam_update.1 = (f32[231,1,256]{2,1,0:T(1,128)}, f32[231,1,256]{2,1,0:T(1,128)}, bf16[231,8192]{1,0:T(8,128)(2,1)}) custom-call(s32[2]{0:T(128)} %pad_add_fusion.where, bf16[8,232,256]{2,1,0:T(8,128)(2,1)} %copy-done.2, f32[231,1,256]{2,1,0:T(1,128)} %bitcast.27, f32[231,1,256]{2,1,0:T(1,128)} %bitcast.28, bf16[8,128,256]{2,1,0:T(8,128)(2,1)} %copy-done.3, ...), custom_call_target="tpu_custom_call" | custom-call | flops 968884224 | bytes 10485760 | tf_op jit(solution)/shard_map/adam_update/pallas_call | solution.py:201
  (30 shorter events, 0.3 us)
Async XLA Ops:
  1.6 2.7 %collective-permute-start = (bf16[512,256]{1,0:T(8,128)(2,1)S(1)}, bf16[512,256]{1,0:T(8,128)(2,1)S(1)}, u32[]{:S(2)}, u32[]{:S(2)}) collective-permute-start(bf16[512,256]{1,0:T(8,128)(2,1)S(1)} %dynamic-slice_bitcast_fusion), channel_id=1, source_target_pairs={{0,8},{8,0},{16,24},{24,16},{32,40},{40,32},{48,56},{56,48},{64,72... | collective-permute-start | bytes 786440 | tf_op jit(solution)/shard_map/ppermute | solution.py:227
  5.3 9.2 %collective-permute-start.3 = (bf16[512,256]{1,0:T(8,128)(2,1)S(1)}, bf16[512,256]{1,0:T(8,128)(2,1)S(1)}, u32[]{:S(2)}, u32[]{:S(2)}) collective-permute-start(bf16[512,256]{1,0:T(8,128)(2,1)S(1)} %bitcast_select_fusion), channel_id=1, source_target_pairs={{0,64},{8,72},{16,80},{24,88},{32,96},{40,104},{48,112},{56,120},{... | collective-permute-start | bytes 786440 | tf_op jit(solution)/shard_map/ppermute | solution.py:237
  8.3 7.5 %collective-permute-start.2 = (bf16[512,256]{1,0:T(8,128)(2,1)S(1)}, bf16[512,256]{1,0:T(8,128)(2,1)S(1)}, u32[]{:S(2)}, u32[]{:S(2)}) collective-permute-start(bf16[512,256]{1,0:T(8,128)(2,1)S(1)} %bitcast_select_fusion), channel_id=1, source_target_pairs={{0,48},{8,56},{16,0},{24,8},{32,16},{40,24},{48,32},{56,40},{64,11... | collective-permute-start | bytes 786440 | tf_op jit(solution)/shard_map/ppermute | solution.py:237
  10.8 8.1 %collective-permute-start.1 = (bf16[512,256]{1,0:T(8,128)(2,1)S(1)}, bf16[512,256]{1,0:T(8,128)(2,1)S(1)}, u32[]{:S(2)}, u32[]{:S(2)}) collective-permute-start(bf16[512,256]{1,0:T(8,128)(2,1)S(1)} %bitcast_select_fusion), channel_id=1, source_target_pairs={{0,16},{8,24},{16,32},{24,40},{32,48},{40,56},{48,0},{56,8},{64,80... | collective-permute-start | bytes 786440 | tf_op jit(solution)/shard_map/ppermute | solution.py:237
  18.9 7.5 %collective-permute-start.5 = (bf16[512,256]{1,0:T(8,128)(2,1)S(1)}, bf16[512,256]{1,0:T(8,128)(2,1)S(1)}, u32[]{:S(2)}, u32[]{:S(2)}) collective-permute-start(bf16[512,256]{1,0:T(8,128)(2,1)S(1)} %select_select_fusion.1), channel_id=1, source_target_pairs={{0,64},{8,72},{16,80},{24,88},{32,96},{40,104},{48,112},{56,120},{... | collective-permute-start | bytes 786440 | tf_op jit(solution)/shard_map/ppermute | solution.py:237
  19.1 7.3 %collective-permute-start.4 = (bf16[512,256]{1,0:T(8,128)(2,1)S(1)}, bf16[512,256]{1,0:T(8,128)(2,1)S(1)}, u32[]{:S(2)}, u32[]{:S(2)}) collective-permute-start(bf16[512,256]{1,0:T(8,128)(2,1)S(1)} %select_select_fusion.1), channel_id=1, source_target_pairs={{0,32},{8,40},{16,48},{24,56},{32,0},{40,8},{48,16},{56,24},{64,96... | collective-permute-start | bytes 786440 | tf_op jit(solution)/shard_map/ppermute | solution.py:237
  26.5 4.1 %collective-permute-start.6 = (bf16[512,256]{1,0:T(8,128)(2,1)S(1)}, bf16[512,256]{1,0:T(8,128)(2,1)S(1)}, u32[]{:S(2)}, u32[]{:S(2)}) collective-permute-start(bf16[512,256]{1,0:T(8,128)(2,1)S(1)} %select_select_fusion.mine), channel_id=1, source_target_pairs={{0,8},{8,0},{16,24},{24,16},{32,40},{40,32},{48,56},{56,48},{64,72... | collective-permute-start | bytes 786440 | tf_op jit(solution)/shard_map/ppermute | solution.py:227
  30.7 2.2 %copy-start = (bf16[2048,1024]{1,0:T(8,128)(2,1)S(1)}, bf16[2048,1024]{1,0:T(8,128)(2,1)}, u32[]{:S(2)}) copy-start(bf16[2048,1024]{1,0:T(8,128)(2,1)} %grad.1) | copy-start | bytes 12582916
  61.6 1.0 copy-start.1
  62.5 17.4 %all-to-all-start.1 = ((bf16[8,256,256]{2,1,0:T(8,128)(2,1)}), bf16[8,256,256]{2,1,0:T(8,128)(2,1)S(1)}, u32[]{:S(2)}, u32[]{:S(2)}) async-start(bf16[8,256,256]{2,1,0:T(8,128)(2,1)} %copy-done.1), calls=%async_computation.1 | async-start | bytes 2097152 | tf_op jit(solution)/shard_map/all_to_all | solution.py:268
  66.1 35.7 %copy-start.3 = (bf16[8,128,256]{2,1,0:T(8,128)(2,1)}, bf16[8,128,256]{2,1,0:T(8,128)(2,1)S(1)}, u32[]{:S(2)}) copy-start(bf16[8,128,256]{2,1,0:T(8,128)(2,1)S(1)} %slice.12.refs_0_) | copy-start | bytes 1572868
  66.2 11.7 %collective-permute-start.8 = (bf16[8,128,256]{2,1,0:T(8,128)(2,1)S(1)}, bf16[8,128,256]{2,1,0:T(8,128)(2,1)S(1)}, u32[]{:S(2)}, u32[]{:S(2)}) collective-permute-start(bf16[8,128,256]{2,1,0:T(8,128)(2,1)S(1)} %slice.12.refs_0_), channel_id=1, source_target_pairs={{0,48},{8,56},{16,0},{24,8},{32,16},{40,24},{48,32},{56,40},{64,11... | collective-permute-start | bytes 1572872 | tf_op jit(solution)/shard_map/ppermute | solution.py:237
  66.5 12.5 %collective-permute-start.7 = (bf16[8,128,256]{2,1,0:T(8,128)(2,1)S(1)}, bf16[8,128,256]{2,1,0:T(8,128)(2,1)S(1)}, u32[]{:S(2)}, u32[]{:S(2)}) collective-permute-start(bf16[8,128,256]{2,1,0:T(8,128)(2,1)S(1)} %slice.12.refs_0_), channel_id=1, source_target_pairs={{0,16},{8,24},{16,32},{24,40},{32,48},{40,56},{48,0},{56,8},{64,80... | collective-permute-start | bytes 1572872 | tf_op jit(solution)/shard_map/ppermute | solution.py:237
  77.8 25.3 %copy-start.4 = (bf16[8,128,256]{2,1,0:T(8,128)(2,1)}, bf16[8,128,256]{2,1,0:T(8,128)(2,1)S(1)}, u32[]{:S(2)}) copy-start(bf16[8,128,256]{2,1,0:T(8,128)(2,1)S(1)} %collective-permute-done.8.refs_4_) | copy-start | bytes 1572868
  79.1 24.0 %copy-start.5 = (bf16[8,128,256]{2,1,0:T(8,128)(2,1)}, bf16[8,128,256]{2,1,0:T(8,128)(2,1)S(1)}, u32[]{:S(2)}) copy-start(bf16[8,128,256]{2,1,0:T(8,128)(2,1)S(1)} %collective-permute-done.7.refs_2_) | copy-start | bytes 1572868
  84.9 9.3 %collective-permute-start.9 = (bf16[8,232,256]{2,1,0:T(8,128)(2,1)S(1)}, bf16[8,232,256]{2,1,0:T(8,128)(2,1)S(1)}, u32[]{:S(2)}, u32[]{:S(2)}) collective-permute-start(bf16[8,232,256]{2,1,0:T(8,128)(2,1)S(1)} %grad_blocks.3), channel_id=1, source_target_pairs={{0,8},{8,0},{16,24},{24,16},{32,40},{40,32},{48,56},{56,48},{64,72... | collective-permute-start | bytes 2850824 | tf_op jit(solution)/shard_map/ppermute | solution.py:227
  87.8 8.0 %collective-permute-start.11 = (bf16[4,128,256]{2,1,0:T(8,128)(2,1)S(1)}, bf16[4,128,256]{2,1,0:T(8,128)(2,1)S(1)}, u32[]{:S(2)}, u32[]{:S(2)}) collective-permute-start(bf16[4,128,256]{2,1,0:T(8,128)(2,1)S(1)} %slice.11), channel_id=1, source_target_pairs={{0,48},{8,56},{16,0},{24,8},{32,16},{40,24},{48,32},{56,40},{64,11... | collective-permute-start | bytes 786440 | tf_op jit(solution)/shard_map/ppermute | solution.py:237
  88.2 8.8 %collective-permute-start.10 = (bf16[4,128,256]{2,1,0:T(8,128)(2,1)S(1)}, bf16[4,128,256]{2,1,0:T(8,128)(2,1)S(1)}, u32[]{:S(2)}, u32[]{:S(2)}) collective-permute-start(bf16[4,128,256]{2,1,0:T(8,128)(2,1)S(1)} %slice.10), channel_id=1, source_target_pairs={{0,16},{8,24},{16,32},{24,40},{32,48},{40,56},{48,0},{56,8},{64,80... | collective-permute-start | bytes 786440 | tf_op jit(solution)/shard_map/ppermute | solution.py:237
  95.8 22.4 %copy-start.8 = (bf16[4,128,256]{2,1,0:T(8,128)(2,1)}, bf16[4,128,256]{2,1,0:T(8,128)(2,1)S(1)}, u32[]{:S(2)}) copy-start(bf16[4,128,256]{2,1,0:T(8,128)(2,1)S(1)} %collective-permute-done.11.refs_8_) | copy-start | bytes 786436
  97.0 0.7 copy-start.9
  97.7 20.4 %all-to-all-start.2 = ((bf16[8,232,256]{2,1,0:T(8,128)(2,1)}), bf16[8,232,256]{2,1,0:T(8,128)(2,1)S(1)}, u32[]{:S(2)}, u32[]{:S(2)}) async-start(bf16[8,232,256]{2,1,0:T(8,128)(2,1)} %add_convert_fusion), calls=%async_computation.2 | async-start | bytes 1900544 | tf_op jit(solution)/shard_map/all_to_all | solution.py:280
  101.9 5.1 %collective-permute-start.12 = (bf16[8,128,256]{2,1,0:T(8,128)(2,1)S(1)}, bf16[8,128,256]{2,1,0:T(8,128)(2,1)S(1)}, u32[]{:S(2)}, u32[]{:S(2)}) collective-permute-start(bf16[8,128,256]{2,1,0:T(8,128)(2,1)S(1)} %slice.12.refs_0_), channel_id=1, source_target_pairs={{0,8},{8,0},{16,24},{24,16},{32,40},{40,32},{48,56},{56,48},{64,72... | collective-permute-start | bytes 1572872 | tf_op jit(solution)/shard_map/ppermute | solution.py:227
  103.1 3.9 %collective-permute-start.13 = (bf16[8,128,256]{2,1,0:T(8,128)(2,1)S(1)}, bf16[8,128,256]{2,1,0:T(8,128)(2,1)S(1)}, u32[]{:S(2)}, u32[]{:S(2)}) collective-permute-start(bf16[8,128,256]{2,1,0:T(8,128)(2,1)S(1)} %collective-permute-done.7.refs_2_), channel_id=1, source_target_pairs={{0,8},{8,0},{16,24},{24,16},{32,40},{40,32},{48,56},{56,48},{64,72... | collective-permute-start | bytes 1572872 | tf_op jit(solution)/shard_map/ppermute | solution.py:227
  103.2 5.4 %collective-permute-start.14 = (bf16[8,128,256]{2,1,0:T(8,128)(2,1)S(1)}, bf16[8,128,256]{2,1,0:T(8,128)(2,1)}, u32[]{:S(2)}, u32[]{:S(2)}) collective-permute-start(bf16[8,128,256]{2,1,0:T(8,128)(2,1)S(1)} %collective-permute-done.8.refs_4_), channel_id=1, source_target_pairs={{0,8},{8,0},{16,24},{24,16},{32,40},{40,32},{48,56},{56,48},{64,72... | collective-permute-start | bytes 1572872 | tf_op jit(solution)/shard_map/ppermute | solution.py:227
  103.6 3.3 %collective-permute-start.15 = (bf16[4,128,256]{2,1,0:T(8,128)(2,1)}, bf16[4,128,256]{2,1,0:T(8,128)(2,1)S(1)}, u32[]{:S(2)}, u32[]{:S(2)}) collective-permute-start(bf16[4,128,256]{2,1,0:T(8,128)(2,1)} %copy-done.9), channel_id=1, source_target_pairs={{0,8},{8,0},{16,24},{24,16},{32,40},{40,32},{48,56},{56,48},{64,72... | collective-permute-start | bytes 786440 | tf_op jit(solution)/shard_map/ppermute | solution.py:227
  103.7 3.3 %collective-permute-start.16 = (bf16[4,128,256]{2,1,0:T(8,128)(2,1)S(1)}, bf16[4,128,256]{2,1,0:T(8,128)(2,1)S(1)}, u32[]{:S(2)}, u32[]{:S(2)}) collective-permute-start(bf16[4,128,256]{2,1,0:T(8,128)(2,1)S(1)} %collective-permute-done.11.refs_8_), channel_id=1, source_target_pairs={{0,8},{8,0},{16,24},{24,16},{32,40},{40,32},{48,56},{56,48},{64,72... | collective-permute-start | bytes 786440 | tf_op jit(solution)/shard_map/ppermute | solution.py:227
  106.9 0.7 copy-start.10
  106.9 0.8 copy-start.11
  106.9 11.2 %copy-start.6 = (bf16[8,128,256]{2,1,0:T(8,128)(2,1)}, bf16[8,128,256]{2,1,0:T(8,128)(2,1)S(1)}, u32[]{:S(2)}) copy-start(bf16[8,128,256]{2,1,0:T(8,128)(2,1)S(1)} %collective-permute-done.12.refs_1_) | copy-start | bytes 1572868
  107.8 0.8 copy-start.7
  118.1 1.0 copy-start.2

commit v5 on v4

--- a/solution.py
+++ b/solution.py
@@ -1,3 +1,5 @@
+import functools
+
 import jax
 import jax.numpy as jnp
 from jax import lax
@@ -21,6 +23,33 @@
 
 def room(mebibytes):
     return pltpu.CompilerParams(vmem_limit_bytes=mebibytes << 20)
+
+
+def hold_kernel(count, source, out, done):
+    rows = source.shape[0] // count
+    copies = [
+        pltpu.make_async_copy(
+            source.at[pl.ds(rows * i, rows)], out.at[pl.ds(rows * i, rows)], done.at[i]
+        )
+        for i in range(count)
+    ]
+    for copy in copies:
+        copy.start()
+    for copy in copies:
+        copy.wait()
+
+
+def hold(source, count):
+    return pl.pallas_call(
+        functools.partial(hold_kernel, count),
+        in_specs=[pl.BlockSpec(memory_space=pl.ANY)],
+        out_specs=pl.BlockSpec(memory_space=pltpu.VMEM),
+        out_shape=jax.ShapeDtypeStruct(source.shape, source.dtype),
+        scratch_shapes=[pltpu.SemaphoreType.DMA((count,))],
+        cost_estimate=cost(0, 4 * source.size),
+        compiler_params=room(4),
+        name="hold",
+    )(source)
 
 
 def partial_kernel(where, mine, other, grad, out, piece):
@@ -218,7 +247,7 @@
             pltpu.SemaphoreType.DMA((10,)),
         ],
         cost_estimate=cost(2 * 231 * 8192 * 256, 10 << 20),
-        compiler_params=room(57),
+        compiler_params=room(50),
         name="adam_update",
     )(where, shares, first, second, *pieces)
 
@@ -237,7 +266,7 @@
     return lax.ppermute(value, FSDP, pairs)
 
 
-def owners_halves(candidate, root):
+def owners_halves(candidate, root, out_grad):
     yh, x, core = (lax.axis_index(a) for a in FSDP)
     halves = candidate.reshape(2, 512, RANK)
     kept = lax.dynamic_index_in_dim(halves, core, 0, keepdims=False)
@@ -245,34 +274,38 @@
     held = jnp.where(root % 2 == core, kept, swap_cores(given))
     dx = (x - root // 2 % 4) % 4
     dy = (yh - root // 8) % 2
+    takes = [
+        (dx == 1) & (dy == 0),
+        (dx == 3) & (dy == 0),
+        (dx == 0) & (dy == 1),
+        dx == 2,
+        (dx % 2 == 1) & (dy == 1),
+    ]
+    where = jnp.stack([core, x * 2 + core]).astype(jnp.int32)
     right, left, across = shift(held, 1, 0), shift(held, 3, 0), shift(held, 0, 1)
-    held = jnp.where(
-        (dx == 1) & (dy == 0),
-        right,
-        jnp.where((dx == 3) & (dy == 0), left, jnp.where((dx == 0) & (dy == 1), across, held)),
-    )
+    out_grad, takes, where = lax.optimization_barrier((out_grad, takes, where))
+    out_grad = hold(out_grad, 4)
+    held = jnp.where(takes[0], right, jnp.where(takes[1], left, jnp.where(takes[2], across, held)))
+    held, out_grad = lax.optimization_barrier((held, out_grad))
     far, across = shift(held, 2, 0), shift(held, 0, 1)
-    held = jnp.where(dx == 2, far, jnp.where((dx % 2 == 1) & (dy == 1), across, held))
-    return held, swap_cores(held)
+    held = jnp.where(takes[3], far, jnp.where(takes[4], across, held))
+    return held, swap_cores(held), out_grad, where
 
 
 def local(hidden, out_grad, projector_bank, owner, first_moment, second_moment):
     core = lax.axis_index("core")
     column = lax.axis_index("x")
 
-    mine, other = owners_halves(projector_bank[0], owner[0])
-    where = jnp.stack([core, column * 2 + core]).astype(jnp.int32)
-    outgoing = partial_and_share(where, mine, other, out_grad)
+    mine, other, held_grad, where = owners_halves(projector_bank[0], owner[0], out_grad)
+    outgoing = partial_and_share(where, mine, other, held_grad)
     parts = lax.all_to_all(outgoing, TP, 0, 0)
     share = parts[:, BLOCK:]
     coeffs = lax.all_to_all(sum_and_copies(parts), TP, 0, 0).reshape(2048, RANK)
-    coeffs, left, right = lax.optimization_barrier(
-        (coeffs, shift(share, 1, 0), shift(share, 3, 0))
-    )
-    ring = [share, left, right, shift(left[:4], 1, 0), shift(right[4:], 3, 0)]
 
     hidden_t = hidden.T
     give = grad_blocks((1 - core)[None], hidden_t, coeffs, bf16)
+    give, left, right = lax.optimization_barrier((give, shift(share, 1, 0), shift(share, 3, 0)))
+    ring = [share, left, right, shift(left[:4], 1, 0), shift(right[4:], 3, 0)]
     got = swap_cores(give)
     keep = grad_blocks(core[None], hidden_t, coeffs, f32)
     pair = (keep + got.astype(f32)).astype(bf16)

time: 126 us -> 123 us (0.976)
  local copies, waits for them, and re-layouts: 7.47 us -> 5.15 us
    ppermute x9, waiting for transfers between devices: 27.2 us -> 13.4 us  [shift(): return lax.ppermute(value, FSDP, pairs)]
    all_to_all x1, waiting for transfers between devices: 0.9 us -> 12.3 us  [local(): coeffs = lax.all_to_all(sum_and_copies(parts), TP, 0, 0).reshape(2048, RANK)]
    unnamed x24 -> x8, local copies, waits for them, and re-layouts: 6.42 us -> 3.16 us
    all_to_all x1, waiting for transfers between devices: 9.56 us -> 11.2 us  [local(): shares = lax.all_to_all(pair, CHIPS, 0, 0)]
  transfers between devices with their start and end apart: 19 -> 19, of which waited for: 13 -> 11; matrix products, arithmetic and copies ran while one was open for 2% -> 2% of each run, Pallas kernels for 4% -> 8%
where the time goes in v5:
time: 123 us
  waiting for transfers between devices  41.3 us (34%)
  starting transfers between devices  27.2 us (22%)
  blocking collectives  26.2 us (21%)
  Pallas kernels  18.7 us (15%)
  local copies, waits for them, and re-layouts  5.15 us (4%)
  other arithmetic  2.43 us (2%)
  between operations  1.45 us (1%)
    all_to_all x1, blocking collectives, local(): parts = lax.all_to_all(outgoing, TP, 0, 0)  26.2 us
    ppermute x9, waiting for transfers between devices, shift(): return lax.ppermute(value, FSDP, pairs)  13.4 us
    all_to_all x1, waiting for transfers between devices, local(): coeffs = lax.all_to_all(sum_and_copies(parts), TP, 0, 0).reshape(2048, RANK)  12.3 us
    all_to_all x1, waiting for transfers between devices, local(): shares = lax.all_to_all(pair, CHIPS, 0, 0)  11.2 us
    ppermute x9, starting transfers between devices, shift(): return lax.ppermute(value, FSDP, pairs)  9.92 us
    pallas_call x2, Pallas kernels, grad_blocks(): pl.pallas_call(grad_kernel, in_specs=[pl.BlockSpec(memory_space=pltpu.SME...  9.82 us
    ppermute x8, starting transfers between devices, swap_cores(): return lax.ppermute(value, FSDP, [(i, i ^ 1) for i in range(16)])  9.5 us
    pallas_call x1, Pallas kernels, finish(): pl.pallas_call(final_kernel, in_specs=[pl.BlockSpec(memory_space=pltpu.SM...  6.12 us
  transfers between devices with their start and end apart: 19, of which 11 were waited for; matrix products, arithmetic and copies ran while one was open for 2% of the time, Pallas kernels for 8%

profile of v5, /device:TPU:1, one launch (start us, length us, event | category | flops | bytes accessed | tf_op | source)
XLA Modules:
  0.0 122.5 jit_solution(16813838887989487767)
XLA Ops:
  0.6 1.0 dynamic-slice_bitcast_fusion
  1.6 1.5 %collective-permute-start = (bf16[512,256]{1,0:T(8,128)(2,1)S(1)}, bf16[512,256]{1,0:T(8,128)(2,1)S(1)}, u32[]{:S(2)}, u32[]{:S(2)}) collective-permute-start(bf16[512,256]{1,0:T(8,128)(2,1)S(1)} %dynamic-slice_bitcast_fusion), channel_id=1, source_target_pairs={{0,8},{8,0},{16,24},{24,16},{32,40},{40,32},{48,56},{56,48},{64,72... | collective-permute-start | bytes 786440 | tf_op jit(solution)/shard_map/ppermute | solution.py:256
  3.8 0.5 collective-permute-done
  4.3 1.0 bitcast_select_fusion
  5.3 3.1 %collective-permute-start.3 = (bf16[512,256]{1,0:T(8,128)(2,1)S(1)}, bf16[512,256]{1,0:T(8,128)(2,1)S(1)}, u32[]{:S(2)}, u32[]{:S(2)}) collective-permute-start(bf16[512,256]{1,0:T(8,128)(2,1)S(1)} %bitcast_select_fusion), channel_id=1, source_target_pairs={{0,64},{8,72},{16,80},{24,88},{32,96},{40,104},{48,112},{56,120},{... | collective-permute-start | bytes 786440 | tf_op jit(solution)/shard_map/ppermute | solution.py:266
  8.3 2.5 %collective-permute-start.2 = (bf16[512,256]{1,0:T(8,128)(2,1)S(1)}, bf16[512,256]{1,0:T(8,128)(2,1)S(1)}, u32[]{:S(2)}, u32[]{:S(2)}) collective-permute-start(bf16[512,256]{1,0:T(8,128)(2,1)S(1)} %bitcast_select_fusion), channel_id=1, source_target_pairs={{0,48},{8,56},{16,0},{24,8},{32,16},{40,24},{48,32},{56,40},{64,11... | collective-permute-start | bytes 786440 | tf_op jit(solution)/shard_map/ppermute | solution.py:266
  10.8 0.0 collective-permute-start.1
  10.8 0.1 pad_add_fusion.1.where
  10.9 2.2 %copy-done = bf16[2048,1024]{1,0:T(8,128)(2,1)S(1)} copy-done((bf16[2048,1024]{1,0:T(8,128)(2,1)S(1)}, bf16[2048,1024]{1,0:T(8,128)(2,1)}, u32[]{:S(2)}) %copy-start) | copy-done | bytes 4194328
  13.1 0.3 hold.1.grad
  13.4 1.0 collective-permute-done.3
  14.4 1.4 %collective-permute-done.2 = bf16[512,256]{1,0:T(8,128)(2,1)S(1)} collective-permute-done((bf16[512,256]{1,0:T(8,128)(2,1)S(1)}, bf16[512,256]{1,0:T(8,128)(2,1)S(1)}, u32[]{:S(2)}, u32[]{:S(2)}) %collective-permute-start.2) | collective-permute-done | bytes 262176 | tf_op jit(solution)/shard_map/ppermute | solution.py:266
  15.8 3.1 %collective-permute-done.1 = bf16[512,256]{1,0:T(8,128)(2,1)S(1)} collective-permute-done((bf16[512,256]{1,0:T(8,128)(2,1)S(1)}, bf16[512,256]{1,0:T(8,128)(2,1)S(1)}, u32[]{:S(2)}, u32[]{:S(2)}) %collective-permute-start.1) | collective-permute-done | bytes 262176 | tf_op jit(solution)/shard_map/ppermute | solution.py:266
  18.9 0.2 collective-permute-start.5
  19.1 1.1 collective-permute-start.4
  20.2 6.2 %collective-permute-done.5 = bf16[512,256]{1,0:T(8,128)(2,1)S(1)} collective-permute-done((bf16[512,256]{1,0:T(8,128)(2,1)S(1)}, bf16[512,256]{1,0:T(8,128)(2,1)S(1)}, u32[]{:S(2)}, u32[]{:S(2)}) %collective-permute-start.5) | collective-permute-done | bytes 262176 | tf_op jit(solution)/shard_map/ppermute | solution.py:266
  26.5 0.0 collective-permute-done.4
  26.5 3.0 %collective-permute-start.6 = (bf16[512,256]{1,0:T(8,128)(2,1)S(1)}, bf16[512,256]{1,0:T(8,128)(2,1)S(1)}, u32[]{:S(2)}, u32[]{:S(2)}) collective-permute-start(bf16[512,256]{1,0:T(8,128)(2,1)S(1)} %select_select_fusion.mine), channel_id=1, source_target_pairs={{0,8},{8,0},{16,24},{24,16},{32,40},{40,32},{48,56},{56,48},{64,72... | collective-permute-start | bytes 786440 | tf_op jit(solution)/shard_map/ppermute | solution.py:256
  29.5 1.2 collective-permute-done.6.other
  30.7 2.3 %partial_coeffs.1 = bf16[8,384,256]{2,1,0:T(8,128)(2,1)S(1)} custom-call(s32[2]{0:T(128)S(1)} %pad_add_fusion.1.where, bf16[512,256]{1,0:T(8,128)(2,1)S(1)} %select_select_fusion.mine, bf16[512,256]{1,0:T(8,128)(2,1)S(1)} %collective-permute-done.6.other, bf16[2048,1024]{1,0:T(8,128)(2,1)S(1)} %hold.1.grad), custom_call_target="tpu_custom_call" | custom-call | flops 1073741824 | bytes 6291456 | tf_op jit(solution)/shard_map/partial_coeffs/pallas_call | solution.py:72
  33.0 26.2 %all_to_all.15.parts = bf16[8,384,256]{2,1,0:T(8,128)(2,1)S(1)} all-to-all(bf16[8,384,256]{2,1,0:T(8,128)(2,1)S(1)} %partial_coeffs.1), channel_id=1, replica_groups=mesh['yh'=2,'x'=4,'core'=2,'z'=4,'yl'=2] {'z','yl'}, dimensions={0} | all-to-all | bytes 3145728 | tf_op jit(solution)/shard_map/all_to_all | solution.py:301
  59.2 0.1 sum_coeffs.1
  59.4 0.0 copy-start.1
  59.4 1.0 copy-done.1
  60.4 3.6 %all-to-all-start.1 = ((bf16[8,256,256]{2,1,0:T(8,128)(2,1)}), bf16[8,256,256]{2,1,0:T(8,128)(2,1)S(1)}, u32[]{:S(2)}, u32[]{:S(2)}) async-start(bf16[8,256,256]{2,1,0:T(8,128)(2,1)} %copy-done.1), calls=%async_computation.1 | async-start | bytes 2097152 | tf_op jit(solution)/shard_map/all_to_all | solution.py:303
  64.0 0.4 collective-permute-start.8
  64.3 1.2 collective-permute-start.7
  65.5 12.3 %all-to-all-done.1 = bf16[8,256,256]{2,1,0:T(8,128)(2,1)S(1)} async-done(((bf16[8,256,256]{2,1,0:T(8,128)(2,1)}), bf16[8,256,256]{2,1,0:T(8,128)(2,1)S(1)}, u32[]{:S(2)}, u32[]{:S(2)}) %all-to-all-start.1) | async-done | bytes 1048608 | tf_op jit(solution)/shard_map/all_to_all | solution.py:303
  77.8 4.9 %grad_blocks.3 = bf16[8,232,256]{2,1,0:T(8,128)(2,1)S(1)} custom-call(s32[1]{0:T(128)} %bitcast.9.parity, bf16[3696,2048]{1,0:T(8,128)(2,1)} %bitcast.25, bf16[2048,256]{1,0:T(8,128)(2,1)S(1)} %bitcast.21), custom_call_target="tpu_custom_call" | custom-call | flops 2147483648 | bytes 9437184 | tf_op jit(solution)/shard_map/grad_blocks/pallas_call | solution.py:137
  82.7 0.0 collective-permute-done.7.refs_2_
  82.7 2.8 %collective-permute-start.9 = (bf16[8,232,256]{2,1,0:T(8,128)(2,1)S(1)}, bf16[8,232,256]{2,1,0:T(8,128)(2,1)S(1)}, u32[]{:S(2)}, u32[]{:S(2)}) collective-permute-start(bf16[8,232,256]{2,1,0:T(8,128)(2,1)S(1)} %grad_blocks.3), channel_id=1, source_target_pairs={{0,8},{8,0},{16,24},{24,16},{32,40},{40,32},{48,56},{56,48},{64,72... | collective-permute-start | bytes 2850824 | tf_op jit(solution)/shard_map/ppermute | solution.py:256
  85.6 1.0 slice.11
  86.5 0.4 collective-permute-start.11
  86.9 1.1 collective-permute-start.10
  88.1 4.9 %grad_blocks.2 = f32[8,232,256]{2,1,0:T(8,128)S(1)} custom-call(s32[1]{0:T(128)} %bitcast.1.parity, bf16[3696,2048]{1,0:T(8,128)(2,1)} %bitcast.26, bf16[2048,256]{1,0:T(8,128)(2,1)S(1)} %bitcast.22), custom_call_target="tpu_custom_call" | custom-call | flops 2147483648 | bytes 9437184 | tf_op jit(solution)/shard_map/grad_blocks/pallas_call | solution.py:137
  93.0 1.2 add_convert_fusion
  94.2 0.4 collective-permute-done.11.refs_8_
  94.6 1.2 collective-permute-done.10.refs_6_
  95.9 4.2 %all-to-all-start.2 = ((bf16[8,232,256]{2,1,0:T(8,128)(2,1)}), bf16[8,232,256]{2,1,0:T(8,128)(2,1)}, u32[]{:S(2)}, u32[]{:S(2)}) async-start(bf16[8,232,256]{2,1,0:T(8,128)(2,1)} %add_convert_fusion), calls=%async_computation.2 | async-start | bytes 1900544 | tf_op jit(solution)/shard_map/all_to_all | solution.py:313
  100.1 1.2 collective-permute-start.12
  101.3 0.1 collective-permute-start.13
  101.4 0.4 collective-permute-start.14
  101.8 0.1 collective-permute-start.15
  101.9 0.4 collective-permute-start.16
  102.3 0.1 pad_add_fusion.where
  102.4 2.8 %collective-permute-done.15.refs_7_ = bf16[4,128,256]{2,1,0:T(8,128)(2,1)S(1)} collective-permute-done((bf16[4,128,256]{2,1,0:T(8,128)(2,1)}, bf16[4,128,256]{2,1,0:T(8,128)(2,1)S(1)}, u32[]{:S(2)}, u32[]{:S(2)}) %collective-permute-start.15) | collective-permute-done | bytes 262176 | tf_op jit(solution)/shard_map/ppermute | solution.py:256
  105.2 11.2 %all-to-all-done.2.shares = bf16[8,232,256]{2,1,0:T(8,128)(2,1)} async-done(((bf16[8,232,256]{2,1,0:T(8,128)(2,1)}), bf16[8,232,256]{2,1,0:T(8,128)(2,1)}, u32[]{:S(2)}, u32[]{:S(2)}) %all-to-all-start.2) | async-done | bytes 950304 | tf_op jit(solution)/shard_map/all_to_all | solution.py:313
  116.4 6.1 %adam_update.1 = (f32[231,1,256]{2,1,0:T(1,128)}, f32[231,1,256]{2,1,0:T(1,128)}, bf16[231,8192]{1,0:T(8,128)(2,1)}) custom-call(s32[2]{0:T(128)S(1)} %pad_add_fusion.where, bf16[8,232,256]{2,1,0:T(8,128)(2,1)} %all-to-all-done.2.shares, f32[231,1,256]{2,1,0:T(1,128)S(1)} %bitcast.23, f32[231,1,256]{2,1,0:T(1,128)S(1)} %bitcast.24, ...), custom_call_target="tpu_custom_call" | custom-call | flops 968884224 | bytes 10485760 | tf_op jit(solution)/shard_map/adam_update/pallas_call | solution.py:230
  (15 shorter events, 0.2 us)
Async XLA Ops:
  1.6 2.7 %collective-permute-start = (bf16[512,256]{1,0:T(8,128)(2,1)S(1)}, bf16[512,256]{1,0:T(8,128)(2,1)S(1)}, u32[]{:S(2)}, u32[]{:S(2)}) collective-permute-start(bf16[512,256]{1,0:T(8,128)(2,1)S(1)} %dynamic-slice_bitcast_fusion), channel_id=1, source_target_pairs={{0,8},{8,0},{16,24},{24,16},{32,40},{40,32},{48,56},{56,48},{64,72... | collective-permute-start | bytes 786440 | tf_op jit(solution)/shard_map/ppermute | solution.py:256
  5.3 9.2 %collective-permute-start.3 = (bf16[512,256]{1,0:T(8,128)(2,1)S(1)}, bf16[512,256]{1,0:T(8,128)(2,1)S(1)}, u32[]{:S(2)}, u32[]{:S(2)}) collective-permute-start(bf16[512,256]{1,0:T(8,128)(2,1)S(1)} %bitcast_select_fusion), channel_id=1, source_target_pairs={{0,64},{8,72},{16,80},{24,88},{32,96},{40,104},{48,112},{56,120},{... | collective-permute-start | bytes 786440 | tf_op jit(solution)/shard_map/ppermute | solution.py:266
  8.3 7.5 %collective-permute-start.2 = (bf16[512,256]{1,0:T(8,128)(2,1)S(1)}, bf16[512,256]{1,0:T(8,128)(2,1)S(1)}, u32[]{:S(2)}, u32[]{:S(2)}) collective-permute-start(bf16[512,256]{1,0:T(8,128)(2,1)S(1)} %bitcast_select_fusion), channel_id=1, source_target_pairs={{0,48},{8,56},{16,0},{24,8},{32,16},{40,24},{48,32},{56,40},{64,11... | collective-permute-start | bytes 786440 | tf_op jit(solution)/shard_map/ppermute | solution.py:266
  10.8 8.1 %collective-permute-start.1 = (bf16[512,256]{1,0:T(8,128)(2,1)S(1)}, bf16[512,256]{1,0:T(8,128)(2,1)S(1)}, u32[]{:S(2)}, u32[]{:S(2)}) collective-permute-start(bf16[512,256]{1,0:T(8,128)(2,1)S(1)} %bitcast_select_fusion), channel_id=1, source_target_pairs={{0,16},{8,24},{16,32},{24,40},{32,48},{40,56},{48,0},{56,8},{64,80... | collective-permute-start | bytes 786440 | tf_op jit(solution)/shard_map/ppermute | solution.py:266
  10.9 2.2 %copy-start = (bf16[2048,1024]{1,0:T(8,128)(2,1)S(1)}, bf16[2048,1024]{1,0:T(8,128)(2,1)}, u32[]{:S(2)}) copy-start(bf16[2048,1024]{1,0:T(8,128)(2,1)} %source) | copy-start | bytes 12582916
  18.9 7.5 %collective-permute-start.5 = (bf16[512,256]{1,0:T(8,128)(2,1)S(1)}, bf16[512,256]{1,0:T(8,128)(2,1)S(1)}, u32[]{:S(2)}, u32[]{:S(2)}) collective-permute-start(bf16[512,256]{1,0:T(8,128)(2,1)S(1)} %select_select_fusion.1), channel_id=1, source_target_pairs={{0,64},{8,72},{16,80},{24,88},{32,96},{40,104},{48,112},{56,120},{... | collective-permute-start | bytes 786440 | tf_op jit(solution)/shard_map/ppermute | solution.py:266
  19.1 7.3 %collective-permute-start.4 = (bf16[512,256]{1,0:T(8,128)(2,1)S(1)}, bf16[512,256]{1,0:T(8,128)(2,1)S(1)}, u32[]{:S(2)}, u32[]{:S(2)}) collective-permute-start(bf16[512,256]{1,0:T(8,128)(2,1)S(1)} %select_select_fusion.1), channel_id=1, source_target_pairs={{0,32},{8,40},{16,48},{24,56},{32,0},{40,8},{48,16},{56,24},{64,96... | collective-permute-start | bytes 786440 | tf_op jit(solution)/shard_map/ppermute | solution.py:266
  26.5 4.1 %collective-permute-start.6 = (bf16[512,256]{1,0:T(8,128)(2,1)S(1)}, bf16[512,256]{1,0:T(8,128)(2,1)S(1)}, u32[]{:S(2)}, u32[]{:S(2)}) collective-permute-start(bf16[512,256]{1,0:T(8,128)(2,1)S(1)} %select_select_fusion.mine), channel_id=1, source_target_pairs={{0,8},{8,0},{16,24},{24,16},{32,40},{40,32},{48,56},{56,48},{64,72... | collective-permute-start | bytes 786440 | tf_op jit(solution)/shard_map/ppermute | solution.py:256
  59.4 1.0 copy-start.1
  60.4 17.4 %all-to-all-start.1 = ((bf16[8,256,256]{2,1,0:T(8,128)(2,1)}), bf16[8,256,256]{2,1,0:T(8,128)(2,1)S(1)}, u32[]{:S(2)}, u32[]{:S(2)}) async-start(bf16[8,256,256]{2,1,0:T(8,128)(2,1)} %copy-done.1), calls=%async_computation.1 | async-start | bytes 2097152 | tf_op jit(solution)/shard_map/all_to_all | solution.py:303
  64.0 18.8 %collective-permute-start.8 = (bf16[8,128,256]{2,1,0:T(8,128)(2,1)S(1)}, bf16[8,128,256]{2,1,0:T(8,128)(2,1)}, u32[]{:S(2)}, u32[]{:S(2)}) collective-permute-start(bf16[8,128,256]{2,1,0:T(8,128)(2,1)S(1)} %slice.12.refs_0_), channel_id=1, source_target_pairs={{0,48},{8,56},{16,0},{24,8},{32,16},{40,24},{48,32},{56,40},{64,11... | collective-permute-start | bytes 1572872 | tf_op jit(solution)/shard_map/ppermute | solution.py:266
  64.3 18.4 %collective-permute-start.7 = (bf16[8,128,256]{2,1,0:T(8,128)(2,1)S(1)}, bf16[8,128,256]{2,1,0:T(8,128)(2,1)S(1)}, u32[]{:S(2)}, u32[]{:S(2)}) collective-permute-start(bf16[8,128,256]{2,1,0:T(8,128)(2,1)S(1)} %slice.12.refs_0_), channel_id=1, source_target_pairs={{0,16},{8,24},{16,32},{24,40},{32,48},{40,56},{48,0},{56,8},{64,80... | collective-permute-start | bytes 1572872 | tf_op jit(solution)/shard_map/ppermute | solution.py:266
  82.7 10.3 %collective-permute-start.9 = (bf16[8,232,256]{2,1,0:T(8,128)(2,1)S(1)}, bf16[8,232,256]{2,1,0:T(8,128)(2,1)S(1)}, u32[]{:S(2)}, u32[]{:S(2)}) collective-permute-start(bf16[8,232,256]{2,1,0:T(8,128)(2,1)S(1)} %grad_blocks.3), channel_id=1, source_target_pairs={{0,8},{8,0},{16,24},{24,16},{32,40},{40,32},{48,56},{56,48},{64,72... | collective-permute-start | bytes 2850824 | tf_op jit(solution)/shard_map/ppermute | solution.py:256
  86.5 8.1 %collective-permute-start.11 = (bf16[4,128,256]{2,1,0:T(8,128)(2,1)S(1)}, bf16[4,128,256]{2,1,0:T(8,128)(2,1)S(1)}, u32[]{:S(2)}, u32[]{:S(2)}) collective-permute-start(bf16[4,128,256]{2,1,0:T(8,128)(2,1)S(1)} %slice.11), channel_id=1, source_target_pairs={{0,48},{8,56},{16,0},{24,8},{32,16},{40,24},{48,32},{56,40},{64,11... | collective-permute-start | bytes 786440 | tf_op jit(solution)/shard_map/ppermute | solution.py:266
  86.9 8.9 %collective-permute-start.10 = (bf16[4,128,256]{2,1,0:T(8,128)(2,1)S(1)}, bf16[4,128,256]{2,1,0:T(8,128)(2,1)}, u32[]{:S(2)}, u32[]{:S(2)}) collective-permute-start(bf16[4,128,256]{2,1,0:T(8,128)(2,1)S(1)} %slice.10), channel_id=1, source_target_pairs={{0,16},{8,24},{16,32},{24,40},{32,48},{40,56},{48,0},{56,8},{64,80... | collective-permute-start | bytes 786440 | tf_op jit(solution)/shard_map/ppermute | solution.py:266
  94.2 22.2 %copy-start.2 = (f32[1,231,256]{2,0,1:T(1,128)S(1)}, f32[1,231,256]{2,0,1:T(1,128)}, u32[]{:S(2)}) copy-start(f32[1,231,256]{2,0,1:T(1,128)} %param.10) | copy-start | bytes 709636
  94.2 22.2 %copy-start.3 = (f32[1,231,256]{2,0,1:T(1,128)S(1)}, f32[1,231,256]{2,0,1:T(1,128)}, u32[]{:S(2)}) copy-start(f32[1,231,256]{2,0,1:T(1,128)} %param.11) | copy-start | bytes 709636
  95.9 20.5 %all-to-all-start.2 = ((bf16[8,232,256]{2,1,0:T(8,128)(2,1)}), bf16[8,232,256]{2,1,0:T(8,128)(2,1)}, u32[]{:S(2)}, u32[]{:S(2)}) async-start(bf16[8,232,256]{2,1,0:T(8,128)(2,1)} %add_convert_fusion), calls=%async_computation.2 | async-start | bytes 1900544 | tf_op jit(solution)/shard_map/all_to_all | solution.py:313
  100.1 5.1 %collective-permute-start.12 = (bf16[8,128,256]{2,1,0:T(8,128)(2,1)S(1)}, bf16[8,128,256]{2,1,0:T(8,128)(2,1)S(1)}, u32[]{:S(2)}, u32[]{:S(2)}) collective-permute-start(bf16[8,128,256]{2,1,0:T(8,128)(2,1)S(1)} %slice.12.refs_0_), channel_id=1, source_target_pairs={{0,8},{8,0},{16,24},{24,16},{32,40},{40,32},{48,56},{56,48},{64,72... | collective-permute-start | bytes 1572872 | tf_op jit(solution)/shard_map/ppermute | solution.py:256
  101.3 3.9 %collective-permute-start.13 = (bf16[8,128,256]{2,1,0:T(8,128)(2,1)S(1)}, bf16[8,128,256]{2,1,0:T(8,128)(2,1)S(1)}, u32[]{:S(2)}, u32[]{:S(2)}) collective-permute-start(bf16[8,128,256]{2,1,0:T(8,128)(2,1)S(1)} %collective-permute-done.7.refs_2_), channel_id=1, source_target_pairs={{0,8},{8,0},{16,24},{24,16},{32,40},{40,32},{48,56},{56,48},{64,72... | collective-permute-start | bytes 1572872 | tf_op jit(solution)/shard_map/ppermute | solution.py:256
  101.4 3.8 %collective-permute-start.14 = (bf16[8,128,256]{2,1,0:T(8,128)(2,1)}, bf16[8,128,256]{2,1,0:T(8,128)(2,1)}, u32[]{:S(2)}, u32[]{:S(2)}) collective-permute-start(bf16[8,128,256]{2,1,0:T(8,128)(2,1)} %collective-permute-done.8.refs_4_), channel_id=1, source_target_pairs={{0,8},{8,0},{16,24},{24,16},{32,40},{40,32},{48,56},{56,48},{64,72... | collective-permute-start | bytes 1572872 | tf_op jit(solution)/shard_map/ppermute | solution.py:256
  101.8 3.4 %collective-permute-start.15 = (bf16[4,128,256]{2,1,0:T(8,128)(2,1)}, bf16[4,128,256]{2,1,0:T(8,128)(2,1)S(1)}, u32[]{:S(2)}, u32[]{:S(2)}) collective-permute-start(bf16[4,128,256]{2,1,0:T(8,128)(2,1)} %collective-permute-done.10.refs_6_), channel_id=1, source_target_pairs={{0,8},{8,0},{16,24},{24,16},{32,40},{40,32},{48,56},{56,48},{64,72... | collective-permute-start | bytes 786440 | tf_op jit(solution)/shard_map/ppermute | solution.py:256
  101.9 3.3 %collective-permute-start.16 = (bf16[4,128,256]{2,1,0:T(8,128)(2,1)S(1)}, bf16[4,128,256]{2,1,0:T(8,128)(2,1)S(1)}, u32[]{:S(2)}, u32[]{:S(2)}) collective-permute-start(bf16[4,128,256]{2,1,0:T(8,128)(2,1)S(1)} %collective-permute-done.11.refs_8_), channel_id=1, source_target_pairs={{0,8},{8,0},{16,24},{24,16},{32,40},{40,32},{48,56},{56,48},{64,72... | collective-permute-start | bytes 786440 | tf_op jit(solution)/shard_map/ppermute | solution.py:256

commit v6 on v5

--- a/solution.py
+++ b/solution.py
@@ -112,7 +112,7 @@
         begin = pl.multiple_of(block_start(2 * i + parity[0]), 16)
         return pltpu.make_async_copy(hidden.at[pl.ds(begin, BLOCK)], rows.at[i], done.at[i])
 
-    for i in range(4):
+    for i in range(6):
         load(i).start()
 
     @pl.loop(0, 4)
@@ -120,10 +120,10 @@
         for j in range(2):
             load(2 * pair + j).wait()
 
-        @pl.when(pair < 2)
+        @pl.when(pair < 1)
         def _():
             for j in range(2):
-                load(2 * pair + 4 + j).start()
+                load(6 + j).start()
 
         for j in range(2):
             i = 2 * pair + j
@@ -206,16 +206,18 @@
         for copy in loads(half):
             copy.wait()
 
-        @pl.loop(4 * half, 4 * half + 4)
-        def _(i):
-            product = lax.dot_general(
-                direction[...],
-                rows[i].reshape(1024, RANK),
-                (((1,), (1,)), ((), ())),
-                preferred_element_type=f32,
-            )
-            blocks[i] = (-4.0 * product).astype(bf16)
-            store(i).start()
+        @pl.loop(2 * half, 2 * half + 2)
+        def _(pair):
+            for j in range(2):
+                product = lax.dot_general(
+                    direction[...],
+                    rows[2 * pair + j].reshape(1024, RANK),
+                    (((1,), (1,)), ((), ())),
+                    preferred_element_type=f32,
+                )
+                blocks[2 * pair + j] = (-4.0 * product).astype(bf16)
+            for j in range(2):
+                store(2 * pair + j).start()
 
     @pl.loop(0, 8)
     def _(i):

time: 123 us -> 122 us (level)
  no operation moved by 1% of the time
where the time goes in v6:
time: 122 us
  waiting for transfers between devices  41.4 us (34%)
  starting transfers between devices  27.2 us (22%)
  blocking collectives  26.2 us (21%)
  Pallas kernels  17.9 us (15%)
  local copies, waits for them, and re-layouts  5.15 us (4%)
  other arithmetic  2.43 us (2%)
  between operations  1.45 us (1%)
    all_to_all x1, blocking collectives, local(): parts = lax.all_to_all(outgoing, TP, 0, 0)  26.2 us
    ppermute x9, waiting for transfers between devices, shift(): return lax.ppermute(value, FSDP, pairs)  13.5 us
    all_to_all x1, waiting for transfers between devices, local(): coeffs = lax.all_to_all(sum_and_copies(parts), TP, 0, 0).reshape(2048, RANK)  12.3 us
    all_to_all x1, waiting for transfers between devices, local(): shares = lax.all_to_all(pair, CHIPS, 0, 0)  11.2 us
    ppermute x9, starting transfers between devices, shift(): return lax.ppermute(value, FSDP, pairs)  9.92 us
    pallas_call x2, Pallas kernels, grad_blocks(): pl.pallas_call(grad_kernel, in_specs=[pl.BlockSpec(memory_space=pltpu.SME...  9.6 us
    ppermute x8, starting transfers between devices, swap_cores(): return lax.ppermute(value, FSDP, [(i, i ^ 1) for i in range(16)])  9.5 us
    pallas_call x1, Pallas kernels, finish(): pl.pallas_call(final_kernel, in_specs=[pl.BlockSpec(memory_space=pltpu.SM...  5.5 us
  transfers between devices with their start and end apart: 19, of which 11 were waited for; matrix products, arithmetic and copies ran while one was open for 2% of the time, Pallas kernels for 8%

profile of v6, /device:TPU:1, one launch (start us, length us, event | category | flops | bytes accessed | tf_op | source)
XLA Modules:
  0.0 121.8 jit_solution(6372663782556336851)
XLA Ops:
  0.6 1.0 dynamic-slice_bitcast_fusion
  1.6 1.5 %collective-permute-start = (bf16[512,256]{1,0:T(8,128)(2,1)S(1)}, bf16[512,256]{1,0:T(8,128)(2,1)S(1)}, u32[]{:S(2)}, u32[]{:S(2)}) collective-permute-start(bf16[512,256]{1,0:T(8,128)(2,1)S(1)} %dynamic-slice_bitcast_fusion), channel_id=1, source_target_pairs={{0,8},{8,0},{16,24},{24,16},{32,40},{40,32},{48,56},{56,48},{64,72... | collective-permute-start | bytes 786440 | tf_op jit(solution)/shard_map/ppermute | solution.py:258
  3.8 0.5 collective-permute-done
  4.3 1.0 bitcast_select_fusion
  5.3 3.1 %collective-permute-start.3 = (bf16[512,256]{1,0:T(8,128)(2,1)S(1)}, bf16[512,256]{1,0:T(8,128)(2,1)S(1)}, u32[]{:S(2)}, u32[]{:S(2)}) collective-permute-start(bf16[512,256]{1,0:T(8,128)(2,1)S(1)} %bitcast_select_fusion), channel_id=1, source_target_pairs={{0,64},{8,72},{16,80},{24,88},{32,96},{40,104},{48,112},{56,120},{... | collective-permute-start | bytes 786440 | tf_op jit(solution)/shard_map/ppermute | solution.py:268
  8.3 2.5 %collective-permute-start.2 = (bf16[512,256]{1,0:T(8,128)(2,1)S(1)}, bf16[512,256]{1,0:T(8,128)(2,1)S(1)}, u32[]{:S(2)}, u32[]{:S(2)}) collective-permute-start(bf16[512,256]{1,0:T(8,128)(2,1)S(1)} %bitcast_select_fusion), channel_id=1, source_target_pairs={{0,48},{8,56},{16,0},{24,8},{32,16},{40,24},{48,32},{56,40},{64,11... | collective-permute-start | bytes 786440 | tf_op jit(solution)/shard_map/ppermute | solution.py:268
  10.8 0.0 collective-permute-start.1
  10.8 0.1 pad_add_fusion.1.where
  10.9 2.2 %copy-done = bf16[2048,1024]{1,0:T(8,128)(2,1)S(1)} copy-done((bf16[2048,1024]{1,0:T(8,128)(2,1)S(1)}, bf16[2048,1024]{1,0:T(8,128)(2,1)}, u32[]{:S(2)}) %copy-start) | copy-done | bytes 4194328
  13.1 0.3 hold.1.grad
  13.4 1.0 collective-permute-done.3
  14.4 1.4 %collective-permute-done.2 = bf16[512,256]{1,0:T(8,128)(2,1)S(1)} collective-permute-done((bf16[512,256]{1,0:T(8,128)(2,1)S(1)}, bf16[512,256]{1,0:T(8,128)(2,1)S(1)}, u32[]{:S(2)}, u32[]{:S(2)}) %collective-permute-start.2) | collective-permute-done | bytes 262176 | tf_op jit(solution)/shard_map/ppermute | solution.py:268
  15.8 3.1 %collective-permute-done.1 = bf16[512,256]{1,0:T(8,128)(2,1)S(1)} collective-permute-done((bf16[512,256]{1,0:T(8,128)(2,1)S(1)}, bf16[512,256]{1,0:T(8,128)(2,1)S(1)}, u32[]{:S(2)}, u32[]{:S(2)}) %collective-permute-start.1) | collective-permute-done | bytes 262176 | tf_op jit(solution)/shard_map/ppermute | solution.py:268
  18.9 0.2 collective-permute-start.5
  19.1 1.1 collective-permute-start.4
  20.2 6.2 %collective-permute-done.5 = bf16[512,256]{1,0:T(8,128)(2,1)S(1)} collective-permute-done((bf16[512,256]{1,0:T(8,128)(2,1)S(1)}, bf16[512,256]{1,0:T(8,128)(2,1)S(1)}, u32[]{:S(2)}, u32[]{:S(2)}) %collective-permute-start.5) | collective-permute-done | bytes 262176 | tf_op jit(solution)/shard_map/ppermute | solution.py:268
  26.5 0.0 collective-permute-done.4
  26.5 3.0 %collective-permute-start.6 = (bf16[512,256]{1,0:T(8,128)(2,1)S(1)}, bf16[512,256]{1,0:T(8,128)(2,1)S(1)}, u32[]{:S(2)}, u32[]{:S(2)}) collective-permute-start(bf16[512,256]{1,0:T(8,128)(2,1)S(1)} %select_select_fusion.mine), channel_id=1, source_target_pairs={{0,8},{8,0},{16,24},{24,16},{32,40},{40,32},{48,56},{56,48},{64,72... | collective-permute-start | bytes 786440 | tf_op jit(solution)/shard_map/ppermute | solution.py:258
  29.5 1.2 collective-permute-done.6.other
  30.7 2.3 %partial_coeffs.1 = bf16[8,384,256]{2,1,0:T(8,128)(2,1)S(1)} custom-call(s32[2]{0:T(128)S(1)} %pad_add_fusion.1.where, bf16[512,256]{1,0:T(8,128)(2,1)S(1)} %select_select_fusion.mine, bf16[512,256]{1,0:T(8,128)(2,1)S(1)} %collective-permute-done.6.other, bf16[2048,1024]{1,0:T(8,128)(2,1)S(1)} %hold.1.grad), custom_call_target="tpu_custom_call" | custom-call | flops 1073741824 | bytes 6291456 | tf_op jit(solution)/shard_map/partial_coeffs/pallas_call | solution.py:72
  33.0 26.2 %all_to_all.15.parts = bf16[8,384,256]{2,1,0:T(8,128)(2,1)S(1)} all-to-all(bf16[8,384,256]{2,1,0:T(8,128)(2,1)S(1)} %partial_coeffs.1), channel_id=1, replica_groups=mesh['yh'=2,'x'=4,'core'=2,'z'=4,'yl'=2] {'z','yl'}, dimensions={0} | all-to-all | bytes 3145728 | tf_op jit(solution)/shard_map/all_to_all | solution.py:303
  59.2 0.1 sum_coeffs.1
  59.4 0.0 copy-start.1
  59.4 1.0 copy-done.1
  60.4 3.6 %all-to-all-start.1 = ((bf16[8,256,256]{2,1,0:T(8,128)(2,1)}), bf16[8,256,256]{2,1,0:T(8,128)(2,1)S(1)}, u32[]{:S(2)}, u32[]{:S(2)}) async-start(bf16[8,256,256]{2,1,0:T(8,128)(2,1)} %copy-done.1), calls=%async_computation.1 | async-start | bytes 2097152 | tf_op jit(solution)/shard_map/all_to_all | solution.py:305
  64.0 0.4 collective-permute-start.8
  64.3 1.2 collective-permute-start.7
  65.5 12.3 %all-to-all-done.1 = bf16[8,256,256]{2,1,0:T(8,128)(2,1)S(1)} async-done(((bf16[8,256,256]{2,1,0:T(8,128)(2,1)}), bf16[8,256,256]{2,1,0:T(8,128)(2,1)S(1)}, u32[]{:S(2)}, u32[]{:S(2)}) %all-to-all-start.1) | async-done | bytes 1048608 | tf_op jit(solution)/shard_map/all_to_all | solution.py:305
  77.8 4.8 %grad_blocks.3 = bf16[8,232,256]{2,1,0:T(8,128)(2,1)S(1)} custom-call(s32[1]{0:T(128)} %bitcast.9.parity, bf16[3696,2048]{1,0:T(8,128)(2,1)} %bitcast.25, bf16[2048,256]{1,0:T(8,128)(2,1)S(1)} %bitcast.21), custom_call_target="tpu_custom_call" | custom-call | flops 2147483648 | bytes 9437184 | tf_op jit(solution)/shard_map/grad_blocks/pallas_call | solution.py:137
  82.6 0.0 collective-permute-done.7.refs_2_
  82.6 2.8 %collective-permute-start.9 = (bf16[8,232,256]{2,1,0:T(8,128)(2,1)S(1)}, bf16[8,232,256]{2,1,0:T(8,128)(2,1)S(1)}, u32[]{:S(2)}, u32[]{:S(2)}) collective-permute-start(bf16[8,232,256]{2,1,0:T(8,128)(2,1)S(1)} %grad_blocks.3), channel_id=1, source_target_pairs={{0,8},{8,0},{16,24},{24,16},{32,40},{40,32},{48,56},{56,48},{64,72... | collective-permute-start | bytes 2850824 | tf_op jit(solution)/shard_map/ppermute | solution.py:258
  85.5 1.0 slice.11
  86.4 0.4 collective-permute-start.11
  86.8 1.1 collective-permute-start.10
  88.0 4.8 %grad_blocks.2 = f32[8,232,256]{2,1,0:T(8,128)S(1)} custom-call(s32[1]{0:T(128)} %bitcast.1.parity, bf16[3696,2048]{1,0:T(8,128)(2,1)} %bitcast.26, bf16[2048,256]{1,0:T(8,128)(2,1)S(1)} %bitcast.22), custom_call_target="tpu_custom_call" | custom-call | flops 2147483648 | bytes 9437184 | tf_op jit(solution)/shard_map/grad_blocks/pallas_call | solution.py:137
  92.8 1.2 add_convert_fusion
  94.0 0.5 collective-permute-done.11.refs_8_
  94.5 1.2 %collective-permute-done.10.refs_6_ = bf16[4,128,256]{2,1,0:T(8,128)(2,1)} collective-permute-done((bf16[4,128,256]{2,1,0:T(8,128)(2,1)S(1)}, bf16[4,128,256]{2,1,0:T(8,128)(2,1)}, u32[]{:S(2)}, u32[]{:S(2)}) %collective-permute-start.10) | collective-permute-done | bytes 262176 | tf_op jit(solution)/shard_map/ppermute | solution.py:268
  95.8 4.2 %all-to-all-start.2 = ((bf16[8,232,256]{2,1,0:T(8,128)(2,1)}), bf16[8,232,256]{2,1,0:T(8,128)(2,1)}, u32[]{:S(2)}, u32[]{:S(2)}) async-start(bf16[8,232,256]{2,1,0:T(8,128)(2,1)} %add_convert_fusion), calls=%async_computation.2 | async-start | bytes 1900544 | tf_op jit(solution)/shard_map/all_to_all | solution.py:315
  100.0 1.2 collective-permute-start.12
  101.2 0.1 collective-permute-start.13
  101.3 0.4 collective-permute-start.14
  101.7 0.1 collective-permute-start.15
  101.8 0.4 collective-permute-start.16
  102.2 0.1 pad_add_fusion.where
  102.3 2.8 %collective-permute-done.15.refs_7_ = bf16[4,128,256]{2,1,0:T(8,128)(2,1)S(1)} collective-permute-done((bf16[4,128,256]{2,1,0:T(8,128)(2,1)}, bf16[4,128,256]{2,1,0:T(8,128)(2,1)S(1)}, u32[]{:S(2)}, u32[]{:S(2)}) %collective-permute-start.15) | collective-permute-done | bytes 262176 | tf_op jit(solution)/shard_map/ppermute | solution.py:258
  105.1 11.2 %all-to-all-done.2.shares = bf16[8,232,256]{2,1,0:T(8,128)(2,1)} async-done(((bf16[8,232,256]{2,1,0:T(8,128)(2,1)}), bf16[8,232,256]{2,1,0:T(8,128)(2,1)}, u32[]{:S(2)}, u32[]{:S(2)}) %all-to-all-start.2) | async-done | bytes 950304 | tf_op jit(solution)/shard_map/all_to_all | solution.py:315
  116.3 5.5 %adam_update.1 = (f32[231,1,256]{2,1,0:T(1,128)}, f32[231,1,256]{2,1,0:T(1,128)}, bf16[231,8192]{1,0:T(8,128)(2,1)}) custom-call(s32[2]{0:T(128)S(1)} %pad_add_fusion.where, bf16[8,232,256]{2,1,0:T(8,128)(2,1)} %all-to-all-done.2.shares, f32[231,1,256]{2,1,0:T(1,128)S(1)} %bitcast.23, f32[231,1,256]{2,1,0:T(1,128)S(1)} %bitcast.24, ...), custom_call_target="tpu_custom_call" | custom-call | flops 968884224 | bytes 10485760 | tf_op jit(solution)/shard_map/adam_update/pallas_call | solution.py:232
  (15 shorter events, 0.2 us)
Async XLA Ops:
  1.6 2.7 %collective-permute-start = (bf16[512,256]{1,0:T(8,128)(2,1)S(1)}, bf16[512,256]{1,0:T(8,128)(2,1)S(1)}, u32[]{:S(2)}, u32[]{:S(2)}) collective-permute-start(bf16[512,256]{1,0:T(8,128)(2,1)S(1)} %dynamic-slice_bitcast_fusion), channel_id=1, source_target_pairs={{0,8},{8,0},{16,24},{24,16},{32,40},{40,32},{48,56},{56,48},{64,72... | collective-permute-start | bytes 786440 | tf_op jit(solution)/shard_map/ppermute | solution.py:258
  5.3 9.2 %collective-permute-start.3 = (bf16[512,256]{1,0:T(8,128)(2,1)S(1)}, bf16[512,256]{1,0:T(8,128)(2,1)S(1)}, u32[]{:S(2)}, u32[]{:S(2)}) collective-permute-start(bf16[512,256]{1,0:T(8,128)(2,1)S(1)} %bitcast_select_fusion), channel_id=1, source_target_pairs={{0,64},{8,72},{16,80},{24,88},{32,96},{40,104},{48,112},{56,120},{... | collective-permute-start | bytes 786440 | tf_op jit(solution)/shard_map/ppermute | solution.py:268
  8.3 7.5 %collective-permute-start.2 = (bf16[512,256]{1,0:T(8,128)(2,1)S(1)}, bf16[512,256]{1,0:T(8,128)(2,1)S(1)}, u32[]{:S(2)}, u32[]{:S(2)}) collective-permute-start(bf16[512,256]{1,0:T(8,128)(2,1)S(1)} %bitcast_select_fusion), channel_id=1, source_target_pairs={{0,48},{8,56},{16,0},{24,8},{32,16},{40,24},{48,32},{56,40},{64,11... | collective-permute-start | bytes 786440 | tf_op jit(solution)/shard_map/ppermute | solution.py:268
  10.8 8.1 %collective-permute-start.1 = (bf16[512,256]{1,0:T(8,128)(2,1)S(1)}, bf16[512,256]{1,0:T(8,128)(2,1)S(1)}, u32[]{:S(2)}, u32[]{:S(2)}) collective-permute-start(bf16[512,256]{1,0:T(8,128)(2,1)S(1)} %bitcast_select_fusion), channel_id=1, source_target_pairs={{0,16},{8,24},{16,32},{24,40},{32,48},{40,56},{48,0},{56,8},{64,80... | collective-permute-start | bytes 786440 | tf_op jit(solution)/shard_map/ppermute | solution.py:268
  10.9 2.2 %copy-start = (bf16[2048,1024]{1,0:T(8,128)(2,1)S(1)}, bf16[2048,1024]{1,0:T(8,128)(2,1)}, u32[]{:S(2)}) copy-start(bf16[2048,1024]{1,0:T(8,128)(2,1)} %source) | copy-start | bytes 12582916
  18.9 7.5 %collective-permute-start.5 = (bf16[512,256]{1,0:T(8,128)(2,1)S(1)}, bf16[512,256]{1,0:T(8,128)(2,1)S(1)}, u32[]{:S(2)}, u32[]{:S(2)}) collective-permute-start(bf16[512,256]{1,0:T(8,128)(2,1)S(1)} %select_select_fusion.1), channel_id=1, source_target_pairs={{0,64},{8,72},{16,80},{24,88},{32,96},{40,104},{48,112},{56,120},{... | collective-permute-start | bytes 786440 | tf_op jit(solution)/shard_map/ppermute | solution.py:268
  19.1 7.3 %collective-permute-start.4 = (bf16[512,256]{1,0:T(8,128)(2,1)S(1)}, bf16[512,256]{1,0:T(8,128)(2,1)S(1)}, u32[]{:S(2)}, u32[]{:S(2)}) collective-permute-start(bf16[512,256]{1,0:T(8,128)(2,1)S(1)} %select_select_fusion.1), channel_id=1, source_target_pairs={{0,32},{8,40},{16,48},{24,56},{32,0},{40,8},{48,16},{56,24},{64,96... | collective-permute-start | bytes 786440 | tf_op jit(solution)/shard_map/ppermute | solution.py:268
  26.5 4.1 %collective-permute-start.6 = (bf16[512,256]{1,0:T(8,128)(2,1)S(1)}, bf16[512,256]{1,0:T(8,128)(2,1)S(1)}, u32[]{:S(2)}, u32[]{:S(2)}) collective-permute-start(bf16[512,256]{1,0:T(8,128)(2,1)S(1)} %select_select_fusion.mine), channel_id=1, source_target_pairs={{0,8},{8,0},{16,24},{24,16},{32,40},{40,32},{48,56},{56,48},{64,72... | collective-permute-start | bytes 786440 | tf_op jit(solution)/shard_map/ppermute | solution.py:258
  59.4 1.0 copy-start.1
  60.4 17.4 %all-to-all-start.1 = ((bf16[8,256,256]{2,1,0:T(8,128)(2,1)}), bf16[8,256,256]{2,1,0:T(8,128)(2,1)S(1)}, u32[]{:S(2)}, u32[]{:S(2)}) async-start(bf16[8,256,256]{2,1,0:T(8,128)(2,1)} %copy-done.1), calls=%async_computation.1 | async-start | bytes 2097152 | tf_op jit(solution)/shard_map/all_to_all | solution.py:305
  64.0 18.7 %collective-permute-start.8 = (bf16[8,128,256]{2,1,0:T(8,128)(2,1)S(1)}, bf16[8,128,256]{2,1,0:T(8,128)(2,1)}, u32[]{:S(2)}, u32[]{:S(2)}) collective-permute-start(bf16[8,128,256]{2,1,0:T(8,128)(2,1)S(1)} %slice.12.refs_0_), channel_id=1, source_target_pairs={{0,48},{8,56},{16,0},{24,8},{32,16},{40,24},{48,32},{56,40},{64,11... | collective-permute-start | bytes 1572872 | tf_op jit(solution)/shard_map/ppermute | solution.py:268
  64.3 18.3 %collective-permute-start.7 = (bf16[8,128,256]{2,1,0:T(8,128)(2,1)S(1)}, bf16[8,128,256]{2,1,0:T(8,128)(2,1)S(1)}, u32[]{:S(2)}, u32[]{:S(2)}) collective-permute-start(bf16[8,128,256]{2,1,0:T(8,128)(2,1)S(1)} %slice.12.refs_0_), channel_id=1, source_target_pairs={{0,16},{8,24},{16,32},{24,40},{32,48},{40,56},{48,0},{56,8},{64,80... | collective-permute-start | bytes 1572872 | tf_op jit(solution)/shard_map/ppermute | solution.py:268
  82.6 10.1 %collective-permute-start.9 = (bf16[8,232,256]{2,1,0:T(8,128)(2,1)S(1)}, bf16[8,232,256]{2,1,0:T(8,128)(2,1)S(1)}, u32[]{:S(2)}, u32[]{:S(2)}) collective-permute-start(bf16[8,232,256]{2,1,0:T(8,128)(2,1)S(1)} %grad_blocks.3), channel_id=1, source_target_pairs={{0,8},{8,0},{16,24},{24,16},{32,40},{40,32},{48,56},{56,48},{64,72... | collective-permute-start | bytes 2850824 | tf_op jit(solution)/shard_map/ppermute | solution.py:258
  86.4 8.1 %collective-permute-start.11 = (bf16[4,128,256]{2,1,0:T(8,128)(2,1)S(1)}, bf16[4,128,256]{2,1,0:T(8,128)(2,1)S(1)}, u32[]{:S(2)}, u32[]{:S(2)}) collective-permute-start(bf16[4,128,256]{2,1,0:T(8,128)(2,1)S(1)} %slice.11), channel_id=1, source_target_pairs={{0,48},{8,56},{16,0},{24,8},{32,16},{40,24},{48,32},{56,40},{64,11... | collective-permute-start | bytes 786440 | tf_op jit(solution)/shard_map/ppermute | solution.py:268
  86.8 8.9 %collective-permute-start.10 = (bf16[4,128,256]{2,1,0:T(8,128)(2,1)S(1)}, bf16[4,128,256]{2,1,0:T(8,128)(2,1)}, u32[]{:S(2)}, u32[]{:S(2)}) collective-permute-start(bf16[4,128,256]{2,1,0:T(8,128)(2,1)S(1)} %slice.10), channel_id=1, source_target_pairs={{0,16},{8,24},{16,32},{24,40},{32,48},{40,56},{48,0},{56,8},{64,80... | collective-permute-start | bytes 786440 | tf_op jit(solution)/shard_map/ppermute | solution.py:268
  94.0 22.3 %copy-start.2 = (f32[1,231,256]{2,0,1:T(1,128)S(1)}, f32[1,231,256]{2,0,1:T(1,128)}, u32[]{:S(2)}) copy-start(f32[1,231,256]{2,0,1:T(1,128)} %param.10) | copy-start | bytes 709636
  94.0 22.3 %copy-start.3 = (f32[1,231,256]{2,0,1:T(1,128)S(1)}, f32[1,231,256]{2,0,1:T(1,128)}, u32[]{:S(2)}) copy-start(f32[1,231,256]{2,0,1:T(1,128)} %param.11) | copy-start | bytes 709636
  95.8 20.5 %all-to-all-start.2 = ((bf16[8,232,256]{2,1,0:T(8,128)(2,1)}), bf16[8,232,256]{2,1,0:T(8,128)(2,1)}, u32[]{:S(2)}, u32[]{:S(2)}) async-start(bf16[8,232,256]{2,1,0:T(8,128)(2,1)} %add_convert_fusion), calls=%async_computation.2 | async-start | bytes 1900544 | tf_op jit(solution)/shard_map/all_to_all | solution.py:315
  100.0 5.1 %collective-permute-start.12 = (bf16[8,128,256]{2,1,0:T(8,128)(2,1)S(1)}, bf16[8,128,256]{2,1,0:T(8,128)(2,1)S(1)}, u32[]{:S(2)}, u32[]{:S(2)}) collective-permute-start(bf16[8,128,256]{2,1,0:T(8,128)(2,1)S(1)} %slice.12.refs_0_), channel_id=1, source_target_pairs={{0,8},{8,0},{16,24},{24,16},{32,40},{40,32},{48,56},{56,48},{64,72... | collective-permute-start | bytes 1572872 | tf_op jit(solution)/shard_map/ppermute | solution.py:258
  101.2 3.9 %collective-permute-start.13 = (bf16[8,128,256]{2,1,0:T(8,128)(2,1)S(1)}, bf16[8,128,256]{2,1,0:T(8,128)(2,1)S(1)}, u32[]{:S(2)}, u32[]{:S(2)}) collective-permute-start(bf16[8,128,256]{2,1,0:T(8,128)(2,1)S(1)} %collective-permute-done.7.refs_2_), channel_id=1, source_target_pairs={{0,8},{8,0},{16,24},{24,16},{32,40},{40,32},{48,56},{56,48},{64,72... | collective-permute-start | bytes 1572872 | tf_op jit(solution)/shard_map/ppermute | solution.py:258
  101.3 3.8 %collective-permute-start.14 = (bf16[8,128,256]{2,1,0:T(8,128)(2,1)}, bf16[8,128,256]{2,1,0:T(8,128)(2,1)}, u32[]{:S(2)}, u32[]{:S(2)}) collective-permute-start(bf16[8,128,256]{2,1,0:T(8,128)(2,1)} %collective-permute-done.8.refs_4_), channel_id=1, source_target_pairs={{0,8},{8,0},{16,24},{24,16},{32,40},{40,32},{48,56},{56,48},{64,72... | collective-permute-start | bytes 1572872 | tf_op jit(solution)/shard_map/ppermute | solution.py:258
  101.7 3.4 %collective-permute-start.15 = (bf16[4,128,256]{2,1,0:T(8,128)(2,1)}, bf16[4,128,256]{2,1,0:T(8,128)(2,1)S(1)}, u32[]{:S(2)}, u32[]{:S(2)}) collective-permute-start(bf16[4,128,256]{2,1,0:T(8,128)(2,1)} %collective-permute-done.10.refs_6_), channel_id=1, source_target_pairs={{0,8},{8,0},{16,24},{24,16},{32,40},{40,32},{48,56},{56,48},{64,72... | collective-permute-start | bytes 786440 | tf_op jit(solution)/shard_map/ppermute | solution.py:258
  101.8 3.3 %collective-permute-start.16 = (bf16[4,128,256]{2,1,0:T(8,128)(2,1)S(1)}, bf16[4,128,256]{2,1,0:T(8,128)(2,1)S(1)}, u32[]{:S(2)}, u32[]{:S(2)}) collective-permute-start(bf16[4,128,256]{2,1,0:T(8,128)(2,1)S(1)} %collective-permute-done.11.refs_8_), channel_id=1, source_target_pairs={{0,8},{8,0},{16,24},{24,16},{32,40},{40,32},{48,56},{56,48},{64,72... | collective-permute-start | bytes 786440 | tf_op jit(solution)/shard_map/ppermute | solution.py:258

commit v7 on v6

--- a/solution.py
+++ b/solution.py
@@ -57,14 +57,18 @@
     piece[pl.ds(pl.multiple_of(core * half, half), half), :] = mine[...]
     piece[pl.ds(pl.multiple_of((1 - core) * half, half), half), :] = other[...]
 
-    @pl.loop(0, 4)
-    def _(i):
-        rows = grad[pl.ds(pl.multiple_of(512 * i, 512), 512), :]
-        product = jnp.dot(rows, piece[...], preferred_element_type=f32).astype(bf16)
-        below = piece[pl.ds(pl.multiple_of(where[1] * 128, 128), 128), :]
+    below = piece[pl.ds(pl.multiple_of(where[1] * 128, 128), 128), :]
+    for i in range(8):
+        out[i, BLOCK:, :] = below
+
+    @pl.loop(0, 2)
+    def _(pair):
         for j in range(2):
-            out[2 * i + j, :BLOCK, :] = product[BLOCK * j : BLOCK * (j + 1)]
-            out[2 * i + j, BLOCK:, :] = below
+            i = 2 * pair + j
+            rows = grad[pl.ds(pl.multiple_of(512 * i, 512), 512), :]
+            product = jnp.dot(rows, piece[...], preferred_element_type=f32).astype(bf16)
+            out[2 * i, :BLOCK, :] = product[:BLOCK]
+            out[2 * i + 1, :BLOCK, :] = product[BLOCK:]
 
 
 def partial_and_share(where, mine, other, out_grad):

time: 122 us -> 122 us (level)
  no operation moved by 1% of the time
where the time goes in v7:
time: 122 us
  waiting for transfers between devices  41.4 us (34%)
  starting transfers between devices  27.2 us (22%)
  blocking collectives  26.2 us (21%)
  Pallas kernels  17.6 us (14%)
  local copies, waits for them, and re-layouts  5.15 us (4%)
  other arithmetic  2.43 us (2%)
  between operations  1.45 us (1%)
    all_to_all x1, blocking collectives, local(): parts = lax.all_to_all(outgoing, TP, 0, 0)  26.2 us
    ppermute x9, waiting for transfers between devices, shift(): return lax.ppermute(value, FSDP, pairs)  13.5 us
    all_to_all x1, waiting for transfers between devices, local(): coeffs = lax.all_to_all(sum_and_copies(parts), TP, 0, 0).reshape(2048, RANK)  12.3 us
    all_to_all x1, waiting for transfers between devices, local(): shares = lax.all_to_all(pair, CHIPS, 0, 0)  11.2 us
    ppermute x9, starting transfers between devices, shift(): return lax.ppermute(value, FSDP, pairs)  9.92 us
    pallas_call x2, Pallas kernels, grad_blocks(): pl.pallas_call(grad_kernel, in_specs=[pl.BlockSpec(memory_space=pltpu.SME...  9.59 us
    ppermute x8, starting transfers between devices, swap_cores(): return lax.ppermute(value, FSDP, [(i, i ^ 1) for i in range(16)])  9.5 us
    pallas_call x1, Pallas kernels, finish(): pl.pallas_call(final_kernel, in_specs=[pl.BlockSpec(memory_space=pltpu.SM...  5.5 us
  transfers between devices with their start and end apart: 19, of which 11 were waited for; matrix products, arithmetic and copies ran while one was open for 2% of the time, Pallas kernels for 8%

profile of v7, /device:TPU:1, one launch (start us, length us, event | category | flops | bytes accessed | tf_op | source)
XLA Modules:
  0.0 121.5 jit_solution(17702250566491443312)
XLA Ops:
  0.6 1.0 dynamic-slice_bitcast_fusion
  1.6 1.5 %collective-permute-start = (bf16[512,256]{1,0:T(8,128)(2,1)S(1)}, bf16[512,256]{1,0:T(8,128)(2,1)S(1)}, u32[]{:S(2)}, u32[]{:S(2)}) collective-permute-start(bf16[512,256]{1,0:T(8,128)(2,1)S(1)} %dynamic-slice_bitcast_fusion), channel_id=1, source_target_pairs={{0,8},{8,0},{16,24},{24,16},{32,40},{40,32},{48,56},{56,48},{64,72... | collective-permute-start | bytes 786440 | tf_op jit(solution)/shard_map/ppermute | solution.py:262
  3.8 0.5 collective-permute-done
  4.3 1.0 bitcast_select_fusion
  5.3 3.1 %collective-permute-start.3 = (bf16[512,256]{1,0:T(8,128)(2,1)S(1)}, bf16[512,256]{1,0:T(8,128)(2,1)S(1)}, u32[]{:S(2)}, u32[]{:S(2)}) collective-permute-start(bf16[512,256]{1,0:T(8,128)(2,1)S(1)} %bitcast_select_fusion), channel_id=1, source_target_pairs={{0,64},{8,72},{16,80},{24,88},{32,96},{40,104},{48,112},{56,120},{... | collective-permute-start | bytes 786440 | tf_op jit(solution)/shard_map/ppermute | solution.py:272
  8.3 2.5 %collective-permute-start.2 = (bf16[512,256]{1,0:T(8,128)(2,1)S(1)}, bf16[512,256]{1,0:T(8,128)(2,1)S(1)}, u32[]{:S(2)}, u32[]{:S(2)}) collective-permute-start(bf16[512,256]{1,0:T(8,128)(2,1)S(1)} %bitcast_select_fusion), channel_id=1, source_target_pairs={{0,48},{8,56},{16,0},{24,8},{32,16},{40,24},{48,32},{56,40},{64,11... | collective-permute-start | bytes 786440 | tf_op jit(solution)/shard_map/ppermute | solution.py:272
  10.8 0.0 collective-permute-start.1
  10.8 0.1 pad_add_fusion.1.where
  10.9 2.2 %copy-done = bf16[2048,1024]{1,0:T(8,128)(2,1)S(1)} copy-done((bf16[2048,1024]{1,0:T(8,128)(2,1)S(1)}, bf16[2048,1024]{1,0:T(8,128)(2,1)}, u32[]{:S(2)}) %copy-start) | copy-done | bytes 4194328
  13.1 0.3 hold.1.grad
  13.4 1.0 collective-permute-done.3
  14.4 1.4 %collective-permute-done.2 = bf16[512,256]{1,0:T(8,128)(2,1)S(1)} collective-permute-done((bf16[512,256]{1,0:T(8,128)(2,1)S(1)}, bf16[512,256]{1,0:T(8,128)(2,1)S(1)}, u32[]{:S(2)}, u32[]{:S(2)}) %collective-permute-start.2) | collective-permute-done | bytes 262176 | tf_op jit(solution)/shard_map/ppermute | solution.py:272
  15.8 3.1 %collective-permute-done.1 = bf16[512,256]{1,0:T(8,128)(2,1)S(1)} collective-permute-done((bf16[512,256]{1,0:T(8,128)(2,1)S(1)}, bf16[512,256]{1,0:T(8,128)(2,1)S(1)}, u32[]{:S(2)}, u32[]{:S(2)}) %collective-permute-start.1) | collective-permute-done | bytes 262176 | tf_op jit(solution)/shard_map/ppermute | solution.py:272
  18.9 0.2 collective-permute-start.5
  19.1 1.1 collective-permute-start.4
  20.2 6.2 %collective-permute-done.5 = bf16[512,256]{1,0:T(8,128)(2,1)S(1)} collective-permute-done((bf16[512,256]{1,0:T(8,128)(2,1)S(1)}, bf16[512,256]{1,0:T(8,128)(2,1)S(1)}, u32[]{:S(2)}, u32[]{:S(2)}) %collective-permute-start.5) | collective-permute-done | bytes 262176 | tf_op jit(solution)/shard_map/ppermute | solution.py:272
  26.5 0.0 collective-permute-done.4
  26.5 3.0 %collective-permute-start.6 = (bf16[512,256]{1,0:T(8,128)(2,1)S(1)}, bf16[512,256]{1,0:T(8,128)(2,1)S(1)}, u32[]{:S(2)}, u32[]{:S(2)}) collective-permute-start(bf16[512,256]{1,0:T(8,128)(2,1)S(1)} %select_select_fusion.mine), channel_id=1, source_target_pairs={{0,8},{8,0},{16,24},{24,16},{32,40},{40,32},{48,56},{56,48},{64,72... | collective-permute-start | bytes 786440 | tf_op jit(solution)/shard_map/ppermute | solution.py:262
  29.5 1.2 collective-permute-done.6.other
  30.7 2.0 %partial_coeffs.1 = bf16[8,384,256]{2,1,0:T(8,128)(2,1)S(1)} custom-call(s32[2]{0:T(128)S(1)} %pad_add_fusion.1.where, bf16[512,256]{1,0:T(8,128)(2,1)S(1)} %select_select_fusion.mine, bf16[512,256]{1,0:T(8,128)(2,1)S(1)} %collective-permute-done.6.other, bf16[2048,1024]{1,0:T(8,128)(2,1)S(1)} %hold.1.grad), custom_call_target="tpu_custom_call" | custom-call | flops 1073741824 | bytes 6291456 | tf_op jit(solution)/shard_map/partial_coeffs/pallas_call | solution.py:76
  32.7 26.2 %all_to_all.15.parts = bf16[8,384,256]{2,1,0:T(8,128)(2,1)S(1)} all-to-all(bf16[8,384,256]{2,1,0:T(8,128)(2,1)S(1)} %partial_coeffs.1), channel_id=1, replica_groups=mesh['yh'=2,'x'=4,'core'=2,'z'=4,'yl'=2] {'z','yl'}, dimensions={0} | all-to-all | bytes 3145728 | tf_op jit(solution)/shard_map/all_to_all | solution.py:307
  58.9 0.1 sum_coeffs.1
  59.1 0.0 copy-start.1
  59.1 1.0 copy-done.1
  60.0 3.6 %all-to-all-start.1 = ((bf16[8,256,256]{2,1,0:T(8,128)(2,1)}), bf16[8,256,256]{2,1,0:T(8,128)(2,1)S(1)}, u32[]{:S(2)}, u32[]{:S(2)}) async-start(bf16[8,256,256]{2,1,0:T(8,128)(2,1)} %copy-done.1), calls=%async_computation.1 | async-start | bytes 2097152 | tf_op jit(solution)/shard_map/all_to_all | solution.py:309
  63.6 0.4 collective-permute-start.8
  64.1 1.1 collective-permute-start.7
  65.2 12.3 %all-to-all-done.1 = bf16[8,256,256]{2,1,0:T(8,128)(2,1)S(1)} async-done(((bf16[8,256,256]{2,1,0:T(8,128)(2,1)}), bf16[8,256,256]{2,1,0:T(8,128)(2,1)S(1)}, u32[]{:S(2)}, u32[]{:S(2)}) %all-to-all-start.1) | async-done | bytes 1048608 | tf_op jit(solution)/shard_map/all_to_all | solution.py:309
  77.5 4.8 %grad_blocks.3 = bf16[8,232,256]{2,1,0:T(8,128)(2,1)S(1)} custom-call(s32[1]{0:T(128)} %bitcast.9.parity, bf16[3696,2048]{1,0:T(8,128)(2,1)} %bitcast.25, bf16[2048,256]{1,0:T(8,128)(2,1)S(1)} %bitcast.21), custom_call_target="tpu_custom_call" | custom-call | flops 2147483648 | bytes 9437184 | tf_op jit(solution)/shard_map/grad_blocks/pallas_call | solution.py:141
  82.3 0.0 collective-permute-done.7.refs_2_
  82.3 2.8 %collective-permute-start.9 = (bf16[8,232,256]{2,1,0:T(8,128)(2,1)S(1)}, bf16[8,232,256]{2,1,0:T(8,128)(2,1)S(1)}, u32[]{:S(2)}, u32[]{:S(2)}) collective-permute-start(bf16[8,232,256]{2,1,0:T(8,128)(2,1)S(1)} %grad_blocks.3), channel_id=1, source_target_pairs={{0,8},{8,0},{16,24},{24,16},{32,40},{40,32},{48,56},{56,48},{64,72... | collective-permute-start | bytes 2850824 | tf_op jit(solution)/shard_map/ppermute | solution.py:262
  85.2 1.0 slice.11
  86.1 0.4 collective-permute-start.11
  86.5 1.1 collective-permute-start.10
  87.7 4.8 %grad_blocks.2 = f32[8,232,256]{2,1,0:T(8,128)S(1)} custom-call(s32[1]{0:T(128)} %bitcast.1.parity, bf16[3696,2048]{1,0:T(8,128)(2,1)} %bitcast.26, bf16[2048,256]{1,0:T(8,128)(2,1)S(1)} %bitcast.22), custom_call_target="tpu_custom_call" | custom-call | flops 2147483648 | bytes 9437184 | tf_op jit(solution)/shard_map/grad_blocks/pallas_call | solution.py:141
  92.5 1.2 %add_convert_fusion = bf16[8,232,256]{2,1,0:T(8,128)(2,1)} fusion(f32[8,232,256]{2,1,0:T(8,128)S(1)} %grad_blocks.2, bf16[8,232,256]{2,1,0:T(8,128)(2,1)S(1)} %collective-permute-done.9), kind=kLoop, calls=%fused_computation | loop fusion | flops 1425408 | bytes 3801088 | tf_op jit(solution)/shard_map/convert_element_type | solution.py:317
  93.7 0.6 collective-permute-done.11.refs_8_
  94.2 1.2 %collective-permute-done.10.refs_6_ = bf16[4,128,256]{2,1,0:T(8,128)(2,1)} collective-permute-done((bf16[4,128,256]{2,1,0:T(8,128)(2,1)S(1)}, bf16[4,128,256]{2,1,0:T(8,128)(2,1)}, u32[]{:S(2)}, u32[]{:S(2)}) %collective-permute-start.10) | collective-permute-done | bytes 262176 | tf_op jit(solution)/shard_map/ppermute | solution.py:272
  95.5 4.2 %all-to-all-start.2 = ((bf16[8,232,256]{2,1,0:T(8,128)(2,1)}), bf16[8,232,256]{2,1,0:T(8,128)(2,1)}, u32[]{:S(2)}, u32[]{:S(2)}) async-start(bf16[8,232,256]{2,1,0:T(8,128)(2,1)} %add_convert_fusion), calls=%async_computation.2 | async-start | bytes 1900544 | tf_op jit(solution)/shard_map/all_to_all | solution.py:319
  99.7 1.2 collective-permute-start.12
  100.9 0.1 collective-permute-start.13
  101.0 0.4 collective-permute-start.14
  101.4 0.1 collective-permute-start.15
  101.5 0.4 collective-permute-start.16
  101.9 0.1 pad_add_fusion.where
  102.0 2.8 %collective-permute-done.15.refs_7_ = bf16[4,128,256]{2,1,0:T(8,128)(2,1)S(1)} collective-permute-done((bf16[4,128,256]{2,1,0:T(8,128)(2,1)}, bf16[4,128,256]{2,1,0:T(8,128)(2,1)S(1)}, u32[]{:S(2)}, u32[]{:S(2)}) %collective-permute-start.15) | collective-permute-done | bytes 262176 | tf_op jit(solution)/shard_map/ppermute | solution.py:262
  104.8 11.2 %all-to-all-done.2.shares = bf16[8,232,256]{2,1,0:T(8,128)(2,1)} async-done(((bf16[8,232,256]{2,1,0:T(8,128)(2,1)}), bf16[8,232,256]{2,1,0:T(8,128)(2,1)}, u32[]{:S(2)}, u32[]{:S(2)}) %all-to-all-start.2) | async-done | bytes 950304 | tf_op jit(solution)/shard_map/all_to_all | solution.py:319
  116.0 5.5 %adam_update.1 = (f32[231,1,256]{2,1,0:T(1,128)}, f32[231,1,256]{2,1,0:T(1,128)}, bf16[231,8192]{1,0:T(8,128)(2,1)}) custom-call(s32[2]{0:T(128)S(1)} %pad_add_fusion.where, bf16[8,232,256]{2,1,0:T(8,128)(2,1)} %all-to-all-done.2.shares, f32[231,1,256]{2,1,0:T(1,128)S(1)} %bitcast.23, f32[231,1,256]{2,1,0:T(1,128)S(1)} %bitcast.24, ...), custom_call_target="tpu_custom_call" | custom-call | flops 968884224 | bytes 10485760 | tf_op jit(solution)/shard_map/adam_update/pallas_call | solution.py:236
  (15 shorter events, 0.2 us)
Async XLA Ops:
  1.6 2.7 %collective-permute-start = (bf16[512,256]{1,0:T(8,128)(2,1)S(1)}, bf16[512,256]{1,0:T(8,128)(2,1)S(1)}, u32[]{:S(2)}, u32[]{:S(2)}) collective-permute-start(bf16[512,256]{1,0:T(8,128)(2,1)S(1)} %dynamic-slice_bitcast_fusion), channel_id=1, source_target_pairs={{0,8},{8,0},{16,24},{24,16},{32,40},{40,32},{48,56},{56,48},{64,72... | collective-permute-start | bytes 786440 | tf_op jit(solution)/shard_map/ppermute | solution.py:262
  5.3 9.2 %collective-permute-start.3 = (bf16[512,256]{1,0:T(8,128)(2,1)S(1)}, bf16[512,256]{1,0:T(8,128)(2,1)S(1)}, u32[]{:S(2)}, u32[]{:S(2)}) collective-permute-start(bf16[512,256]{1,0:T(8,128)(2,1)S(1)} %bitcast_select_fusion), channel_id=1, source_target_pairs={{0,64},{8,72},{16,80},{24,88},{32,96},{40,104},{48,112},{56,120},{... | collective-permute-start | bytes 786440 | tf_op jit(solution)/shard_map/ppermute | solution.py:272
  8.3 7.5 %collective-permute-start.2 = (bf16[512,256]{1,0:T(8,128)(2,1)S(1)}, bf16[512,256]{1,0:T(8,128)(2,1)S(1)}, u32[]{:S(2)}, u32[]{:S(2)}) collective-permute-start(bf16[512,256]{1,0:T(8,128)(2,1)S(1)} %bitcast_select_fusion), channel_id=1, source_target_pairs={{0,48},{8,56},{16,0},{24,8},{32,16},{40,24},{48,32},{56,40},{64,11... | collective-permute-start | bytes 786440 | tf_op jit(solution)/shard_map/ppermute | solution.py:272
  10.8 8.1 %collective-permute-start.1 = (bf16[512,256]{1,0:T(8,128)(2,1)S(1)}, bf16[512,256]{1,0:T(8,128)(2,1)S(1)}, u32[]{:S(2)}, u32[]{:S(2)}) collective-permute-start(bf16[512,256]{1,0:T(8,128)(2,1)S(1)} %bitcast_select_fusion), channel_id=1, source_target_pairs={{0,16},{8,24},{16,32},{24,40},{32,48},{40,56},{48,0},{56,8},{64,80... | collective-permute-start | bytes 786440 | tf_op jit(solution)/shard_map/ppermute | solution.py:272
  10.9 2.2 %copy-start = (bf16[2048,1024]{1,0:T(8,128)(2,1)S(1)}, bf16[2048,1024]{1,0:T(8,128)(2,1)}, u32[]{:S(2)}) copy-start(bf16[2048,1024]{1,0:T(8,128)(2,1)} %source) | copy-start | bytes 12582916
  18.9 7.5 %collective-permute-start.5 = (bf16[512,256]{1,0:T(8,128)(2,1)S(1)}, bf16[512,256]{1,0:T(8,128)(2,1)S(1)}, u32[]{:S(2)}, u32[]{:S(2)}) collective-permute-start(bf16[512,256]{1,0:T(8,128)(2,1)S(1)} %select_select_fusion.1), channel_id=1, source_target_pairs={{0,64},{8,72},{16,80},{24,88},{32,96},{40,104},{48,112},{56,120},{... | collective-permute-start | bytes 786440 | tf_op jit(solution)/shard_map/ppermute | solution.py:272
  19.1 7.3 %collective-permute-start.4 = (bf16[512,256]{1,0:T(8,128)(2,1)S(1)}, bf16[512,256]{1,0:T(8,128)(2,1)S(1)}, u32[]{:S(2)}, u32[]{:S(2)}) collective-permute-start(bf16[512,256]{1,0:T(8,128)(2,1)S(1)} %select_select_fusion.1), channel_id=1, source_target_pairs={{0,32},{8,40},{16,48},{24,56},{32,0},{40,8},{48,16},{56,24},{64,96... | collective-permute-start | bytes 786440 | tf_op jit(solution)/shard_map/ppermute | solution.py:272
  26.5 4.1 %collective-permute-start.6 = (bf16[512,256]{1,0:T(8,128)(2,1)S(1)}, bf16[512,256]{1,0:T(8,128)(2,1)S(1)}, u32[]{:S(2)}, u32[]{:S(2)}) collective-permute-start(bf16[512,256]{1,0:T(8,128)(2,1)S(1)} %select_select_fusion.mine), channel_id=1, source_target_pairs={{0,8},{8,0},{16,24},{24,16},{32,40},{40,32},{48,56},{56,48},{64,72... | collective-permute-start | bytes 786440 | tf_op jit(solution)/shard_map/ppermute | solution.py:262
  59.1 1.0 copy-start.1
  60.0 17.4 %all-to-all-start.1 = ((bf16[8,256,256]{2,1,0:T(8,128)(2,1)}), bf16[8,256,256]{2,1,0:T(8,128)(2,1)S(1)}, u32[]{:S(2)}, u32[]{:S(2)}) async-start(bf16[8,256,256]{2,1,0:T(8,128)(2,1)} %copy-done.1), calls=%async_computation.1 | async-start | bytes 2097152 | tf_op jit(solution)/shard_map/all_to_all | solution.py:309
  63.6 18.7 %collective-permute-start.8 = (bf16[8,128,256]{2,1,0:T(8,128)(2,1)S(1)}, bf16[8,128,256]{2,1,0:T(8,128)(2,1)}, u32[]{:S(2)}, u32[]{:S(2)}) collective-permute-start(bf16[8,128,256]{2,1,0:T(8,128)(2,1)S(1)} %slice.12.refs_0_), channel_id=1, source_target_pairs={{0,48},{8,56},{16,0},{24,8},{32,16},{40,24},{48,32},{56,40},{64,11... | collective-permute-start | bytes 1572872 | tf_op jit(solution)/shard_map/ppermute | solution.py:272
  64.1 18.3 %collective-permute-start.7 = (bf16[8,128,256]{2,1,0:T(8,128)(2,1)S(1)}, bf16[8,128,256]{2,1,0:T(8,128)(2,1)S(1)}, u32[]{:S(2)}, u32[]{:S(2)}) collective-permute-start(bf16[8,128,256]{2,1,0:T(8,128)(2,1)S(1)} %slice.12.refs_0_), channel_id=1, source_target_pairs={{0,16},{8,24},{16,32},{24,40},{32,48},{40,56},{48,0},{56,8},{64,80... | collective-permute-start | bytes 1572872 | tf_op jit(solution)/shard_map/ppermute | solution.py:272
  82.3 10.1 %collective-permute-start.9 = (bf16[8,232,256]{2,1,0:T(8,128)(2,1)S(1)}, bf16[8,232,256]{2,1,0:T(8,128)(2,1)S(1)}, u32[]{:S(2)}, u32[]{:S(2)}) collective-permute-start(bf16[8,232,256]{2,1,0:T(8,128)(2,1)S(1)} %grad_blocks.3), channel_id=1, source_target_pairs={{0,8},{8,0},{16,24},{24,16},{32,40},{40,32},{48,56},{56,48},{64,72... | collective-permute-start | bytes 2850824 | tf_op jit(solution)/shard_map/ppermute | solution.py:262
  86.1 8.1 %collective-permute-start.11 = (bf16[4,128,256]{2,1,0:T(8,128)(2,1)S(1)}, bf16[4,128,256]{2,1,0:T(8,128)(2,1)S(1)}, u32[]{:S(2)}, u32[]{:S(2)}) collective-permute-start(bf16[4,128,256]{2,1,0:T(8,128)(2,1)S(1)} %slice.11), channel_id=1, source_target_pairs={{0,48},{8,56},{16,0},{24,8},{32,16},{40,24},{48,32},{56,40},{64,11... | collective-permute-start | bytes 786440 | tf_op jit(solution)/shard_map/ppermute | solution.py:272
  86.5 8.9 %collective-permute-start.10 = (bf16[4,128,256]{2,1,0:T(8,128)(2,1)S(1)}, bf16[4,128,256]{2,1,0:T(8,128)(2,1)}, u32[]{:S(2)}, u32[]{:S(2)}) collective-permute-start(bf16[4,128,256]{2,1,0:T(8,128)(2,1)S(1)} %slice.10), channel_id=1, source_target_pairs={{0,16},{8,24},{16,32},{24,40},{32,48},{40,56},{48,0},{56,8},{64,80... | collective-permute-start | bytes 786440 | tf_op jit(solution)/shard_map/ppermute | solution.py:272
  93.7 22.3 %copy-start.2 = (f32[1,231,256]{2,0,1:T(1,128)S(1)}, f32[1,231,256]{2,0,1:T(1,128)}, u32[]{:S(2)}) copy-start(f32[1,231,256]{2,0,1:T(1,128)} %param.10) | copy-start | bytes 709636
  93.7 22.3 %copy-start.3 = (f32[1,231,256]{2,0,1:T(1,128)S(1)}, f32[1,231,256]{2,0,1:T(1,128)}, u32[]{:S(2)}) copy-start(f32[1,231,256]{2,0,1:T(1,128)} %param.11) | copy-start | bytes 709636
  95.5 20.5 %all-to-all-start.2 = ((bf16[8,232,256]{2,1,0:T(8,128)(2,1)}), bf16[8,232,256]{2,1,0:T(8,128)(2,1)}, u32[]{:S(2)}, u32[]{:S(2)}) async-start(bf16[8,232,256]{2,1,0:T(8,128)(2,1)} %add_convert_fusion), calls=%async_computation.2 | async-start | bytes 1900544 | tf_op jit(solution)/shard_map/all_to_all | solution.py:319
  99.7 5.1 %collective-permute-start.12 = (bf16[8,128,256]{2,1,0:T(8,128)(2,1)S(1)}, bf16[8,128,256]{2,1,0:T(8,128)(2,1)S(1)}, u32[]{:S(2)}, u32[]{:S(2)}) collective-permute-start(bf16[8,128,256]{2,1,0:T(8,128)(2,1)S(1)} %slice.12.refs_0_), channel_id=1, source_target_pairs={{0,8},{8,0},{16,24},{24,16},{32,40},{40,32},{48,56},{56,48},{64,72... | collective-permute-start | bytes 1572872 | tf_op jit(solution)/shard_map/ppermute | solution.py:262
  100.9 3.9 %collective-permute-start.13 = (bf16[8,128,256]{2,1,0:T(8,128)(2,1)S(1)}, bf16[8,128,256]{2,1,0:T(8,128)(2,1)S(1)}, u32[]{:S(2)}, u32[]{:S(2)}) collective-permute-start(bf16[8,128,256]{2,1,0:T(8,128)(2,1)S(1)} %collective-permute-done.7.refs_2_), channel_id=1, source_target_pairs={{0,8},{8,0},{16,24},{24,16},{32,40},{40,32},{48,56},{56,48},{64,72... | collective-permute-start | bytes 1572872 | tf_op jit(solution)/shard_map/ppermute | solution.py:262
  101.0 3.8 %collective-permute-start.14 = (bf16[8,128,256]{2,1,0:T(8,128)(2,1)}, bf16[8,128,256]{2,1,0:T(8,128)(2,1)}, u32[]{:S(2)}, u32[]{:S(2)}) collective-permute-start(bf16[8,128,256]{2,1,0:T(8,128)(2,1)} %collective-permute-done.8.refs_4_), channel_id=1, source_target_pairs={{0,8},{8,0},{16,24},{24,16},{32,40},{40,32},{48,56},{56,48},{64,72... | collective-permute-start | bytes 1572872 | tf_op jit(solution)/shard_map/ppermute | solution.py:262
  101.4 3.4 %collective-permute-start.15 = (bf16[4,128,256]{2,1,0:T(8,128)(2,1)}, bf16[4,128,256]{2,1,0:T(8,128)(2,1)S(1)}, u32[]{:S(2)}, u32[]{:S(2)}) collective-permute-start(bf16[4,128,256]{2,1,0:T(8,128)(2,1)} %collective-permute-done.10.refs_6_), channel_id=1, source_target_pairs={{0,8},{8,0},{16,24},{24,16},{32,40},{40,32},{48,56},{56,48},{64,72... | collective-permute-start | bytes 786440 | tf_op jit(solution)/shard_map/ppermute | solution.py:262
  101.5 3.3 %collective-permute-start.16 = (bf16[4,128,256]{2,1,0:T(8,128)(2,1)S(1)}, bf16[4,128,256]{2,1,0:T(8,128)(2,1)S(1)}, u32[]{:S(2)}, u32[]{:S(2)}) collective-permute-start(bf16[4,128,256]{2,1,0:T(8,128)(2,1)S(1)} %collective-permute-done.11.refs_8_), channel_id=1, source_target_pairs={{0,8},{8,0},{16,24},{24,16},{32,40},{40,32},{48,56},{56,48},{64,72... | collective-permute-start | bytes 786440 | tf_op jit(solution)/shard_map/ppermute | solution.py:262
